TPU v7x, 128 devices: a whole 4x4x4 slice. The times are simulated.
128 devices in a mesh: dp: 16 (over x, y), expert: 8 (over z, core).
Axes of the slice: x: 4, y: 4, z: 4, core: 2. Of those that a mesh axis runs over, the one named last changes fastest.
Arguments:
- inputs: bfloat16 [49152, 512], P(('dp', 'expert')), may hold values from -6 to 6
- cotangent: bfloat16 [49152, 512], P(('dp', 'expert')), may hold values from -6 to 6
- norm_gain: float32 [512], replicated, may hold values from 0.5 to 1.5
- ffn_gain: float32 [512], replicated, may hold values from 0.5 to 1.5
- kv_weight: bfloat16 [512, 128], replicated, may hold values from -0.25 to 0.25
- router_weight: bfloat16 [512, 24], replicated, may hold values from -0.125 to 0.125
- query_weight: bfloat16 [24, 512, 64], P('expert'), may hold values from -0.25 to 0.25
- output_weight: bfloat16 [24, 64, 512], P('expert'), may hold values from -6 to 6
- up_weight: bfloat16 [512, 2048], replicated, may hold values from -0.25 to 0.25
- down_weight: bfloat16 [2048, 512], replicated, may hold values from -0.125 to 0.125
- routes: int32 [49152, 8], P(('dp', 'expert')), may hold values from 0 to 23, all different within a row; in each aligned block of 384 rows (0 to 383, 384 to 767, ...) at most 160 rows name the same one
- segment_ids: int32 [49152], P(('dp', 'expert')), may hold values from 0 to 2, as said below
Outputs:
- block_output: bfloat16 [49152, 512], P(('dp', 'expert'))
- input_grad: bfloat16 [49152, 512], P(('dp', 'expert'))
- norm_gain_grad: float32 [512], replicated
- ffn_gain_grad: float32 [512], replicated
- kv_weight_grad: float32 [512, 128], replicated
- router_weight_grad: float32 [512, 24], replicated
- query_weight_grad: float32 [24, 512, 64], P('expert')
- output_weight_grad: float32 [24, 64, 512], P('expert')
- up_weight_grad: float32 [512, 2048], replicated
- down_weight_grad: float32 [2048, 512], replicated
Inputs may be any that keep to these rules, and one draw needn't show every extreme that they name: `routes`: each token names 8 different experts; the 384 rows of one device name any expert at most 160 times. `segment_ids`: within each group of 3072 consecutive tokens the ids start at 0 and never fall; three sequences, of which sequence 1 begins at a place from 1 to 383 of its group and ends at a place from 2688 to 3070.
All inputs are finite; a program needn't handle non-finite values.
Results may differ from a plain program's by a relative error of at most 0.019.
Values may be sent and summed in bfloat16 or wider, within the bound.
A program may use at most 320 MiB of HBM per device.

v0:
```python
import jax
import jax.numpy as jnp
from jax import lax
from jax.sharding import PartitionSpec as P

epsilon = 1e-06
masked_score = -1e30
highest_precision = lax.Precision.HIGHEST


def rms_scale(values, gain_vector):
    inverse = lax.rsqrt(jnp.mean(values * values, axis=-1, keepdims=True) + epsilon)
    return values * inverse * gain_vector


def gelu_curve(values):
    return (
        0.5
        * values
        * (1.0 + jnp.tanh(0.7978845608028654 * (values + 0.044715 * values * values * values)))
    )


def soft_rows(scores):
    exp_terms = jnp.exp(scores - jnp.max(scores, axis=-1, keepdims=True))
    return exp_terms / jnp.sum(exp_terms, axis=-1, keepdims=True)


def matmul_low(left_side, right_side):
    return jnp.dot(left_side, right_side, preferred_element_type=jnp.float32)


def matmul_left_t(left_side, right_side):
    return lax.dot_general(
        left_side, right_side, (((0,), (0,)), ((), ())), preferred_element_type=jnp.float32
    )


def matmul_right_t(left_side, right_side):
    return lax.dot_general(
        left_side, right_side, (((1,), (1,)), ((), ())), preferred_element_type=jnp.float32
    )


def visible_mask(query_pos, segment_all):
    key_pos = jnp.arange(segment_all.shape[0])
    same_segment = segment_all[query_pos][:, None] == segment_all[None, :]
    return same_segment & (key_pos[None, :] <= query_pos[:, None])


def attend_block(queries, query_pos, kv_all, segment_all):
    head_size = queries.shape[1]
    allowed = visible_mask(query_pos, segment_all)
    scores = jnp.where(allowed, matmul_right_t(queries, kv_all[:, :head_size]), masked_score)
    row_top = jnp.max(scores, axis=1, keepdims=True)
    exp_terms = jnp.exp(scores - row_top)
    row_total = jnp.sum(exp_terms, axis=1, keepdims=True)
    weights_soft = (exp_terms / row_total).astype(jnp.bfloat16)
    attended = matmul_low(weights_soft, kv_all[:, head_size:]).astype(jnp.bfloat16)
    return (attended, (row_top + jnp.log(row_total))[:, 0])


def attend_grad(queries, query_pos, kv_all, segment_all, log_total, grad_attended):
    head_size = queries.shape[1]
    allowed = visible_mask(query_pos, segment_all)
    scores = matmul_right_t(queries, kv_all[:, :head_size])
    weights_soft = jnp.where(allowed, jnp.exp(scores - log_total[:, None]), 0.0)
    grad_probs = matmul_right_t(grad_attended, kv_all[:, head_size:])
    row_inner = jnp.sum(weights_soft * grad_probs, axis=1, keepdims=True)
    grad_scores = (weights_soft * (grad_probs - row_inner)).astype(jnp.bfloat16)
    grad_queries = matmul_low(grad_scores, kv_all[:, :head_size]).astype(jnp.bfloat16)
    grad_keys = matmul_left_t(grad_scores, queries)
    grad_values = matmul_left_t(weights_soft.astype(jnp.bfloat16), grad_attended)
    return (grad_queries, jnp.concatenate([grad_keys, grad_values], axis=1))


def per_device(
    inputs,
    cotangent,
    norm_gain,
    ffn_gain,
    kv_weight,
    router_weight,
    query_weight,
    output_weight,
    up_weight,
    down_weight,
    routes,
    segment_ids,
):
    tok_rows, model_width = inputs.shape
    route_count = routes.shape[1]
    local_experts = query_weight.shape[0]
    head_size = query_weight.shape[2]
    group_size = lax.axis_size("expert")
    experts = local_experts * group_size
    capacity = min(tok_rows, 5 * route_count * tok_rows // (4 * experts))
    device_rank = lax.axis_index("expert")
    input_values = inputs.astype(jnp.float32)
    normed, first_pull = jax.vjp(rms_scale, input_values, norm_gain)
    normed_low = normed.astype(jnp.bfloat16)
    kv_local = matmul_low(normed_low, kv_weight).astype(jnp.bfloat16)
    kv_all, segment_all = (
        lax.all_gather(kv_local, "expert", axis=0, tiled=True),
        lax.all_gather(segment_ids, "expert", axis=0, tiled=True),
    )
    logits = matmul_low(normed_low, router_weight)
    gate_weights = soft_rows(jnp.take_along_axis(logits, routes, axis=1))
    onehot = (routes[:, :, None] == jnp.arange(experts)[None, None, :]).astype(jnp.float32)
    marked = jnp.sum(onehot, axis=1)
    token_ranks = jnp.cumsum(marked, axis=0) - marked
    slot_rank = jnp.sum(onehot * token_ranks[:, None, :], axis=2).astype(jnp.int32)
    slot_index = routes * capacity + slot_rank
    pair_index = jnp.arange(tok_rows)[:, None] * route_count + jnp.arange(route_count)[None, :]
    sentinel = tok_rows * route_count
    slot_pair = (
        jnp.full((experts * capacity,), sentinel, jnp.int32)
        .at[slot_index.reshape(-1)]
        .set(pair_index.reshape(-1))
    )
    slot_token = slot_pair // route_count
    filled = slot_pair < sentinel
    padded_rows = jnp.concatenate([normed_low, jnp.zeros((1, model_width), jnp.bfloat16)], axis=0)
    send_rows = padded_rows[slot_token].reshape(group_size, local_experts * capacity, model_width)
    send_pos = jnp.where(filled, device_rank * tok_rows + slot_token, 0)
    send_pos = send_pos.reshape(group_size, local_experts * capacity)
    recv_rows, recv_pos = (
        lax.all_to_all(send_rows, "expert", split_axis=0, concat_axis=0, tiled=True),
        lax.all_to_all(send_pos, "expert", split_axis=0, concat_axis=0, tiled=True),
    )
    rows_by = recv_rows.reshape(group_size, local_experts, capacity, model_width)
    pos_by = recv_pos.reshape(group_size, local_experts, capacity)
    kept_blocks = []
    out_blocks = []
    for local_slot in range(local_experts):
        slot_rows = rows_by[:, local_slot].reshape(group_size * capacity, model_width)
        positions = pos_by[:, local_slot].reshape(-1)
        queries = (matmul_low(slot_rows, query_weight[local_slot]) * 0.125).astype(jnp.bfloat16)
        attended, log_total = attend_block(queries, positions, kv_all, segment_all)
        expert_out = matmul_low(attended, output_weight[local_slot]).astype(jnp.bfloat16)
        out_blocks.append(expert_out.reshape(group_size, capacity, model_width))
        kept_blocks.append((slot_rows, positions, queries, attended, log_total))
    send_back = jnp.stack(out_blocks, axis=1).reshape(
        group_size, local_experts * capacity, model_width
    )
    returned_flat = lax.all_to_all(send_back, "expert", split_axis=0, concat_axis=0, tiled=True)
    returned = returned_flat.reshape(experts * capacity, model_width)[slot_index]
    returned_values = returned.astype(jnp.float32)
    mixed_sum = input_values + jnp.sum(gate_weights[:, :, None] * returned_values, axis=1)
    second, second_pull = jax.vjp(rms_scale, mixed_sum, ffn_gain)
    second_low = second.astype(jnp.bfloat16)
    hidden = matmul_low(second_low, up_weight)
    active, active_pull = jax.vjp(gelu_curve, hidden)
    active_low = active.astype(jnp.bfloat16)
    block_output = (mixed_sum + matmul_low(active_low, down_weight)).astype(jnp.bfloat16)
    grad_down = matmul_left_t(active_low, cotangent)
    grad_active = matmul_right_t(cotangent, down_weight)
    grad_hidden = active_pull(grad_active)[0].astype(jnp.bfloat16)
    grad_up = matmul_left_t(second_low, grad_hidden)
    grad_second = matmul_right_t(grad_hidden, up_weight)
    grad_mixed_norm, grad_ffn_gain = second_pull(grad_second)
    grad_mixed = cotangent.astype(jnp.float32) + grad_mixed_norm
    grad_gates = jnp.sum(grad_mixed[:, None, :] * returned_values, axis=2)
    grad_returned = (gate_weights[:, :, None] * grad_mixed[:, None, :]).astype(jnp.bfloat16)
    grad_chosen = gate_weights * (
        grad_gates - jnp.sum(gate_weights * grad_gates, axis=1, keepdims=True)
    )
    grad_logits = jnp.einsum("tje,tj->te", onehot, grad_chosen, precision=highest_precision)
    grad_router = jnp.dot(
        normed_low.astype(jnp.float32).T, grad_logits, precision=highest_precision
    )
    grad_normed = jnp.dot(
        grad_logits, router_weight.astype(jnp.float32).T, precision=highest_precision
    )
    grad_kv = jnp.zeros((kv_all.shape[0], 2 * head_size), jnp.float32)
    padded_grad = jnp.concatenate(
        [
            grad_returned.reshape(tok_rows * route_count, model_width),
            jnp.zeros((1, model_width), jnp.bfloat16),
        ],
        axis=0,
    )
    send_grad = padded_grad[slot_pair].reshape(group_size, local_experts * capacity, model_width)
    recv_grad = lax.all_to_all(send_grad, "expert", split_axis=0, concat_axis=0, tiled=True)
    grad_by = recv_grad.reshape(group_size, local_experts, capacity, model_width)
    query_grads = []
    output_grads = []
    grad_rows = []
    for local_slot in range(local_experts):
        slot_rows, positions, queries, attended, log_total = kept_blocks[local_slot]
        grad_out = grad_by[:, local_slot].reshape(group_size * capacity, model_width)
        output_grads.append(matmul_left_t(attended, grad_out))
        grad_attended = matmul_right_t(grad_out, output_weight[local_slot]).astype(jnp.bfloat16)
        grad_queries, grad_pair = attend_grad(
            queries, positions, kv_all, segment_all, log_total, grad_attended
        )
        grad_kv = grad_kv + grad_pair
        query_grads.append(matmul_left_t(slot_rows, grad_queries) * 0.125)
        row_grad = (matmul_right_t(grad_queries, query_weight[local_slot]) * 0.125).astype(
            jnp.bfloat16
        )
        grad_rows.append(row_grad.reshape(group_size, capacity, model_width))
    send_rows_grad = jnp.stack(grad_rows, axis=1).reshape(
        group_size, local_experts * capacity, model_width
    )
    back_rows = lax.all_to_all(send_rows_grad, "expert", split_axis=0, concat_axis=0, tiled=True)
    back_picked = back_rows.reshape(experts * capacity, model_width)[slot_index]
    grad_copies = jnp.sum(back_picked.astype(jnp.float32), axis=1)
    expert_query_grad = jnp.stack(query_grads, axis=0)
    expert_output_grad = jnp.stack(output_grads, axis=0)
    grad_kv_own = lax.psum_scatter(
        grad_kv.astype(jnp.bfloat16), "expert", scatter_dimension=0, tiled=True
    )
    grad_kv_weight = matmul_left_t(normed_low, grad_kv_own)
    grad_normed = grad_normed + grad_copies + matmul_right_t(grad_kv_own, kv_weight)
    grad_input_norm, grad_norm_gain = first_pull(grad_normed)
    input_grad = (grad_mixed + grad_input_norm).astype(jnp.bfloat16)
    query_grad, output_grad = (
        lax.psum(expert_query_grad.astype(jnp.bfloat16), "dp").astype(jnp.float32),
        lax.psum(expert_output_grad.astype(jnp.bfloat16), "dp").astype(jnp.float32),
    )
    shared_sums = lax.psum(
        (grad_norm_gain, grad_ffn_gain, grad_kv_weight, grad_router, grad_up, grad_down),
        ("dp", "expert"),
    )
    return (
        block_output,
        input_grad,
        shared_sums[0],
        shared_sums[1],
        shared_sums[2],
        shared_sums[3],
        query_grad,
        output_grad,
        shared_sums[4],
        shared_sums[5],
    )


def solution(mesh):
    placed = (
        P(("dp", "expert"), None),
        P(("dp", "expert"), None),
        P(),
        P(),
        P(),
        P(),
        P("expert", None, None),
        P("expert", None, None),
        P(),
        P(),
        P(("dp", "expert"), None),
        P(("dp", "expert")),
    )
    return jax.shard_map(
        per_device,
        mesh=mesh,
        in_specs=placed,
        out_specs=(
            P(("dp", "expert"), None),
            P(("dp", "expert"), None),
            P(),
            P(),
            P(),
            P(),
            P("expert", None, None),
            P("expert", None, None),
            P(),
            P(),
        ),
        check_vma=False,
    )
```

profile of v0, /device:TPU:0, one launch (start us, length us, event | category | flops | bytes accessed | tf_op | source)
XLA Modules:
  0.0 775.6 jit_solution(7952140511102848014)
XLA Ops:
  12.8 11.8 %scatter_custom_fusion = s32[3840]{0:T(1024)S(1)} fusion(s32[3072]{0:T(1024)S(1)} %bitcast.214, s32[3072]{0:T(1024)S(1)} %reshape.383, s32[]{:T(128)} %constant.36.clone.1), kind=kCustom, calls=%fused_computation.224 | custom fusion | bytes 15364 | tf_op jit(solution)/shard_map/scatter | solution.py:119
  25.3 5.4 all-to-all-start
  33.7 11.7 %gather_fusion.1 = bf16[3840,512]{1,0:T(8,128)(2,1)} fusion(bf16[385,512]{1,0:T(8,128)(2,1)S(1)} %concatenate.15, s32[4096]{0:T(1024)S(1)} %get-tuple-element.58), kind=kCustom, calls=%fused_computation.1 | custom fusion | bytes 7879680 | tf_op jit(solution)/shard_map/gather | solution.py:124
  50.4 51.4 %all-gather = s32[8,1,384]{2,1,0:T(1,128)S(1)} all-gather(s32[1,1,384]{2,1,0:T(1,128)S(1)} %reshape.400), channel_id=1, replica_groups=mesh['dp'=16,'expert'=8] {'expert'}, dimensions={0}, use_global_device_ids=true | all-gather | bytes 13824 | tf_op jit(solution)/shard_map/all_gather | solution.py:105
  102.1 13.9 %all_gather.7 = bf16[3072,128]{1,0:T(8,128)(2,1)S(1)} all-gather(bf16[384,128]{1,0:T(8,128)(2,1)S(1)} %convolution_convert_fusion.9), channel_id=1, replica_groups=mesh['dp'=16,'expert'=8] {'expert'}, dimensions={0}, use_global_device_ids=true | all-gather | bytes 884736 | tf_op jit(solution)/shard_map/all_gather | solution.py:104
  116.7 7.1 gather_fusion
  123.9 7.1 gather_fusion.2
  131.0 7.1 gather_fusion.3
  144.6 8.6 %fusion.9 = (f32[1280]{0:T(1024)S(1)}, f32[1280,3072]{1,0:T(8,128)}) fusion(s32[1280]{0:T(1024)S(1)} %le.36, s32[3072]{0:T(1024)S(1)} %bitcast.175, s32[1280]{0:T(1024)S(1)} %gather_fusion, bf16[1280,64]{0,1:T(8,128)(2,1)S(1)} %fusion.33, bf16[3072,128]{1,0:T(8,128)(2,1)S(1)} %all_gather.7), kind=kOutput, calls=%fused_computation.36 | convolution fusion | flops 522976000 | bytes 16706560 | tf_op jit(solution)/shard_map/dot_general | solution.py:40
  153.2 19.6 %fusion.3 = (f32[1280]{0:T(1024)S(1)}, f32[1280]{0:T(1024)S(1)}, f32[1280]{0:T(1024)S(1)}, f32[1280,3072]{1,0:T(8,128)}) fusion(f32[1280,3072]{1,0:T(8,128)} %get-tuple-element.50, f32[1280]{0:T(1024)S(1)} %get-tuple-element.49, s32[1280]{0:T(1024)S(1)} %le.36, s32[3072]{0:T(1024)S(1)} %bitcast.176, s32[1280]{0:T(1024)S(1)} %gather_fusion, ...), kind=kOutput, calls=%fused_computation.30 | convolution fusion | flops 566227200 | bytes 48199680 | tf_op jit(solution)/shard_map/dot_general | solution.py:40
  172.8 9.4 %fusion.38 = bf16[1280,64]{0,1:T(8,128)(2,1)S(1)} fusion(f32[1280,3072]{1,0:T(8,128)} %get-tuple-element.50, f32[1280]{0:T(1024)S(1)} %get-tuple-element.20, f32[1280]{0:T(1024)S(1)} %get-tuple-element.49, s32[1280]{0:T(1024)S(1)} %le.36, s32[3072]{0:T(1024)S(1)} %bitcast.177, s32[1280]{0:T(1024)S(1)} %gather_fusion, bf16[3072,128]{1,0:T(8,128)(2,1)S(1)} %all_gather.7), kind=kOutput, calls=%fused_computation.85 | convolution fusion | flops 530923520 | bytes 16711680 | tf_op jit(solution)/shard_map/dot_general | solution.py:30
  182.3 12.1 %fusion.4 = (f32[1280]{0:T(1024)S(1)}, f32[1280]{0:T(1024)S(1)}) fusion(f32[1280,3072]{1,0:T(8,128)} %get-tuple-element.51, f32[1280]{0:T(1024)S(1)} %get-tuple-element.21, s32[1280]{0:T(1024)S(1)} %le.40, s32[3072]{0:T(1024)S(1)} %bitcast.178, s32[1280]{0:T(1024)S(1)} %gather_fusion.2, f32[1280]{0:T(1024)S(1)} %get-tuple-element.22, ...), kind=kLoop, calls=%fused_computation.31 | loop fusion | flops 47183360 | bytes 31510528 | tf_op jit(solution)/shard_map/reduce_sum | solution.py:57
  194.5 9.4 %fusion.37 = bf16[1280,64]{0,1:T(8,128)(2,1)S(1)} fusion(f32[1280,3072]{1,0:T(8,128)} %get-tuple-element.51, f32[1280]{0:T(1024)S(1)} %get-tuple-element.23, f32[1280]{0:T(1024)S(1)} %get-tuple-element.21, s32[1280]{0:T(1024)S(1)} %le.40, s32[3072]{0:T(1024)S(1)} %bitcast.179, s32[1280]{0:T(1024)S(1)} %gather_fusion.2, bf16[3072,128]{1,0:T(8,128)(2,1)S(1)} %all_gather.7), kind=kOutput, calls=%fused_computation.84 | convolution fusion | flops 530923520 | bytes 16711680 | tf_op jit(solution)/shard_map/dot_general | solution.py:30
  205.1 5.7 fusion.36
  220.5 25.0 %gather_fusion.7 = f32[3072]{0:T(1024)S(1)} fusion(f32[384,24]{0,1:T(8,128)S(1)} %fusion.124, s32[3072]{0:T(1024)S(1)} %reshape.373), kind=kCustom, calls=%fused_computation.7 | custom fusion | bytes 49152 | tf_op jit(solution)/shard_map/jit(take_along_axis)/gather | solution.py:108
  253.1 12.1 %all-to-all-done.2 = bf16[8,480,512]{2,1,0:T(8,128)(2,1)} async-done(((bf16[8,480,512]{2,1,0:T(8,128)(2,1)}), bf16[8,480,512]{2,1,0:T(8,128)(2,1)}, u32[]{:S(2)}, u32[]{:S(2)}) %all-to-all-start.2) | async-done | bytes 3932192 | tf_op jit(solution)/shard_map/all_to_all | solution.py:146
  265.2 15.9 %gather_fusion.4 = bf16[3072,512]{1,0:T(8,128)(2,1)} fusion(bf16[3840,512]{1,0:T(8,128)(2,1)} %bitcast.23, s32[3072]{0:T(1024)S(1)} %broadcast_clamp_fusion), kind=kCustom, calls=%fused_computation.4 | custom fusion | bytes 6303744 | tf_op jit(solution)/shard_map/gather | solution.py:147
  295.3 14.2 %gather_fusion.5 = bf16[3840,512]{1,0:T(8,128)(2,1)} fusion(bf16[3073,512]{1,0:T(8,128)(2,1)} %concatenate.16, s32[4096]{0:T(1024)S(1)} %copy-done.56), kind=kCustom, calls=%fused_computation.5 | custom fusion | bytes 7879680 | tf_op jit(solution)/shard_map/gather | solution.py:183
  323.2 37.8 %all-to-all-done.3 = bf16[8,480,512]{2,1,0:T(8,128)(2,1)} async-done(((bf16[8,480,512]{2,1,0:T(8,128)(2,1)}), bf16[8,480,512]{2,1,0:T(8,128)(2,1)}, u32[]{:S(2)}, u32[]{:S(2)}) %all-to-all-start.3) | async-done | bytes 3932192 | tf_op jit(solution)/shard_map/all_to_all | solution.py:184
  366.2 7.8 %fusion.65 = f32[1280,3072]{1,0:T(8,128)} fusion(bf16[1280,64]{0,1:T(8,128)(2,1)S(1)} %convolution_convert_fusion.5, bf16[3072,128]{1,0:T(8,128)(2,1)S(1)} %all_gather.7), kind=kOutput, calls=%fused_computation.139 | convolution fusion | flops 503316480 | bytes 16678912 | tf_op jit(solution)/shard_map/dot_general | solution.py:40
  374.1 7.7 fusion.63
  381.8 33.8 %multiply_reduce_fusion = (f32[1280]{0:T(1024)S(1)}, f32[1280]{0:T(1024)S(1)}, f32[1280]{0:T(1024)S(1)}, f32[1280,3072]{1,0:T(8,128)}) fusion(f32[1280,3072]{1,0:T(8,128)} %copy-done.2, f32[1280]{0:T(1024)S(1)} %log_add_fusion, s32[1280]{0:T(1024)S(1)} %le.44, s32[3072]{0:T(1024)S(1)} %bitcast.181, s32[1280]{0:T(1024)S(1)} %copy-done.55, ...), kind=kOutput, calls=%fused_computation.10 | convolution fusion | flops 585888000 | bytes 95395840 | tf_op jit(solution)/shard_map/dot_general | solution.py:40
  415.6 40.6 %multiply_convert_fusion = (bf16[1280,3072]{1,0:T(8,128)(2,1)}, bf16[1280,3072]{1,0:T(8,128)(2,1)}, bf16[1280,3072]{1,0:T(8,128)(2,1)}) fusion(f32[1280,3072]{1,0:T(8,128)} %get-tuple-element.55, f32[1280]{0:T(1024)S(1)} %get-tuple-element.17, f32[1280,3072]{1,0:T(8,128)} %copy-done.2, f32[1280]{0:T(1024)S(1)} %log_add_fusion, s32[1280]{0:T(1024)S(1)} %le.44, ...), kind=kLoop, calls=%fused_computation.9 | loop fusion | flops 94371840 | bytes 118038528 | tf_op jit(solution)/shard_map/convert_element_type | solution.py:70
  456.2 5.9 convolution_convert_fusion.6
  463.7 8.5 %fusion.12 = f32[3072,64]{0,1:T(8,128)S(1)} fusion(bf16[1280,64]{0,1:T(8,128)(2,1)S(1)} %convolution_convert_fusion.3, f32[1280,3072]{1,0:T(8,128)} %copy-done.2, f32[1280]{0:T(1024)S(1)} %log_add_fusion, s32[1280]{0:T(1024)S(1)} %le.44, s32[3072]{0:T(1024)S(1)} %bitcast.183, s32[1280]{0:T(1024)S(1)} %copy-done.55), kind=kOutput, calls=%fused_computation.41 | convolution fusion | flops 526909440 | bytes 16706560 | tf_op jit(solution)/shard_map/dot_general | solution.py:34
  481.2 8.7 %fusion.16 = f32[3072,64]{0,1:T(8,128)S(1)} fusion(bf16[1280,64]{0,1:T(8,128)(2,1)S(1)} %convolution_convert_fusion.5, f32[1280,3072]{1,0:T(8,128)} %get-tuple-element.50, f32[1280]{0:T(1024)S(1)} %log_add_fusion.2, s32[1280]{0:T(1024)S(1)} %copy-done.68, s32[3072]{0:T(1024)S(1)} %bitcast.185, s32[1280]{0:T(1024)S(1)} %copy-done.70), kind=kOutput, calls=%fused_computation.45 | convolution fusion | flops 526909440 | bytes 16706560 | tf_op jit(solution)/shard_map/dot_general | solution.py:34
  494.5 5.9 convolution_convert_fusion.8
  514.7 13.5 %reduce-scatter.4.cloned.1.call-done = bf16[384,128]{1,0:T(8,128)(2,1)} async-done(((bf16[3072,128]{1,0:T(8,128)(2,1)}), bf16[384,128]{1,0:T(8,128)(2,1)}) %reduce-scatter.4.cloned.1.call-update) | async-done | bytes 98320
  538.8 51.3 %all-reduce.10.cloned.1.call-done = (bf16[3,512,64]{1,2,0:T(8,128)(2,1)}, bf16[3,64,512]{2,1,0:T(8,128)(2,1)}) async-done(((bf16[3,512,64]{1,2,0:T(8,128)(2,1)}, bf16[3,64,512]{2,1,0:T(8,128)(2,1)}), (bf16[3,512,64]{1,2,0:T(8,128)(2,1)}, bf16[3,64,512]{2,1,0:T(8,128)(2,1)})) %all-reduce.10.cloned.1.call-update) | async-done | bytes 393232 | tf_op jit(solution)/shard_map/psum | solution.py:219
  593.8 16.2 %gather_fusion.6 = bf16[3072,512]{1,0:T(8,128)(2,1)} fusion(bf16[3840,512]{1,0:T(8,128)(2,1)} %bitcast.39, s32[3072]{0:T(1024)S(1)} %copy-done.8), kind=kCustom, calls=%fused_computation.6 | custom fusion | bytes 6303744 | tf_op jit(solution)/shard_map/gather | solution.py:207
  615.2 65.4 %all-reduce.2 = (f32[512]{0:T(512)}, f32[512]{0:T(512)}, f32[512,24]{0,1:T(8,128)}) all-reduce(f32[512]{0:T(512)S(1)} %get-tuple-element.12, f32[512]{0:T(512)S(1)} %copy-done.81, f32[512,24]{0,1:T(8,128)S(1)} %fusion.128), channel_id=1, replica_groups=mesh['dp'=16,'expert'=8] {'dp','expert'}, use_global_device_ids=true, to_apply=%region_26.27 | all-reduce | flops 13312 | bytes 106496 | tf_op jit(solution)/shard_map/psum | solution.py:222
  681.6 77.8 %all-reduce.8.cloned.1.call-done = (f32[512,128]{1,0:T(8,128)}, f32[512,2048]{1,0:T(8,128)}, f32[2048,512]{1,0:T(8,128)}) async-done(((f32[512,128]{1,0:T(8,128)}, f32[512,2048]{1,0:T(8,128)}, f32[2048,512]{1,0:T(8,128)}), (f32[512,128]{1,0:T(8,128)}, f32[512,2048]{1,0:T(8,128)}, f32[2048,512]{1,0:T(8,128)})) %all-reduce.8.cloned.1.call-update) | async-done | bytes 8650768 | tf_op jit(solution)/shard_map/psum | solution.py:222
  (315 shorter events, 130.0 us)
Async XLA Ops:
  8.0 277.4 %copy-start = (bf16[512,2048]{1,0:T(8,128)(2,1)S(1)}, bf16[512,2048]{1,0:T(8,128)(2,1)}, u32[]{:S(2)}) copy-start(bf16[512,2048]{1,0:T(8,128)(2,1)} %param.20) | copy-start | bytes 6291460
  25.3 20.1 %all-to-all-start = ((s32[8,1,480]{2,1,0:T(1,128)}), s32[8,1,480]{2,1,0:T(1,128)S(1)}, u32[]{:S(2)}, u32[]{:S(2)}) async-start(s32[8,1,480]{2,1,0:T(1,128)} %all_to_all.18), calls=%async_computation | async-start | bytes 32768 | tf_op jit(solution)/shard_map/all_to_all | solution.py:129
  31.8 13.6 %copy-start.71 = (f32[384]{0:T(512)}, f32[384]{0:T(512)S(1)}, u32[]{:S(2)}) copy-start(f32[384]{0:T(512)S(1)} %fusion.113) | copy-start | bytes 4612
  33.0 68.8 %copy-start.4 = (bf16[384,512]{1,0:T(8,128)(2,1)}, bf16[384,512]{1,0:T(8,128)(2,1)S(1)}, u32[]{:S(2)}) copy-start(bf16[384,512]{1,0:T(8,128)(2,1)S(1)} %fusion.54) | copy-start | bytes 1179652
  45.4 56.4 %copy-start.44 = (bf16[512,128]{1,0:T(8,128)(2,1)S(1)}, bf16[512,128]{1,0:T(8,128)(2,1)}, u32[]{:S(2)}) copy-start(bf16[512,128]{1,0:T(8,128)(2,1)} %param.16) | copy-start | bytes 393220
  45.4 92.7 %all-to-all-start.1 = ((bf16[8,480,512]{2,1,0:T(8,128)(2,1)}), bf16[8,480,512]{2,1,0:T(8,128)(2,1)}, u32[]{:S(2)}, u32[]{:S(2)}) async-start(bf16[8,480,512]{2,1,0:T(8,128)(2,1)} %bitcast.194), calls=%async_computation.1 | async-start | bytes 7864320 | tf_op jit(solution)/shard_map/all_to_all | solution.py:128
  116.4 56.4 %copy-start.67 = (s32[1280]{0:T(1024)}, s32[1280]{0:T(1024)S(1)}, u32[]{:S(2)}) copy-start(s32[1280]{0:T(1024)S(1)} %le.36) | copy-start | bytes 15364
  116.5 77.9 %copy-start.50 = (s32[1280]{0:T(1024)}, s32[1280]{0:T(1024)S(1)}, u32[]{:S(2)}) copy-start(s32[1280]{0:T(1024)S(1)} %le.40) | copy-start | bytes 15364
  123.8 49.0 %copy-start.69 = (s32[1280]{0:T(1024)}, s32[1280]{0:T(1024)S(1)}, u32[]{:S(2)}) copy-start(s32[1280]{0:T(1024)S(1)} %gather_fusion) | copy-start | bytes 15364
  131.0 63.5 %copy-start.52 = (s32[1280]{0:T(1024)}, s32[1280]{0:T(1024)S(1)}, u32[]{:S(2)}) copy-start(s32[1280]{0:T(1024)S(1)} %gather_fusion.2) | copy-start | bytes 15364
  138.1 66.9 %copy-start.54 = (s32[1280]{0:T(1024)}, s32[1280]{0:T(1024)S(1)}, u32[]{:S(2)}) copy-start(s32[1280]{0:T(1024)S(1)} %gather_fusion.3) | copy-start | bytes 15364
  144.6 60.4 %copy-start.2 = (f32[1280,3072]{1,0:T(8,128)}, f32[1280,3072]{1,0:T(8,128)S(1)}, u32[]{:S(2)}) copy-start(f32[1280,3072]{1,0:T(8,128)S(1)} %fusion.73) | copy-start | bytes 47185924
  153.2 19.7 %copy-start.76 = (f32[1280]{0:T(1024)}, f32[1280]{0:T(1024)S(1)}, u32[]{:S(2)}) copy-start(f32[1280]{0:T(1024)S(1)} %get-tuple-element.49) | copy-start | bytes 15364
  172.8 21.6 %copy-start.61 = (f32[1280]{0:T(1024)}, f32[1280]{0:T(1024)S(1)}, u32[]{:S(2)}) copy-start(f32[1280]{0:T(1024)S(1)} %get-tuple-element.21) | copy-start | bytes 15364
  172.8 32.2 %copy-start.59 = (f32[1280]{0:T(1024)}, f32[1280]{0:T(1024)S(1)}, u32[]{:S(2)}) copy-start(f32[1280]{0:T(1024)S(1)} %get-tuple-element.22) | copy-start | bytes 15364
  182.3 21.7 %copy-start.38 = (bf16[1280,64]{0,1:T(8,128)(2,1)}, bf16[1280,64]{0,1:T(8,128)(2,1)S(1)}, u32[]{:S(2)}) copy-start(bf16[1280,64]{0,1:T(8,128)(2,1)S(1)} %fusion.38) | copy-start | bytes 491524
  213.4 51.8 %all-to-all-start.2 = ((bf16[8,480,512]{2,1,0:T(8,128)(2,1)}), bf16[8,480,512]{2,1,0:T(8,128)(2,1)}, u32[]{:S(2)}, u32[]{:S(2)}) async-start(bf16[8,480,512]{2,1,0:T(8,128)(2,1)} %bitcast.193), calls=%async_computation.2 | async-start | bytes 7864320 | tf_op jit(solution)/shard_map/all_to_all | solution.py:146
  220.5 28.3 %copy-start.28 = (bf16[384,512]{1,0:T(8,128)(2,1)S(1)}, bf16[384,512]{1,0:T(8,128)(2,1)}, u32[]{:S(2)}) copy-start(bf16[384,512]{1,0:T(8,128)(2,1)} %param.13) | copy-start | bytes 1179652
  248.8 32.4 %copy-start.7 = (s32[3072]{0:T(1024)}, s32[3072]{0:T(1024)S(1)}, u32[]{:S(2)}) copy-start(s32[3072]{0:T(1024)S(1)} %broadcast_clamp_fusion) | copy-start | bytes 36868
  309.5 51.5 %all-to-all-start.3 = ((bf16[8,480,512]{2,1,0:T(8,128)(2,1)}), bf16[8,480,512]{2,1,0:T(8,128)(2,1)}, u32[]{:S(2)}, u32[]{:S(2)}) async-start(bf16[8,480,512]{2,1,0:T(8,128)(2,1)} %bitcast.195), calls=%async_computation.3 | async-start | bytes 7864320 | tf_op jit(solution)/shard_map/all_to_all | solution.py:184
  314.2 214.1 %reduce-scatter.4.cloned.1.call-start = ((), (), s32[]{:S(2)}) async-start(), calls=%async_computation.6 | async-start | bytes 884736
  462.1 27.8 %copy-start.25 = (bf16[1280,64]{0,1:T(8,128)(2,1)}, bf16[1280,64]{0,1:T(8,128)(2,1)S(1)}, u32[]{:S(2)}) copy-start(bf16[1280,64]{0,1:T(8,128)(2,1)S(1)} %convolution_convert_fusion.6) | copy-start | bytes 491524
  474.8 15.5 %copy-start.26 = (bf16[1280,64]{0,1:T(8,128)(2,1)}, bf16[1280,64]{0,1:T(8,128)(2,1)S(1)}, u32[]{:S(2)}) copy-start(bf16[1280,64]{0,1:T(8,128)(2,1)S(1)} %convolution_convert_fusion.7) | copy-start | bytes 491524
  476.7 13.9 %slice-start = ((s8[7864320]{0:T(1024)(128)(4,1)}), s8[4194304]{0:T(1024)(128)(4,1)S(1)}, s32[]{:S(2)}) async-start(s8[7864320]{0:T(1024)(128)(4,1)} %bitcast.186), calls=%async_computation.9 | async-start | bytes 8388608
  493.7 96.4 %all-reduce.10.cloned.1.call-start = ((), (), s32[]{:S(2)}) async-start(), calls=%async_computation.8 | async-start | bytes 786432 | tf_op jit(solution)/shard_map/psum | solution.py:219
  509.9 18.3 %copy-start.6 = (bf16[384,512]{1,0:T(8,128)(2,1)S(1)}, bf16[384,512]{1,0:T(8,128)(2,1)}, u32[]{:S(2)}) copy-start(bf16[384,512]{1,0:T(8,128)(2,1)} %copy-done.4) | copy-start | bytes 1179652
  509.9 83.9 %all-to-all-start.4 = ((bf16[8,480,512]{2,1,0:T(8,128)(2,1)}), bf16[8,480,512]{2,1,0:T(8,128)(2,1)}, u32[]{:S(2)}, u32[]{:S(2)}) async-start(bf16[8,480,512]{2,1,0:T(8,128)(2,1)} %bitcast.192), calls=%async_computation.4 | async-start | bytes 7864320 | tf_op jit(solution)/shard_map/all_to_all | solution.py:206
  514.7 244.7 %all-reduce.8.cloned.1.call-start = ((), (), s32[]{:S(2)}) async-start(), calls=%async_computation.7 | async-start | bytes 17301504 | tf_op jit(solution)/shard_map/psum | solution.py:222
  534.4 59.2 %copy-start.45 = (bf16[512,128]{1,0:T(8,128)(2,1)S(1)}, bf16[512,128]{1,0:T(8,128)(2,1)}, u32[]{:S(2)}) copy-start(bf16[512,128]{1,0:T(8,128)(2,1)} %param.16) | copy-start | bytes 393220
  534.4 59.2 %copy-start.46 = (bf16[384,128]{1,0:T(8,128)(2,1)S(1)}, bf16[384,128]{1,0:T(8,128)(2,1)}, u32[]{:S(2)}) copy-start(bf16[384,128]{1,0:T(8,128)(2,1)} %reduce-scatter.4.cloned.1.call-done) | copy-start | bytes 294916
  534.4 59.4 %copy-start.8 = (s32[3072]{0:T(1024)S(1)}, s32[3072]{0:T(1024)}, u32[]{:S(2)}) copy-start(s32[3072]{0:T(1024)} %copy-done.7) | copy-start | bytes 36868
  610.0 70.6 %copy-start.74 = (f32[384]{0:T(512)S(1)}, f32[384]{0:T(512)}, u32[]{:S(2)}) copy-start(f32[384]{0:T(512)} %copy-done.73) | copy-start | bytes 4612
  (67 other events, 366.7 us)
Sparse Core Ops, SparseCore 0:
  493.8 34.3 reduce-scatter.3
Sparse Core Ops, SparseCore 1:
  506.8 83.2 all-reduce.9
  597.5 161.8 all-reduce.7
where the time goes:
time: 781 us; the launch traced here: 776 us
  waiting for transfers between devices  193 us (25%)
  matrix products  185 us (24%)
  local copies, waits for them, and re-layouts  140 us (18%)
  blocking collectives  131 us (17%)
  other arithmetic  85.1 us (11%)
  starting transfers between devices  25.2 us (3%)
  between operations  17.2 us (2%)
    dot_general x15, matrix products, matmul_right_t(): lax.dot_general(left_side, right_side, (((1,), (1,)), ((), ())), preferre...  92.9 us
    psum x1, waiting for transfers between devices, per_device(): lax.psum((grad_norm_gain, grad_ffn_gain, grad_kv_weight, grad_router, gra...  77.8 us
    psum x1, blocking collectives, per_device(): lax.psum((grad_norm_gain, grad_ffn_gain, grad_kv_weight, grad_router, gra...  65.4 us
    dot_general x16, matrix products, matmul_low(): return jnp.dot(left_side, right_side, preferred_element_type=jnp.float32)  52.1 us
    all_gather x1, blocking collectives, per_device(): lax.all_gather(segment_ids, 'expert', axis=0, tiled=True)  51.4 us
    psum x1, waiting for transfers between devices, per_device(): lax.psum(expert_query_grad.astype(jnp.bfloat16), 'dp').astype(jnp.float32)  51.3 us
    convert_element_type x1, other arithmetic, attend_grad(): grad_scores = (weights_soft * (grad_probs - row_inner)).astype(jnp.bfloat16)  40.6 us
    dot_general x15, matrix products, matmul_left_t(): lax.dot_general(left_side, right_side, (((0,), (0,)), ((), ())), preferre...  38.5 us
  transfers between devices with their start and end apart: 8, of which 5 were waited for; matrix products, arithmetic and copies ran while one was open for 17% of the time, Pallas kernels for 0%

commit v1 on v0

v1 whole, which is shorter than its diff:
```python
import functools
import jax
import jax.numpy as jnp
from jax import lax
from jax.experimental import pallas as pl
from jax.experimental.pallas import tpu as pltpu
from jax.sharding import PartitionSpec as P

f32, bf16, i32 = jnp.float32, jnp.bfloat16, jnp.int32
T, D, H, J, E, FF, NB = 384, 512, 64, 8, 24, 2048, 8
EW = E * H
PAIRS = E // 2
HALF_J = 4
ROWS = HALF_J * T
eps = 1e-06
NEG = -1e30
VM = pltpu.VMEM


def nn(a, b):
    return lax.dot_general(a, b, (((1,), (0,)), ((), ())), preferred_element_type=f32)


def nt(a, b):
    return lax.dot_general(a, b, (((1,), (1,)), ((), ())), preferred_element_type=f32)


def tn(a, b):
    return lax.dot_general(a, b, (((0,), (0,)), ((), ())), preferred_element_type=f32)


def lanes(rows):
    return lax.broadcasted_iota(i32, (rows, 128), 1)


def split3(v):
    a = v.astype(bf16).astype(f32)
    b = (v - a).astype(bf16).astype(f32)
    c = (v - a - b).astype(bf16).astype(f32)
    return a, b, c


def causal(rows, cols):
    return lax.broadcasted_iota(i32, (rows, cols), 1) <= lax.broadcasted_iota(i32, (rows, cols), 0)


def segment_of(pos, bnd_ref):
    b0 = bnd_ref[0:1, :]
    b1 = bnd_ref[1:2, :]
    return (pos >= b0).astype(i32) + (pos >= b1).astype(i32)


def pick_rows(route_cols, row0, rows, j):
    return jnp.broadcast_to(route_cols[row0 : row0 + rows, j : j + 1], (rows, 128))


def expert_lane(rows):
    return (lanes(rows) >= H).astype(i32)


def kernel_a(x_ref, gain_ref, kvw_ref, rw_ref, routes_ref, normed_ref, kv_ref, gate_ref):
    x = x_ref[...].astype(f32)
    inv = lax.rsqrt(jnp.mean(x * x, axis=-1, keepdims=True) + eps)
    normed = (x * inv * gain_ref[...]).astype(bf16)
    normed_ref[...] = normed
    kv_ref[...] = nn(normed, kvw_ref[...]).astype(bf16)
    logits = nt(normed, rw_ref[...])
    cols = jnp.transpose(routes_ref[...])
    eid = lax.broadcasted_iota(i32, (T, E), 1)
    chosen = cols[:, 0:1] == eid
    for j in range(1, J):
        chosen = chosen | (cols[:, j : j + 1] == eid)
    logits = jnp.where(chosen, logits, NEG)
    top = jnp.max(logits, axis=-1, keepdims=True)
    e = jnp.where(chosen, jnp.exp(logits - top), 0.0)
    gate_ref[...] = e / jnp.sum(e, axis=-1, keepdims=True)


def prepare_keys(kv_ref, bnd_ref, kaug, vaug):
    ln = lanes(T)
    for b in range(NB):
        kv = kv_ref[b].astype(f32)
        pos = lax.broadcasted_iota(i32, (T, 128), 0) + b * T
        seg = segment_of(pos, bnd_ref)
        feat = jnp.where((ln < H + 3) & (seg != ln - H), NEG, 0.0)
        feat = jnp.where((ln >= H + 3) & (ln < H + 6), 1.0, feat)
        kaug[b] = jnp.where(ln < H, kv, feat).astype(bf16)
        one = jnp.where(ln < H + 3, 1.0, 0.0)
        vaug[b] = jnp.where(ln < H, pltpu.roll(kv, H, 1), one).astype(bf16)


def pick_queries(normed_ref, wq_ref, routes_ref, bnd_ref, me, qall, cols_ref, qa):
    cols_ref[...] = jnp.transpose(routes_ref[...])
    normed = normed_ref[...]
    for c in range(6):
        qall[:, c * 256 : (c + 1) * 256] = nt(normed, wq_ref[c * 256 : (c + 1) * 256, :]) * 0.125
    R = 128
    ln = lanes(R)
    half = expert_lane(R)

    def chunk(i, _):
        r0 = pl.multiple_of(i * R, R)
        pos = lax.broadcasted_iota(i32, (R, 128), 0) + me * T + r0
        seg = segment_of(pos, bnd_ref)
        feat = jnp.where((ln >= H) & (seg == ln - H), 1.0, 0.0)
        for j in range(J):
            rj = jnp.broadcast_to(cols_ref[pl.ds(r0, R), j : j + 1], (R, 128)) - half
            acc = jnp.zeros((R, 128), f32)
            for p in range(PAIRS):
                acc = jnp.where(rj == 2 * p, qall[pl.ds(r0, R), p * 128 : (p + 1) * 128], acc)
            acc = acc + pltpu.roll(acc, H, 1)
            qa[j, pl.ds(r0, R), :] = jnp.where(ln < H, acc, feat).astype(bf16)
        return 0

    lax.fori_loop(0, T // R, chunk, 0)


def attend_set(me, s, qa, kaug, vaug, att_ref, sbuf, mbuf, acc):
    mbuf[...] = jnp.full(mbuf.shape, NEG, f32)
    acc[...] = jnp.zeros(acc.shape, f32)

    def score(kb, masked):
        for j in range(HALF_J):
            sc = nt(qa[s * HALF_J + j], kaug[kb])
            if masked:
                sc = jnp.where(causal(T, T), sc, NEG)
            sbuf[kb, j] = sc
            m = jnp.maximum(sc[:, 0:128], jnp.maximum(sc[:, 128:256], sc[:, 256:384]))
            mbuf[j] = jnp.maximum(mbuf[j], m)

    lax.fori_loop(0, me, lambda kb, c: (score(kb, False), c)[1], 0)
    score(me, True)
    for j in range(HALF_J):
        mbuf[j] = jnp.broadcast_to(jnp.max(mbuf[j], axis=-1, keepdims=True), (T, 128))

    def weigh(kb, c):
        for j in range(HALF_J):
            m = mbuf[j]
            p = jnp.exp(sbuf[kb, j] - jnp.concatenate([m, m, m], axis=1)).astype(bf16)
            acc[j] += nn(p, vaug[kb])
        return c

    lax.fori_loop(0, me + 1, weigh, 0)
    ln = lanes(T)
    for j in range(HALF_J):
        a = acc[j]
        tot = jnp.broadcast_to(a[:, H : H + 1], (T, 128))
        att_ref[s * HALF_J + j] = (a / tot).astype(bf16)
        l1, l2, l3 = split3(-(mbuf[j] + jnp.log(tot)))
        lse = jnp.where(ln == H + 3, l1, jnp.where(ln == H + 4, l2, l3))
        old = qa[s * HALF_J + j].astype(f32)
        qa[s * HALF_J + j] = jnp.where((ln >= H + 3) & (ln < H + 6), lse, old).astype(bf16)


def kernel_b(normed_ref, wq_ref, routes_ref, bnd_ref, kv_ref, att_ref, qa_ref, qall, cols_ref, kaug, vaug, sbuf, mbuf, acc):
    me = lax.axis_index("expert")
    prepare_keys(kv_ref, bnd_ref, kaug, vaug)
    pick_queries(normed_ref, wq_ref, routes_ref, bnd_ref, me, qall, cols_ref, qa_ref)
    lax.fori_loop(0, 2, lambda s, c: (attend_set(me, s, qa_ref, kaug, vaug, att_ref, sbuf, mbuf, acc), c)[1], 0)


SCRATCH_B = [VM((T, EW), f32), VM((T, J), i32), VM((NB, T, 128), bf16), VM((NB, T, 128), bf16),
             VM((NB, HALF_J, T, T), f32), VM((HALF_J, T, 128), f32), VM((HALF_J, T, 128), f32)]


def kernel_c(x_ref, cot_ref, gate_ref, routes_ref, att_ref, wo_ref, up_ref, down_ref, fgain_ref, normed_ref, rw_ref,
             out_ref, da_ref, gm_ref, gn_ref, dwo_ref, dup_ref, ddown_ref, drw_ref, dfg_ref,
             cols_ref, gcol, ga, gall, hid, act, gmlow, gg):
    cols_ref[...] = jnp.transpose(routes_ref[...])
    R = 128
    ln = lanes(R)
    half = expert_lane(R)
    eidr = lax.broadcasted_iota(i32, (R, E), 1)

    def spread(i, _):
        r0 = pl.multiple_of(i * R, R)
        g = gate_ref[pl.ds(r0, R), :]
        tiles = []
        for j in range(J):
            rj = cols_ref[pl.ds(r0, R), j : j + 1]
            gj = jnp.sum(jnp.where(rj == eidr, g, 0.0), axis=-1, keepdims=True)
            gcol[j, pl.ds(r0, R), :] = jnp.broadcast_to(gj, (R, 128))
            a = att_ref[j, pl.ds(r0, R), :].astype(f32)
            a = jnp.where(ln < H, a, pltpu.roll(a, H, 1)) * gj
            tiles.append((jnp.broadcast_to(rj, (R, 128)) - half, a))
        for p in range(PAIRS):
            acc = jnp.zeros((R, 128), f32)
            for rj, a in tiles:
                acc = jnp.where(rj == 2 * p, a, acc)
            ga[pl.ds(r0, R), p * 128 : (p + 1) * 128] = acc.astype(bf16)
        return 0

    lax.fori_loop(0, T // R, spread, 0)
    x = x_ref[...].astype(f32)
    mixed = x + nn(ga[...], wo_ref[...])
    inv = lax.rsqrt(jnp.mean(mixed * mixed, axis=-1, keepdims=True) + eps)
    n = mixed * inv
    fgain = fgain_ref[...]
    second = (n * fgain).astype(bf16)
    cot = cot_ref[...]
    C = 512
    out = mixed
    gsec = jnp.zeros((T, D), f32)
    for c in range(FF // C):
        cs = slice(c * C, (c + 1) * C)
        v = nn(second, up_ref[:, cs])
        v2 = v * v
        th = jnp.tanh(0.7978845608028654 * (v + 0.044715 * v * v2))
        a = (0.5 * v * (1.0 + th)).astype(bf16)
        act[:, cs] = a
        dth = 0.5 * (1.0 + th) + 0.5 * v * (1.0 - th * th) * (0.7978845608028654 * (1.0 + 0.134145 * v2))
        gh = (nt(cot, down_ref[cs, :]) * dth).astype(bf16)
        out = out + nn(a, down_ref[cs, :])
        gsec = gsec + nt(gh, up_ref[:, cs])
        ddown_ref[cs, :] = tn(a, cot).astype(bf16)
        dup_ref[:, cs] = tn(second, gh).astype(bf16)
    out_ref[...] = out.astype(bf16)
    dfg_ref[...] = jnp.sum(gsec * n, axis=0, keepdims=True)
    hh = gsec * fgain
    gm = cot.astype(f32) + inv * (hh - n * jnp.mean(hh * n, axis=-1, keepdims=True))
    gm_ref[...] = gm
    gml = gm.astype(bf16)
    gmlow[...] = gml
    for c in range(3):
        gall[:, c * 512 : (c + 1) * 512] = nt(gml, wo_ref[c * 512 : (c + 1) * 512, :])

    def grads(i, _):
        r0 = pl.multiple_of(i * R, R)
        inner = jnp.zeros((R, 1), f32)
        ggs = []
        for j in range(J):
            rj = cols_ref[pl.ds(r0, R), j : j + 1]
            rb = jnp.broadcast_to(rj, (R, 128)) - half
            acc = jnp.zeros((R, 128), f32)
            for p in range(PAIRS):
                acc = jnp.where(rb == 2 * p, gall[pl.ds(r0, R), p * 128 : (p + 1) * 128], acc)
            acc = acc + pltpu.roll(acc, H, 1)
            a = att_ref[j, pl.ds(r0, R), :].astype(f32)
            dot = jnp.sum(jnp.where(ln < H, acc * a, 0.0), axis=-1, keepdims=True)
            gj = gcol[j, pl.ds(r0, R), :]
            g1 = gj[:, 0:1]
            inner = inner + g1 * dot
            ggs.append((rj, g1, dot))
            da = acc * gj
            d1, d2, d3 = split3(-jnp.broadcast_to(dot * g1, (R, 128)))
            ft = jnp.where(ln == H, d1, jnp.where(ln == H + 1, d2, jnp.where(ln == H + 2, d3, 0.0)))
            da_ref[j, pl.ds(r0, R), :] = jnp.where(ln < H, da, ft).astype(bf16)
        gl = jnp.zeros((R, E), f32)
        for rj, g1, dot in ggs:
            gl = jnp.where(rj == eidr, g1 * (dot - inner), gl)
        gg[pl.ds(r0, R), :] = gl
        return 0

    lax.fori_loop(0, T // R, grads, 0)
    gl = gg[...]
    hi = gl.astype(bf16)
    lo = (gl - hi.astype(f32)).astype(bf16)
    rw = rw_ref[...]
    gn_ref[...] = nn(hi, rw) + nn(lo, rw)
    nm = normed_ref[...]
    drw_ref[...] = tn(hi, nm) + tn(lo, nm)
    for c in range(3):
        dwo_ref[c * 512 : (c + 1) * 512, :] = tn(ga[:, c * 512 : (c + 1) * 512], gmlow[...]).astype(bf16)


SCRATCH_C = [VM((T, J), i32), VM((J, T, 128), f32), VM((T, EW), bf16), VM((T, EW), f32), VM((8, 128), f32),
             VM((T, FF), bf16), VM((T, D), bf16), VM((T, E), f32)]


def kernel_d(kv_ref, bnd_ref, qa_ref, da_ref, dq_ref, gkv_ref, kaug, vaug, qt, dat, dqacc):
    me = lax.axis_index("expert")
    prepare_keys(kv_ref, bnd_ref, kaug, vaug)
    for j in range(J):
        qt[j] = jnp.transpose(qa_ref[j].astype(f32))[:H].astype(bf16)
        dat[j] = jnp.transpose(da_ref[j].astype(f32))[:H].astype(bf16)
    dqacc[...] = jnp.zeros(dqacc.shape, f32)
    gkv_ref[...] = jnp.zeros(gkv_ref.shape, bf16)

    def block(kb, masked):
        def rows(j, tot):
            p = jnp.exp(nt(qa_ref[j], kaug[kb]))
            if masked:
                p = jnp.where(causal(T, T), p, 0.0)
            ds = (p * nt(da_ref[j], vaug[kb])).astype(bf16)
            dqacc[j] += nn(ds, kv_ref[kb])
            dk = nn(qt[j], ds)
            dv = nn(dat[j], p.astype(bf16))
            return tot + jnp.concatenate([dk, dv], axis=0)

        tot = lax.fori_loop(0, J, rows, jnp.zeros((128, T), f32))
        gkv_ref[kb] = jnp.transpose(tot).astype(bf16)

    lax.fori_loop(0, me, lambda kb, c: (block(kb, False), c)[1], 0)
    block(me, True)
    for j in range(J):
        dq_ref[j] = dqacc[j].astype(bf16)


SCRATCH_D = [VM((NB, T, 128), bf16), VM((NB, T, 128), bf16), VM((J, H, T), bf16), VM((J, H, T), bf16), VM((J, T, 128), f32)]


def kernel_e(dq_ref, routes_ref, wq_ref, normed_ref, gkv_ref, kvw_ref, gn_ref, x_ref, gain_ref, gm_ref,
             dwq_ref, ing_ref, dkvw_ref, dgain_ref, cols_ref, dqs):
    cols_ref[...] = jnp.transpose(routes_ref[...])
    R = 128
    ln = lanes(R)
    half = expert_lane(R)

    def spread(i, _):
        r0 = pl.multiple_of(i * R, R)
        tiles = []
        for j in range(J):
            a = dq_ref[j, pl.ds(r0, R), :].astype(f32)
            a = jnp.where(ln < H, a, pltpu.roll(a, H, 1)) * 0.125
            tiles.append((jnp.broadcast_to(cols_ref[pl.ds(r0, R), j : j + 1], (R, 128)) - half, a))
        for p in range(PAIRS):
            acc = jnp.zeros((R, 128), f32)
            for rj, a in tiles:
                acc = jnp.where(rj == 2 * p, a, acc)
            dqs[pl.ds(r0, R), p * 128 : (p + 1) * 128] = acc.astype(bf16)
        return 0

    lax.fori_loop(0, T // R, spread, 0)
    nm = normed_ref[...]
    for c in range(3):
        dwq_ref[c * 512 : (c + 1) * 512, :] = tn(dqs[:, c * 512 : (c + 1) * 512], nm).astype(bf16)
    gkv = gkv_ref[...]
    dkvw_ref[...] = tn(nm, gkv)
    gn = gn_ref[...] + nn(dqs[...], wq_ref[...]) + nt(gkv, kvw_ref[...])
    x = x_ref[...].astype(f32)
    inv = lax.rsqrt(jnp.mean(x * x, axis=-1, keepdims=True) + eps)
    n = x * inv
    dgain_ref[...] = jnp.sum(gn * n, axis=0, keepdims=True)
    hh = gn * gain_ref[...]
    ing_ref[...] = (gm_ref[...] + inv * (hh - n * jnp.mean(hh * n, axis=-1, keepdims=True))).astype(bf16)


SCRATCH_E = [VM((T, J), i32), VM((T, EW), bf16)]


def call(body, outs, scratch, vmem=56 << 20, flops=0, **kw):
    n = 0
    def run(*args):
        return pl.pallas_call(
            body,
            out_shape=[jax.ShapeDtypeStruct(s, t) for s, t in outs],
            in_specs=[pl.BlockSpec(memory_space=VM)] * len(args),
            out_specs=[pl.BlockSpec(memory_space=VM)] * len(outs),
            scratch_shapes=scratch,
            compiler_params=pltpu.CompilerParams(vmem_limit_bytes=vmem, **kw),
            cost_estimate=pl.CostEstimate(flops=flops, bytes_accessed=1 << 22, transcendentals=0),
        )(*args)
    return run


def per_device(inputs, cotangent, norm_gain, ffn_gain, kv_weight, router_weight, query_weight, output_weight, up_weight,
               down_weight, routes, segment_ids):
    wq = jnp.swapaxes(query_weight, 1, 2).reshape(3 * H, D)
    wo = output_weight.reshape(3 * H, D)
    rw = router_weight.T
    rt = routes.T
    gain = norm_gain.reshape(1, D)
    fgain = ffn_gain.reshape(1, D)
    wq_all = lax.all_gather(wq, "expert", axis=0, tiled=True)
    wo_all = lax.all_gather(wo, "expert", axis=0, tiled=True)
    seg = lax.all_gather(jnp.stack([jnp.sum(segment_ids == 0), jnp.sum(segment_ids <= 1)]), "expert", axis=0)
    seg = jnp.sum(seg, axis=0)
    bnd = jnp.broadcast_to(jnp.concatenate([seg, jnp.zeros((6,), i32)])[:, None], (8, 128))
    normed, kv, gate = call(kernel_a, [((T, D), bf16), ((T, 128), bf16), ((T, E), f32)], [])(
        inputs, gain, kv_weight, rw, rt)
    kv_all = lax.all_gather(kv, "expert", axis=0)
    att, qa = call(kernel_b, [((J, T, 128), bf16), ((J, T, 128), bf16)], SCRATCH_B, flops=1 << 33)(normed, wq_all, rt, bnd, kv_all)
    out, da, gm, gn, dwo, dup, ddown, drw, dfg = call(
        kernel_c,
        [((T, D), bf16), ((J, T, 128), bf16), ((T, D), f32), ((T, D), f32), ((EW, D), bf16), ((D, FF), bf16), ((FF, D), bf16),
         ((E, D), f32), ((1, D), f32)],
        SCRATCH_C, flops=1 << 33)(inputs, cotangent, gate, rt, att, wo_all, up_weight, down_weight, fgain, normed, rw)
    both = ("dp", "expert")
    dup, ddown = lax.psum((dup, ddown), both)
    dwo = lax.psum(lax.psum_scatter(dwo, "expert", scatter_dimension=0, tiled=True), "dp")
    dq, gkv = call(kernel_d, [((J, T, 128), bf16), ((NB, T, 128), bf16)], SCRATCH_D, flops=1 << 35)(kv_all, bnd, qa, da)
    gkv = lax.psum_scatter(gkv, "expert", scatter_dimension=0, tiled=False)
    dwq, ing, dkvw, dgain = call(
        kernel_e, [((EW, D), bf16), ((T, D), bf16), ((D, 128), f32), ((1, D), f32)], SCRATCH_E)(
        dq, rt, wq_all, normed, gkv, kv_weight, gn, inputs, gain, gm)
    dwq = lax.psum(lax.psum_scatter(dwq, "expert", scatter_dimension=0, tiled=True), "dp")
    dkvw, drw, dgain, dfg = lax.psum((dkvw, drw, dgain, dfg), both)
    return (out, ing, dgain.reshape(D), dfg.reshape(D), dkvw, drw.T,
            jnp.swapaxes(dwq.astype(f32).reshape(3, H, D), 1, 2), dwo.astype(f32).reshape(3, H, D),
            dup.astype(f32), ddown.astype(f32))


def solution(mesh):
    both = P(("dp", "expert"), None)
    ex = P("expert", None, None)
    return jax.shard_map(
        per_device, mesh=mesh,
        in_specs=(both, both, P(), P(), P(), P(), ex, ex, P(), P(), both, P(("dp", "expert"))),
        out_specs=(both, both, P(), P(), P(), P(), ex, ex, P(), P()),
        check_vma=False)
```

time: 781 us -> 633 us (0.81)
  waiting for transfers between devices: 193 us -> 455 us
  matrix products: 185 us -> 0 us
  local copies, waits for them, and re-layouts: 140 us -> 3.68 us
  other arithmetic: 85.1 us -> 13.1 us
  Pallas kernels: 0 us -> 54.2 us
  blocking collectives: 131 us -> 91.2 us
  starting transfers between devices: 25.2 us -> 0.31 us
    psum x2 -> x3, waiting for transfers between devices: 129 us -> 316 us  [the longest x1 144 us: per_device(): dkvw, drw, dgain, dfg = lax.psum((dkvw, drw, dgain, dfg), both)]
    dot_general x48 -> x0, matrix products: 185 us -> none  [the longest x15 92.9 us: matmul_right_t(): lax.dot_general(left_side, right_side, (((1,), (1,)), ((), ())), preferre...]
    reduce_scatter x0 -> x3, waiting for transfers between devices: none -> 124 us  [the longest x1 64 us: per_device(): gkv = lax.psum_scatter(gkv, 'expert', scatter_dimension=0, tiled=False)]
    gather x12 -> x0, local copies, waits for them, and re-layouts: 106 us -> none  [the longest x5 27 us: per_device(): gate_weights = soft_rows(jnp.take_along_axis(logits, routes, axis=1))]
    pallas_call x0 -> x5, Pallas kernels: none -> 54.2 us  [run(): pl.pallas_call(body, out_shape=[jax.ShapeDtypeStruct(s, t) for s, t in ou...]
    all_gather x2 -> x1, blocking collectives: 65.3 us -> 14.9 us  [per_device(): kv_all = lax.all_gather(kv, 'expert', axis=0)]
    all_to_all x5 -> x0, waiting for transfers between devices: 49.9 us -> none  [the longest x1 37.8 us: per_device(): lax.all_to_all(send_grad, 'expert', split_axis=0, concat_axis=0, tiled=True)]
    convert_element_type x7 -> x2, other arithmetic: 47.9 us -> 6.89 us  [the longest x1 4.28 us: per_device(): dup.astype(f32)]
  transfers between devices with their start and end apart: 8 -> 8, of which waited for: 5 -> 7; matrix products, arithmetic and copies ran while one was open for 17% -> 2% of each run, Pallas kernels for 0% -> 3%
where the time goes in v1:
time: 633 us; the launch traced here: 632 us
  waiting for transfers between devices  455 us (72%)
  blocking collectives  91.2 us (14%)
  Pallas kernels  54.2 us (9%)
  between operations  14.9 us (2%)
  other arithmetic  13.1 us (2%)
    psum x1, waiting for transfers between devices, per_device(): dkvw, drw, dgain, dfg = lax.psum((dkvw, drw, dgain, dfg), both)  144 us
    psum x1, waiting for transfers between devices, per_device(): dup, ddown = lax.psum((dup, ddown), both)  93.2 us
    psum x1, waiting for transfers between devices, per_device(): lax.psum(lax.psum_scatter(dwq, 'expert', scatter_dimension=0, tiled=True)...  79.2 us
    psum x1, blocking collectives, per_device(): dkvw, drw, dgain, dfg = lax.psum((dkvw, drw, dgain, dfg), both)  65.6 us
    reduce_scatter x1, waiting for transfers between devices, per_device(): gkv = lax.psum_scatter(gkv, 'expert', scatter_dimension=0, tiled=False)  64 us
    pallas_call x5, Pallas kernels, run(): pl.pallas_call(body, out_shape=[jax.ShapeDtypeStruct(s, t) for s, t in ou...  54.2 us
    reduce_scatter x1, waiting for transfers between devices, per_device(): lax.psum_scatter(dwq, 'expert', scatter_dimension=0, tiled=True)  34 us
    reduce_scatter x1, waiting for transfers between devices, per_device(): lax.psum_scatter(dwo, 'expert', scatter_dimension=0, tiled=True)  25.5 us
  transfers between devices with their start and end apart: 8, of which 7 were waited for; matrix products, arithmetic and copies ran while one was open for 2% of the time, Pallas kernels for 3%

profile of v1, /device:TPU:0, one launch (start us, length us, event | category | flops | bytes accessed | tf_op | source)
XLA Modules:
  0.0 632.0 jit_solution(332430581391919257)
XLA Ops:
  7.2 0.7 all-gather.5.cloned.1.call-update
  8.0 0.7 all-gather.7.cloned.1.call-update
  8.7 1.2 dynamic-slice
  10.6 1.3 convert_reduce_fusion.1
  11.9 1.5 add_dynamic-update-slice_fusion
  13.4 10.6 %all-reduce.1 = s32[16]{0:T(128)S(1)} all-reduce(s32[16]{0:T(128)S(1)} %add_dynamic-update-slice_fusion), channel_id=2, replica_groups=mesh['dp'=16,'expert'=8] {'expert'}, use_global_device_ids=true, to_apply=%add.1 | all-reduce | flops 16 | bytes 128
  24.0 0.1 reshape.58
  24.1 2.7 shard_map.195
  26.8 14.9 %all-gather.1 = bf16[3072,128]{1,0:T(8,128)(2,1)} all-gather(bf16[384,128]{1,0:T(8,128)(2,1)} %get-tuple-element.32), channel_id=3, replica_groups=mesh['dp'=16,'expert'=8] {'expert'}, dimensions={0}, use_global_device_ids=true | all-gather | bytes 884736 | tf_op jit(solution)/shard_map/all_gather | solution.py:371
  41.7 0.7 broadcast_in_dim.2.bnd_ref
  42.4 10.4 %shard_map.196 = (bf16[8,384,128]{2,1,0:T(8,128)(2,1)}, bf16[8,384,128]{2,1,0:T(8,128)(2,1)}) custom-call(bf16[384,512]{1,0:T(8,128)(2,1)} %get-tuple-element.31.normed_ref, bf16[1536,512]{1,0:T(8,128)(2,1)} %all-gather.5.cloned.1.call-done.wq_ref, s32[8,384]{1,0:T(8,128)} %bitcast.29, s32[8,128]{1,0:T(8,128)} %broadcast_in_dim.2.bnd_ref, ...), custom_call_target="tpu_custom_call" | custom-call | flops 8589934592 | bytes 4194304 | tf_op jit(solution)/shard_map/pallas_call | solution.py:344
  52.8 11.6 %all-gather.7.cloned.1.call-done.wo_ref = bf16[1536,512]{1,0:T(8,128)(2,1)} async-done(((bf16[192,512]{1,0:T(8,128)(2,1)}), bf16[1536,512]{1,0:T(8,128)(2,1)}) %all-gather.7.cloned.1.call-update) | async-done | bytes 1572880 | tf_op jit(solution)/shard_map/all_gather | solution.py:365
  64.4 24.5 %shard_map.197 = (bf16[384,512]{1,0:T(8,128)(2,1)}, bf16[8,384,128]{2,1,0:T(8,128)(2,1)}, f32[384,512]{1,0:T(8,128)}, f32[384,512]{1,0:T(8,128)}, bf16[1536,512]...) custom-call(bf16[384,512]{1,0:T(8,128)(2,1)} %x_ref.5, ...), custom_call_target="tpu_custom_call" | custom-call | flops 8589934592 | bytes 4194304 | tf_op jit(solution)/shard_map/pallas_call | solution.py:344
  89.0 8.7 %shard_map.198 = (bf16[8,384,128]{2,1,0:T(8,128)(2,1)}, bf16[8,384,128]{2,1,0:T(8,128)(2,1)}) custom-call(bf16[8,384,128]{2,1,0:T(8,128)(2,1)} %bitcast.21, s32[8,128]{1,0:T(8,128)} %broadcast_in_dim.2.bnd_ref, bf16[8,384,128]{2,1,0:T(8,128)(2,1)} %get-tuple-element.35.qa_ref, bf16[8,384,128]{2,1,0:T(8,128)(2,1)} %get-tuple-element.36.da_ref), custom_call_target="tpu_custom_call" | custom-call | flops 34359738368 | bytes 4194304 | tf_op jit(solution)/shard_map/pallas_call | solution.py:344
  97.7 0.0 reduce-scatter.8.cloned.1.call-start
  97.7 0.5 reduce-scatter.8.cloned.1.call-update
  98.3 64.0 %reduce-scatter.4.cloned.1.call-done = bf16[1,384,128]{2,1,0:T(8,128)(2,1)} async-done(((bf16[8,384,128]{2,1,0:T(8,128)(2,1)}), bf16[1,384,128]{2,1,0:T(8,128)(2,1)}) %reduce-scatter.4.cloned.1.call-update) | async-done | bytes 98320 | tf_op jit(solution)/shard_map/reduce_scatter | solution.py:382
  162.4 7.8 %shard_map.199 = (bf16[1536,512]{1,0:T(8,128)(2,1)}, bf16[384,512]{1,0:T(8,128)(2,1)}, f32[512,128]{1,0:T(8,128)}, f32[1,512]{1,0:T(1,128)}) custom-call(bf16[8,384,128]{2,1,0:T(8,128)(2,1)} %get-tuple-element.37.dq_ref, s32[8,384]{1,0:T(8,128)} %bitcast.31, bf16[1536,512]{1,0:T(8,128)(2,1)} %all-gather.5.cloned.1.call-done.wq_ref, ...), custom_call_target="tpu_custom_call" | custom-call | bytes 4194304 | tf_op jit(solution)/shard_map/pallas_call | solution.py:344
  170.2 0.0 all-reduce.11.cloned.1.call-start
  170.2 0.5 all-reduce.11.cloned.1.call-update
  170.8 25.5 %reduce-scatter.8.cloned.1.call-done = bf16[192,512]{1,0:T(8,128)(2,1)} async-done(((bf16[1536,512]{1,0:T(8,128)(2,1)}), bf16[192,512]{1,0:T(8,128)(2,1)}) %reduce-scatter.8.cloned.1.call-update) | async-done | bytes 196624 | tf_op jit(solution)/shard_map/reduce_scatter | solution.py:380
  196.3 34.0 %reduce-scatter.6.cloned.1.call-done = bf16[192,512]{1,0:T(8,128)(2,1)} async-done(((bf16[1536,512]{1,0:T(8,128)(2,1)}), bf16[192,512]{1,0:T(8,128)(2,1)}) %reduce-scatter.6.cloned.1.call-update) | async-done | bytes 196624 | tf_op jit(solution)/shard_map/reduce_scatter | solution.py:386
  230.4 0.7 all-reduce.9.cloned.1.call-update
  231.1 65.6 %all-reduce.2 = (f32[512]{0:T(512)}, f32[512]{0:T(512)}, f32[512,24]{0,1:T(8,128)}) all-reduce(f32[512]{0:T(512)S(1)} %bitcast.37, f32[512]{0:T(512)S(1)} %bitcast.36, f32[512,24]{0,1:T(8,128)S(1)} %bitcast.27), channel_id=1, replica_groups=mesh['dp'=16,'expert'=8] {'dp','expert'}, use_global_device_ids=true, to_apply=%region_4.0 | all-reduce | flops 13312 | bytes 106496 | tf_op jit(solution)/shard_map/psum | solution.py:387
  296.8 93.2 %all-reduce.11.cloned.1.call-done = (bf16[512,2048]{1,0:T(8,128)(2,1)}, bf16[2048,512]{1,0:T(8,128)(2,1)}) async-done(((bf16[512,2048]{1,0:T(8,128)(2,1)}, bf16[2048,512]{1,0:T(8,128)(2,1)}), (bf16[512,2048]{1,0:T(8,128)(2,1)}, bf16[2048,512]{1,0:T(8,128)(2,1)})) %all-reduce.11.cloned.1.call-update) | async-done | bytes 4194320 | tf_op jit(solution)/shard_map/psum | solution.py:379
  390.0 4.3 convert_element_type.16
  394.2 2.6 convert_element_type.17
  396.8 79.2 %all-reduce.13.cloned.1.call-done = (bf16[3,512,64]{1,2,0:T(8,128)(2,1)}, bf16[3,64,512]{2,1,0:T(8,128)(2,1)}) async-done(((bf16[3,512,64]{1,2,0:T(8,128)(2,1)}, bf16[3,64,512]{2,1,0:T(8,128)(2,1)}), (bf16[3,512,64]{1,2,0:T(8,128)(2,1)}, bf16[3,64,512]{2,1,0:T(8,128)(2,1)})) %all-reduce.13.cloned.1.call-update) | async-done | bytes 393232 | tf_op jit(solution)/shard_map/psum | solution.py:386
  476.0 1.7 transpose.24
  477.8 1.7 reshape.57
  479.5 144.0 %all-reduce.9.cloned.1.call-done = f32[512,128]{1,0:T(8,128)} async-done(((f32[512,128]{1,0:T(8,128)}), f32[512,128]{1,0:T(8,128)}) %all-reduce.9.cloned.1.call-update) | async-done | bytes 262160 | tf_op jit(solution)/shard_map/psum | solution.py:387
  623.5 1.7 copy.28
  (21 shorter events, 0.3 us)
Async XLA Ops:
  7.2 34.6 %all-gather.5.cloned.1.call-start = ((), (), s32[]{:S(2)}) async-start(), calls=%async_computation.3 | async-start | bytes 1769472 | tf_op jit(solution)/shard_map/all_gather | solution.py:364
  7.9 56.5 %all-gather.7.cloned.1.call-start = ((), (), s32[]{:S(2)}) async-start(), calls=%async_computation.4 | async-start | bytes 1769472 | tf_op jit(solution)/shard_map/all_gather | solution.py:365
  8.7 153.7 %reduce-scatter.4.cloned.1.call-start = ((), (), s32[]{:S(2)}) async-start(), calls=%async_computation.5 | async-start | bytes 884736 | tf_op jit(solution)/shard_map/reduce_scatter | solution.py:382
  97.7 98.6 %reduce-scatter.8.cloned.1.call-start = ((), (), s32[]{:S(2)}) async-start(), calls=%async_computation.8 | async-start | bytes 1769472 | tf_op jit(solution)/shard_map/reduce_scatter | solution.py:380
  98.3 132.1 %reduce-scatter.6.cloned.1.call-start = ((), (), s32[]{:S(2)}) async-start(), calls=%async_computation.7 | async-start | bytes 1769472 | tf_op jit(solution)/shard_map/reduce_scatter | solution.py:386
  170.2 219.8 %all-reduce.11.cloned.1.call-start = ((), (), s32[]{:S(2)}) async-start(), calls=%async_computation.9 | async-start | bytes 8388608 | tf_op jit(solution)/shard_map/psum | solution.py:379
  170.2 60.9 %copy-start.1 = (f32[24,512]{1,0:T(8,128)S(1)}, f32[24,512]{1,0:T(8,128)}, u32[]{:S(2)}) copy-start(f32[24,512]{1,0:T(8,128)} %get-tuple-element.45) | copy-start | bytes 147460
  170.2 60.9 %copy-start.2 = (f32[1,512]{1,0:T(1,128)S(1)}, f32[1,512]{1,0:T(1,128)}, u32[]{:S(2)}) copy-start(f32[1,512]{1,0:T(1,128)} %get-tuple-element.43) | copy-start | bytes 6148
  170.2 60.9 %copy-start.3 = (f32[1,512]{1,0:T(1,128)S(1)}, f32[1,512]{1,0:T(1,128)}, u32[]{:S(2)}) copy-start(f32[1,512]{1,0:T(1,128)} %get-tuple-element.42) | copy-start | bytes 6148
  170.7 305.3 %all-reduce.13.cloned.1.call-start = ((), (), s32[]{:S(2)}) async-start(), calls=%async_computation.10 | async-start | bytes 786432 | tf_op jit(solution)/shard_map/psum | solution.py:386
  230.4 393.1 %all-reduce.9.cloned.1.call-start = ((), (), s32[]{:S(2)}) async-start(), calls=%async_computation.6 | async-start | bytes 524288 | tf_op jit(solution)/shard_map/psum | solution.py:387
  390.0 4.3 copy-start
Sparse Core Ops, SparseCore 0:
  9.7 28.5 all-gather.4
  40.0 24.3 all-gather.6
  97.8 64.5 reduce-scatter.3
  164.8 31.5 reduce-scatter.7
  198.7 31.5 reduce-scatter.5
  236.7 153.2 all-reduce.10
  393.5 82.4 all-reduce.12
  482.1 141.3 all-reduce.8

commit v2 on v1

v2 whole, which is shorter than its diff:
```python
import functools
import jax
import jax.numpy as jnp
from jax import lax
from jax.experimental import pallas as pl
from jax.experimental.pallas import tpu as pltpu
from jax.sharding import PartitionSpec as P

f32, bf16, i32 = jnp.float32, jnp.bfloat16, jnp.int32
T, D, H, J, E, FF, NB = 384, 512, 64, 8, 24, 2048, 8
EW = E * H
PAIRS = E // 2
HALF_J = 4
ROWS = HALF_J * T
eps = 1e-06
NEG = -1e30
VM = pltpu.VMEM


def nn(a, b):
    return lax.dot_general(a, b, (((1,), (0,)), ((), ())), preferred_element_type=f32)


def nt(a, b):
    return lax.dot_general(a, b, (((1,), (1,)), ((), ())), preferred_element_type=f32)


def tn(a, b):
    return lax.dot_general(a, b, (((0,), (0,)), ((), ())), preferred_element_type=f32)


def lanes(rows):
    return lax.broadcasted_iota(i32, (rows, 128), 1)


def split3(v):
    a = v.astype(bf16).astype(f32)
    b = (v - a).astype(bf16).astype(f32)
    c = (v - a - b).astype(bf16).astype(f32)
    return a, b, c


def causal(rows, cols):
    return lax.broadcasted_iota(i32, (rows, cols), 1) <= lax.broadcasted_iota(i32, (rows, cols), 0)


def segment_of(pos, bounds):
    return (pos >= bounds[0]).astype(i32) + (pos >= bounds[1]).astype(i32)


def expert_lane(rows):
    return (lanes(rows) >= H).astype(i32)


MESH = pl.DeviceIdType.MESH
LINES = [(a, k) for a in "xyz" for k in (1, 2, 3)]
ALL_PEERS = [("c", 0)] + LINES


class Place:
    def __init__(self):
        dp, ex = lax.axis_index("dp"), lax.axis_index("expert")
        self.ex = ex
        self.at = {"x": dp // 4, "y": dp % 4, "z": ex // 2, "c": ex % 2}
        self.peers = {("c", 0): self.device(c=1 - self.at["c"])}
        for axis, k in LINES:
            self.peers[axis, k] = self.device(**{axis: (self.at[axis] + k) % 4})

    def device(self, **moved):
        at = {**self.at, **moved}
        return (at["x"] * 4 + at["y"], at["z"] * 2 + at["c"])

    def enter(self, peers):
        bar = pltpu.get_barrier_semaphore()
        for p in peers:
            pl.semaphore_signal(bar, inc=1, device_id=self.peers[p], device_id_type=MESH)
        pl.semaphore_wait(bar, len(peers))


class Copies:
    def __init__(self, place, send, recv):
        self.place, self.send, self.recv, self.made = place, send, recv, []

    def add(self, src, dst, peer):
        self.made.append((src, dst, peer))
        return len(self.made) - 1

    def get(self, i):
        src, dst, peer = self.made[i]
        return pltpu.make_async_remote_copy(src_ref=src(), dst_ref=dst(), send_sem=self.send.at[i], recv_sem=self.recv.at[i],
                                            device_id=self.place.peers[peer], device_id_type=MESH)

    def start(self, ids):
        for i in ids:
            self.get(i).start()

    def arrived(self, ids):
        for i in ids:
            self.get(i).wait_recv()

    def sent(self, ids):
        for i in ids:
            self.get(i).wait_send()

    def drain(self):
        self.sent(range(len(self.made)))


class Scatter:
    def __init__(self, copies, src, total, r, u0, u1, order):
        self.cp, self.src, self.total, self.r = copies, src, total, r
        self.u0, self.u1 = u0, u1
        at = copies.place.at
        self.c, self.m = at["c"], [at[a] for a in order]
        us = pl.ds(u0, u1 - u0)
        self.ids = [[copies.add(lambda: src.at[us, 1 - self.c], lambda: r[0].at[us], ("c", 0))]]
        for level in (1, 2, 3):
            def piece(k, level=level):
                pre = tuple(self.m[: level - 1])
                return total.at[(us,) + pre + ((self.m[level - 1] + k) % 4,)]
            self.ids.append([
                copies.add(functools.partial(piece, k), lambda k=k, level=level: r[level].at[us, k - 1], (order[level - 1], k))
                for k in (1, 2, 3)])

    def start(self, level):
        self.cp.start(self.ids[level])

    def finish(self, level):
        self.cp.arrived(self.ids[level])
        for u in range(self.u0, self.u1):
            if level == 0:
                for a in range(4):
                    v = self.src[u, self.c, a].astype(f32) + self.r[0][u, a].astype(f32)
                    self.total[u, a] = v.astype(bf16)
                continue
            at = (u,) + tuple(self.m[:level])
            v = self.total[at].astype(f32)
            for k in range(3):
                v = v + self.r[level][u, k].astype(f32)
            self.total[at] = v.astype(bf16)

    def result(self, u):
        return self.total[(u,) + tuple(self.m)]


class Spread:
    def __init__(self, copies, out, u0, u1, order):
        self.cp, self.out = copies, out
        at = copies.place.at
        self.c, self.m = at["c"], [at[a] for a in order]
        us = pl.ds(u0, u1 - u0)
        self.ids = []
        for level in range(4):
            ref = lambda level=level: out.at[(us, self.c) + tuple(self.m[:level])]
            peers = [("c", 0)] if level == 0 else [(order[level - 1], k) for k in (1, 2, 3)]
            self.ids.append([copies.add(ref, ref, p) for p in peers])

    def put(self, u, value):
        self.out[(u, self.c) + tuple(self.m)] = value

    def start(self, level):
        self.cp.start(self.ids[level])

    def finish(self, level):
        self.cp.arrived(self.ids[level])


class SpreadPlane:
    def __init__(self, copies, out, u0, u1):
        self.cp, self.out = copies, out
        self.x, self.y = copies.place.at["x"], copies.place.at["y"]
        us = pl.ds(u0, u1 - u0)
        one = lambda: out.at[us, self.x, self.y]
        row = lambda: out.at[us, self.x]
        self.ids = {"y": [copies.add(one, one, ("y", k)) for k in (1, 2, 3)],
                    "x": [copies.add(row, row, ("x", k)) for k in (1, 2, 3)]}

    def put(self, u, value):
        self.out[u, self.x, self.y] = value

    def start(self, axis):
        self.cp.start(self.ids[axis])

    def finish(self, axis):
        self.cp.arrived(self.ids[axis])


class SmallSum:
    def __init__(self, copies, src, half, r0, r1, by, bz, out):
        self.cp, self.src, self.half, self.r0, self.r1, self.by, self.bz, self.out = copies, src, half, r0, r1, by, bz, out
        at = copies.place.at
        self.c, self.x, self.y, self.z = at["c"], at["x"], at["y"], at["z"]
        own_half = lambda: out.at[self.c]
        own = lambda: out.at[self.c, self.x]
        self.ids = [
            [copies.add(lambda: src.at[1 - self.c], lambda: r0, ("c", 0))],
            [copies.add(lambda k=k: half.at[(self.x + k) % 4], lambda k=k: r1.at[k - 1], ("x", k)) for k in (1, 2, 3)],
            [copies.add(lambda: by.at[self.y], lambda: by.at[self.y], ("y", k)) for k in (1, 2, 3)],
            [copies.add(lambda: bz.at[self.z], lambda: bz.at[self.z], ("z", k)) for k in (1, 2, 3)],
            [copies.add(own, own, ("x", k)) for k in (1, 2, 3)],
            [copies.add(own_half, own_half, ("c", 0))],
        ]

    def step(self, i):
        if i:
            self.cp.arrived(self.ids[i - 1])
        if i == 1:
            for a in range(4):
                self.half[a] = (self.src[self.c, a].astype(f32) + self.r0[a].astype(f32)).astype(bf16)
        if i == 2:
            v = self.half[self.x].astype(f32)
            for k in range(3):
                v = v + self.r1[k].astype(f32)
            self.by[self.y] = v.astype(bf16)
        if i in (3, 4):
            b = self.by if i == 3 else self.bz
            v = (b[0].astype(f32) + b[1].astype(f32) + b[2].astype(f32) + b[3].astype(f32)).astype(bf16)
            if i == 3:
                self.bz[self.z] = v
            else:
                self.out[self.c, self.x] = v
        if i < 6:
            self.cp.start(self.ids[i])


ORDERS = ["xyz", "yzx", "zxy"]
BATCHES = [(0, 4), (4, 8), (8, 11)]
ALL_BATCHES = [(0, 3), (3, 6), (6, 8)]
UP_UNIT, DOWN_UNIT, WO_UNIT = [0, 1, 2, 4], [5, 6, 8, 9], [3, 7, 10]
UNITS = 11
STEPS = [(u, i) for i, u in enumerate(sorted(UP_UNIT + DOWN_UNIT))]


def expert_row(ex, piece, order):
    at = {"x": piece // 4, "y": piece % 4, "z": ex // 2}
    r = ex % 2
    for a in order:
        r = r * 4 + at[a]
    return r * 16


def store_expert(ref, units, ex0, value):
    low = value.astype(bf16)
    for o in range(2):
        for row in range(0, 768, 16):
            v, piece = row // 256, (row % 256) // 16
            ct, r = row // 192, row % 192
            base = expert_row(ex0 + o, piece, ORDERS[v])
            ref[units[v], base : base + 16, :] = low[o * 192 + r : o * 192 + r + 16, ct * 128 : (ct + 1) * 128]


KVR = T + 16


class Gather:
    def __init__(self, copies, out):
        self.cp, self.out = copies, out
        at, ex = copies.place.at, copies.place.ex
        own = lambda: out.at[ex]
        from_z = lambda k: out.at[((at["z"] - k + 4) % 4) * 2 + at["c"]]
        self.line = [copies.add(own, own, ("z", k)) for k in (1, 2, 3)]
        self.core = [copies.add(functools.partial(from_z, k), functools.partial(from_z, k), ("c", 0)) for k in (0, 1, 2, 3)]

    def start(self):
        self.cp.start(self.line)
        self.cp.start(self.core[:1])

    def forward(self):
        for k in range(3):
            self.cp.arrived(self.line[k : k + 1])
            self.cp.start(self.core[k + 1 : k + 2])

    def finish(self):
        self.cp.arrived(self.core)


def bounds_of(kv_ref):
    n0 = n1 = 0.0
    for b in range(NB):
        tail = kv_ref[b, T:KVR, :].astype(f32)
        n0 = n0 + 16.0 * tail[0:1] + tail[1:2]
        n1 = n1 + 16.0 * tail[2:3] + tail[3:4]
    return n0, n1


def prepare_keys(kv_ref, bounds, kaug, vaug):
    ln = lanes(T)
    for b in range(NB):
        kv = kv_ref[b, 0:T, :].astype(f32)
        pos = (lax.broadcasted_iota(i32, (T, 128), 0) + b * T).astype(f32)
        seg = segment_of(pos, bounds)
        feat = jnp.where((ln < H + 3) & (seg != ln - H), NEG, 0.0)
        feat = jnp.where((ln >= H + 3) & (ln < H + 6), 1.0, feat)
        kaug[b] = jnp.where(ln < H, kv, feat).astype(bf16)
        one = jnp.where(ln < H + 3, 1.0, 0.0)
        vaug[b] = jnp.where(ln < H, pltpu.roll(kv, H, 1), one).astype(bf16)


def project_queries(normed_ref, wq_ref, qall):
    normed = normed_ref[...]
    for c in range(4):
        w = wq_ref[2 * c : 2 * c + 2].reshape(2 * 3 * H, D)
        qall[:, c * 384 : (c + 1) * 384] = nt(normed, w) * 0.125


def pick_queries(cols_ref, bounds, me, qall, qa):
    R = 128
    ln = lanes(R)
    half = expert_lane(R)

    def chunk(i, _):
        r0 = pl.multiple_of(i * R, R)
        pos = (lax.broadcasted_iota(i32, (R, 128), 0) + me * T + r0).astype(f32)
        seg = segment_of(pos, bounds)
        feat = jnp.where((ln >= H) & (seg == ln - H), 1.0, 0.0)
        for j in range(J):
            rj = jnp.broadcast_to(cols_ref[pl.ds(r0, R), j : j + 1], (R, 128)) - half
            acc = jnp.zeros((R, 128), f32)
            for p in range(PAIRS):
                acc = jnp.where(rj == 2 * p, qall[pl.ds(r0, R), p * 128 : (p + 1) * 128], acc)
            acc = acc + pltpu.roll(acc, H, 1)
            qa[j, pl.ds(r0, R), :] = jnp.where(ln < H, acc, feat).astype(bf16)
        return 0

    lax.fori_loop(0, T // R, chunk, 0)

def attend_set(me, s, qa, kaug, vaug, att_ref, sbuf, mbuf, acc):
    mbuf[...] = jnp.full(mbuf.shape, NEG, f32)
    acc[...] = jnp.zeros(acc.shape, f32)

    def score(kb, masked):
        for j in range(HALF_J):
            sc = nt(qa[s * HALF_J + j], kaug[kb])
            if masked:
                sc = jnp.where(causal(T, T), sc, NEG)
            sbuf[kb, j] = sc
            m = jnp.maximum(sc[:, 0:128], jnp.maximum(sc[:, 128:256], sc[:, 256:384]))
            mbuf[j] = jnp.maximum(mbuf[j], m)

    lax.fori_loop(0, me, lambda kb, c: (score(kb, False), c)[1], 0)
    score(me, True)
    for j in range(HALF_J):
        mbuf[j] = jnp.broadcast_to(jnp.max(mbuf[j], axis=-1, keepdims=True), (T, 128))

    def weigh(kb, c):
        for j in range(HALF_J):
            m = mbuf[j]
            p = jnp.exp(sbuf[kb, j] - jnp.concatenate([m, m, m], axis=1)).astype(bf16)
            acc[j] += nn(p, vaug[kb])
        return c

    lax.fori_loop(0, me + 1, weigh, 0)
    ln = lanes(T)
    for j in range(HALF_J):
        a = acc[j]
        tot = jnp.broadcast_to(a[:, H : H + 1], (T, 128))
        att_ref[s * HALF_J + j] = (a / tot).astype(bf16)
        l1, l2, l3 = split3(-(mbuf[j] + jnp.log(tot)))
        lse = jnp.where(ln == H + 3, l1, jnp.where(ln == H + 4, l2, l3))
        old = qa[s * HALF_J + j].astype(f32)
        qa[s * HALF_J + j] = jnp.where((ln >= H + 3) & (ln < H + 6), lse, old).astype(bf16)


def kernel_ab(x_ref, gain_ref, kvw_ref, rw_ref, routes_ref, seg_ref, wq_in, wo_in,
              normed_ref, gate_ref, kv_ref, wq_ref, wo_ref, att_ref, qa_ref,
              qall, cols_ref, kaug, vaug, sbuf, mbuf, acc, send, recv):
    place = Place()
    me = place.ex
    copies = Copies(place, send, recv)
    gq, gk, go = Gather(copies, wq_ref), Gather(copies, kv_ref), Gather(copies, wo_ref)
    wq_ref[me] = wq_in[...]
    wo_ref[me] = wo_in[...]
    place.enter([("c", 0)] + [("z", k) for k in (1, 2, 3)])
    gq.start()
    x = x_ref[...].astype(f32)
    inv = lax.rsqrt(jnp.mean(x * x, axis=-1, keepdims=True) + eps)
    normed = (x * inv * gain_ref[...]).astype(bf16)
    normed_ref[...] = normed
    kv_ref[me, 0:T, :] = nn(normed, kvw_ref[...]).astype(bf16)
    seg = seg_ref[...]
    row = lax.broadcasted_iota(i32, (16, 128), 0)
    tail = jnp.zeros((16, 128), f32)
    for s in range(2):
        n = jnp.sum(jnp.sum((seg <= s).astype(f32), axis=0, keepdims=True), axis=1, keepdims=True)
        n = jnp.broadcast_to(n, (16, 128))
        hi = jnp.floor(n * 0.0625)
        tail = jnp.where(row == 2 * s, hi, jnp.where(row == 2 * s + 1, n - 16.0 * hi, tail))
    kv_ref[me, T:KVR, :] = tail.astype(bf16)
    gk.start()
    cols_ref[...] = jnp.transpose(routes_ref[...])
    cols = cols_ref[...]
    logits = nt(normed, rw_ref[...])
    eid = lax.broadcasted_iota(i32, (T, E), 1)
    chosen = cols[:, 0:1] == eid
    for j in range(1, J):
        chosen = chosen | (cols[:, j : j + 1] == eid)
    logits = jnp.where(chosen, logits, NEG)
    top = jnp.max(logits, axis=-1, keepdims=True)
    e = jnp.where(chosen, jnp.exp(logits - top), 0.0)
    gate_ref[...] = e / jnp.sum(e, axis=-1, keepdims=True)
    gq.forward()
    go.start()
    gk.forward()
    gq.finish()
    project_queries(normed_ref, wq_ref, qall)
    gk.finish()
    bounds = bounds_of(kv_ref)
    prepare_keys(kv_ref, bounds, kaug, vaug)
    pick_queries(cols_ref, bounds, me, qall, qa_ref)
    go.forward()
    lax.fori_loop(0, 2, lambda s, c: (attend_set(me, s, qa_ref, kaug, vaug, att_ref, sbuf, mbuf, acc), c)[1], 0)
    go.finish()
    copies.drain()


SCRATCH_AB = [VM((T, EW), f32), VM((T, J), i32), VM((NB, T, 128), bf16), VM((NB, T, 128), bf16),
              VM((NB, HALF_J, T, T), f32), VM((HALF_J, T, 128), f32), VM((HALF_J, T, 128), f32),
              pltpu.SemaphoreType.DMA((21,)), pltpu.SemaphoreType.DMA((21,))]


def kernel_c(x_ref, cot_ref, gate_ref, routes_ref, att_ref, wo_ref, up_ref, down_ref, fgain_ref, normed_ref, rw_ref,
             out_ref, da_ref, gm_ref, gn_ref, big_ref, drw_ref, dfg_ref,
             cols_ref, gcol, ga, gall, act, gmlow, gg):
    cols_ref[...] = jnp.transpose(routes_ref[...])
    R = 128
    ln = lanes(R)
    half = expert_lane(R)
    eidr = lax.broadcasted_iota(i32, (R, E), 1)

    def spread(i, _):
        r0 = pl.multiple_of(i * R, R)
        g = gate_ref[pl.ds(r0, R), :]
        tiles = []
        for j in range(J):
            rj = cols_ref[pl.ds(r0, R), j : j + 1]
            gj = jnp.sum(jnp.where(rj == eidr, g, 0.0), axis=-1, keepdims=True)
            gcol[j, pl.ds(r0, R), :] = jnp.broadcast_to(gj, (R, 128))
            a = att_ref[j, pl.ds(r0, R), :].astype(f32)
            a = jnp.where(ln < H, a, pltpu.roll(a, H, 1)) * gj
            tiles.append((jnp.broadcast_to(rj, (R, 128)) - half, a))
        for p in range(PAIRS):
            acc = jnp.zeros((R, 128), f32)
            for rj, a in tiles:
                acc = jnp.where(rj == 2 * p, a, acc)
            ga[pl.ds(r0, R), p * 128 : (p + 1) * 128] = acc.astype(bf16)
        return 0

    lax.fori_loop(0, T // R, spread, 0)
    x = x_ref[...].astype(f32)
    mixed = x + nn(ga[...], wo_ref[...])
    inv = lax.rsqrt(jnp.mean(mixed * mixed, axis=-1, keepdims=True) + eps)
    n = mixed * inv
    fgain = fgain_ref[...]
    second = (n * fgain).astype(bf16)
    cot = cot_ref[...]
    C = 512
    out = mixed
    gsec = jnp.zeros((T, D), f32)
    for c in range(FF // C):
        cs = slice(c * C, (c + 1) * C)
        v = nn(second, up_ref[:, cs])
        v2 = v * v
        th = jnp.tanh(0.7978845608028654 * (v + 0.044715 * v * v2))
        a = (0.5 * v * (1.0 + th)).astype(bf16)
        act[:, cs] = a
        dth = 0.5 * (1.0 + th) + 0.5 * v * (1.0 - th * th) * (0.7978845608028654 * (1.0 + 0.134145 * v2))
        gh = (nt(cot, down_ref[cs, :]) * dth).astype(bf16)
        out = out + nn(a, down_ref[cs, :])
        gsec = gsec + nt(gh, up_ref[:, cs])
        gdown = tn(a, cot).astype(bf16)
        gup = tn(second, gh).astype(bf16)
        for t in range(4):
            big_ref[DOWN_UNIT[t], cs, :] = gdown[:, t * 128 : (t + 1) * 128]
            big_ref[UP_UNIT[c], t * 512 : (t + 1) * 512, :] = gup[:, t * 128 : (t + 1) * 128]
    out_ref[...] = out.astype(bf16)
    dfg_ref[...] = jnp.sum(gsec * n, axis=0, keepdims=True)
    hh = gsec * fgain
    gm = cot.astype(f32) + inv * (hh - n * jnp.mean(hh * n, axis=-1, keepdims=True))
    gm_ref[...] = gm
    gml = gm.astype(bf16)
    gmlow[...] = gml
    for c in range(3):
        gall[:, c * 512 : (c + 1) * 512] = nt(gml, wo_ref[c * 512 : (c + 1) * 512, :])

    def grads(i, _):
        r0 = pl.multiple_of(i * R, R)
        inner = jnp.zeros((R, 1), f32)
        ggs = []
        for j in range(J):
            rj = cols_ref[pl.ds(r0, R), j : j + 1]
            rb = jnp.broadcast_to(rj, (R, 128)) - half
            acc = jnp.zeros((R, 128), f32)
            for p in range(PAIRS):
                acc = jnp.where(rb == 2 * p, gall[pl.ds(r0, R), p * 128 : (p + 1) * 128], acc)
            acc = acc + pltpu.roll(acc, H, 1)
            a = att_ref[j, pl.ds(r0, R), :].astype(f32)
            dot = jnp.sum(jnp.where(ln < H, acc * a, 0.0), axis=-1, keepdims=True)
            gj = gcol[j, pl.ds(r0, R), :]
            g1 = gj[:, 0:1]
            inner = inner + g1 * dot
            ggs.append((rj, g1, dot))
            da = acc * gj
            d1, d2, d3 = split3(-jnp.broadcast_to(dot * g1, (R, 128)))
            ft = jnp.where(ln == H, d1, jnp.where(ln == H + 1, d2, jnp.where(ln == H + 2, d3, 0.0)))
            da_ref[j, pl.ds(r0, R), :] = jnp.where(ln < H, da, ft).astype(bf16)
        gl = jnp.zeros((R, E), f32)
        for rj, g1, dot in ggs:
            gl = jnp.where(rj == eidr, g1 * (dot - inner), gl)
        gg[pl.ds(r0, R), :] = gl
        return 0

    lax.fori_loop(0, T // R, grads, 0)
    gl = gg[...]
    hi = gl.astype(bf16)
    lo = (gl - hi.astype(f32)).astype(bf16)
    rw = rw_ref[...]
    gn_ref[...] = nn(hi, rw) + nn(lo, rw)
    nm = normed_ref[...]
    drw_ref[...] = tn(hi, nm) + tn(lo, nm)
    for c in range(4):
        store_expert(big_ref, WO_UNIT, 2 * c, tn(ga[:, c * 384 : (c + 1) * 384], gmlow[...]))


SCRATCH_C = [VM((T, J), i32), VM((J, T, 128), f32), VM((T, EW), bf16), VM((T, EW), f32),
             VM((T, FF), bf16), VM((T, D), bf16), VM((T, E), f32)]


def kernel_d(kv_ref, qa_ref, da_ref, big_ref, dq_ref, gkv_ref, red_ref,
             kaug, vaug, qt, dat, dqacc, gsend, grecv, total, r0, r1, r2, r3, send, recv, ksend, krecv):
    place = Place()
    me = place.ex
    dp = lax.axis_index("dp")
    copies = Copies(place, send, recv)
    sums = [Scatter(copies, big_ref, total, (r0, r1, r2, r3), u0, u1, o) for (u0, u1), o in zip(BATCHES, ORDERS)]
    bar = pltpu.get_barrier_semaphore()
    for p in ALL_PEERS:
        pl.semaphore_signal(bar, inc=1, device_id=place.peers[p], device_id_type=MESH)
    for k in range(1, NB):
        pl.semaphore_signal(bar, inc=1, device_id=(dp, (me + k) % NB), device_id_type=MESH)
    pl.semaphore_wait(bar, len(ALL_PEERS) + NB - 1)
    for s in sums:
        s.start(0)
    prepare_keys(kv_ref, bounds_of(kv_ref), kaug, vaug)
    for j in range(J):
        qt[j] = jnp.transpose(qa_ref[j].astype(f32))[:H].astype(bf16)
        dat[j] = jnp.transpose(da_ref[j].astype(f32))[:H].astype(bf16)
    dqacc[...] = jnp.zeros(dqacc.shape, f32)

    def block(kb, masked):
        def rows(j, tot):
            p = jnp.exp(nt(qa_ref[j], kaug[kb]))
            if masked:
                p = jnp.where(causal(T, T), p, 0.0)
            ds = (p * nt(da_ref[j], vaug[kb])).astype(bf16)
            dqacc[j] += nn(ds, kv_ref[kb, 0:T, :])
            dk = nn(qt[j], ds)
            dv = nn(dat[j], p.astype(bf16))
            return tot + jnp.concatenate([dk, dv], axis=0)

        return jnp.transpose(lax.fori_loop(0, J, rows, jnp.zeros((128, T), f32)))

    def to_owner(kb):
        return pltpu.make_async_remote_copy(src_ref=gsend.at[kb], dst_ref=grecv.at[me], send_sem=ksend.at[kb],
                                            recv_sem=krecv.at[me], device_id=(dp, kb), device_id_type=MESH)

    def from_device(b):
        return pltpu.make_async_remote_copy(src_ref=gsend.at[b], dst_ref=grecv.at[b], send_sem=ksend.at[b],
                                            recv_sem=krecv.at[b], device_id=(dp, b), device_id_type=MESH)

    def step(i, carry):
        @pl.when(i < me)
        def _():
            gsend[i] = block(i, False).astype(bf16)
            to_owner(i).start()

        for at, level in ((1, 0), (4, 1), (5, 2), (6, 3)):
            @pl.when(i == at)
            def _(level=level):
                for s in sums:
                    s.finish(level)
                    if level < 3:
                        s.start(level + 1)

        return carry

    lax.fori_loop(0, NB - 1, step, 0)
    own = block(me, True)
    for j in range(J):
        dq_ref[j] = dqacc[j].astype(bf16)
    for s in sums:
        for u in range(s.u0, s.u1):
            red_ref[u] = s.result(u)
    gkv_ref[...] = own
    for b in range(1, NB):
        @pl.when(b > me)
        def _(b=b):
            from_device(b).wait_recv()
            gkv_ref[...] += grecv[b].astype(f32)
    for b in range(NB - 1):
        @pl.when(b < me)
        def _(b=b):
            to_owner(b).wait_send()
    copies.drain()


def dma_sems(n):
    return [pltpu.SemaphoreType.DMA((n,)), pltpu.SemaphoreType.DMA((n,))]


SCRATCH_D = [VM((NB, T, 128), bf16), VM((NB, T, 128), bf16), VM((J, H, T), bf16), VM((J, H, T), bf16), VM((J, T, 128), f32),
             VM((NB, T, 128), bf16), VM((NB, T, 128), bf16),
             VM((UNITS, 4, 4, 4, 16, 128), bf16), VM((UNITS, 4, 4, 4, 16, 128), bf16), VM((UNITS, 3, 4, 4, 16, 128), bf16),
             VM((UNITS, 3, 4, 16, 128), bf16), VM((UNITS, 3, 16, 128), bf16)] + dma_sems(30) + dma_sems(NB)


SMALL = 640


def kernel_e(dq_ref, routes_ref, wq_ref, normed_ref, gkv_ref, kvw_ref, gn_ref, x_ref, gain_ref, gm_ref, drw_ref, dfg_ref, red_ref,
             ing_ref, all_ref, wo_ref, dwq_ref, small_ref,
             cols_ref, dqs, big, total, r0, r1, r2, r3, ssrc, shalf, s0, s1, sy, sz, send, recv):
    place = Place()
    copies = Copies(place, send, recv)
    spreads = [Spread(copies, all_ref, u0, u1, o) for (u0, u1), o in zip(ALL_BATCHES, ORDERS)]
    plane_o = SpreadPlane(copies, wo_ref, 0, 3)
    plane_q = SpreadPlane(copies, dwq_ref, 0, 3)
    big7 = big.reshape(3, 2, 4, 4, 4, 16, 128)
    sums = [Scatter(copies, big7, total, (r0, r1, r2, r3), u, u + 1, o) for u, o in enumerate(ORDERS)]
    small = SmallSum(copies, ssrc, shalf, s0, s1, sy, sz, small_ref)
    for (u0, u1), s in zip(ALL_BATCHES, spreads):
        for u in range(u0, u1):
            s.put(u, red_ref[sorted(UP_UNIT + DOWN_UNIT)[u]])
    for v in range(3):
        plane_o.put(v, red_ref[WO_UNIT[v]])
    place.enter(ALL_PEERS)
    for s in spreads:
        s.start(3)
    plane_o.start("y")
    cols_ref[...] = jnp.transpose(routes_ref[...])
    R = 128
    ln = lanes(R)
    half = expert_lane(R)

    def spread(i, _):
        r_ = pl.multiple_of(i * R, R)
        tiles = []
        for j in range(J):
            a = dq_ref[j, pl.ds(r_, R), :].astype(f32)
            a = jnp.where(ln < H, a, pltpu.roll(a, H, 1)) * 0.125
            tiles.append((jnp.broadcast_to(cols_ref[pl.ds(r_, R), j : j + 1], (R, 128)) - half, a))
        for p in range(PAIRS):
            acc = jnp.zeros((R, 128), f32)
            for rj, a in tiles:
                acc = jnp.where(rj == 2 * p, a, acc)
            dqs[pl.ds(r_, R), p * 128 : (p + 1) * 128] = acc.astype(bf16)
        return 0

    lax.fori_loop(0, T // R, spread, 0)
    nm = normed_ref[...]
    for c in range(4):
        store_expert(big, [0, 1, 2], 2 * c, tn(dqs[:, c * 384 : (c + 1) * 384], nm))
    for s in sums:
        s.start(0)
    for s in spreads:
        s.finish(3)
        s.start(2)
    plane_o.finish("y")
    plane_o.start("x")
    gkv = gkv_ref[...].astype(bf16)
    dkvw = tn(nm, gkv).astype(bf16)
    gn = gn_ref[...] + nn(dqs[...], wq_ref[...]) + nt(gkv, kvw_ref[...])
    x = x_ref[...].astype(f32)
    inv = lax.rsqrt(jnp.mean(x * x, axis=-1, keepdims=True) + eps)
    n = x * inv
    dgain = jnp.sum(gn * n, axis=0, keepdims=True)
    drw = drw_ref[...]
    dfg = dfg_ref[...]
    rows = [dkvw.astype(f32)] + [drw[:, t * 128 : (t + 1) * 128] for t in range(4)]
    rows += [v[:, t * 128 : (t + 1) * 128] for v in (dgain, dfg) for t in range(4)] + [jnp.zeros((SMALL - 616, 128), f32)]
    ssrc[...] = jnp.concatenate(rows, axis=0).astype(bf16).reshape(2, 4, SMALL // 8, 128)
    small.step(0)
    for s in sums:
        s.finish(0)
        s.start(1)
    small.step(1)
    for s in spreads:
        s.finish(2)
        s.start(1)
    plane_o.finish("x")
    hh = gn * gain_ref[...]
    ing_ref[...] = (gm_ref[...] + inv * (hh - n * jnp.mean(hh * n, axis=-1, keepdims=True))).astype(bf16)
    small.step(2)
    for level in (1, 2):
        for s in sums:
            s.finish(level)
            s.start(level + 1)
        small.step(level + 2)
    for s in sums:
        s.finish(3)
    for v in range(3):
        plane_q.put(v, sums[v].result(v))
    plane_q.start("y")
    for s in spreads:
        s.finish(1)
        s.start(0)
    small.step(5)
    plane_q.finish("y")
    plane_q.start("x")
    small.step(6)
    plane_q.finish("x")
    for s in spreads:
        s.finish(0)
    copies.drain()


SCRATCH_E = [VM((T, J), i32), VM((T, EW), bf16), VM((3, 2048, 128), bf16),
             VM((3, 4, 4, 4, 16, 128), bf16), VM((3, 4, 4, 4, 16, 128), bf16), VM((3, 3, 4, 4, 16, 128), bf16),
             VM((3, 3, 4, 16, 128), bf16), VM((3, 3, 16, 128), bf16),
             VM((2, 4, SMALL // 8, 128), bf16), VM((4, SMALL // 8, 128), bf16), VM((4, SMALL // 8, 128), bf16),
             VM((3, SMALL // 8, 128), bf16), VM((4, SMALL // 8, 128), bf16), VM((4, SMALL // 8, 128), bf16)] + dma_sems(86)


def call(body, outs, scratch, vmem=56 << 20, flops=0, **kw):
    n = 0
    def run(*args):
        return pl.pallas_call(
            body,
            out_shape=[jax.ShapeDtypeStruct(s, t) for s, t in outs],
            in_specs=[pl.BlockSpec(memory_space=VM)] * len(args),
            out_specs=[pl.BlockSpec(memory_space=VM)] * len(outs),
            scratch_shapes=scratch,
            compiler_params=pltpu.CompilerParams(vmem_limit_bytes=vmem, **kw),
            cost_estimate=pl.CostEstimate(flops=flops, bytes_accessed=1 << 22, transcendentals=0),
        )(*args)
    return run


def columns(blocks, rows):
    return jnp.swapaxes(blocks, 0, 1).reshape(rows, -1).astype(f32)


def per_device(inputs, cotangent, norm_gain, ffn_gain, kv_weight, router_weight, query_weight, output_weight, up_weight,
               down_weight, routes, segment_ids):
    wq = jnp.swapaxes(query_weight, 1, 2).reshape(3 * H, D)
    wo = output_weight.reshape(3 * H, D)
    rw = router_weight.T
    rt = routes.T
    gain = norm_gain.reshape(1, D)
    fgain = ffn_gain.reshape(1, D)
    normed, gate, kv_all, wq_all, wo_all, att, qa = call(
        kernel_ab,
        [((T, D), bf16), ((T, E), f32), ((NB, KVR, 128), bf16), ((NB, 3 * H, D), bf16), ((NB, 3 * H, D), bf16),
         ((J, T, 128), bf16), ((J, T, 128), bf16)],
        SCRATCH_AB, flops=1 << 33, collective_id=1, has_side_effects=True)(
        inputs, gain, kv_weight, rw, rt, segment_ids.reshape(3, 128), wq, wo)
    wq_all, wo_all = wq_all.reshape(EW, D), wo_all.reshape(EW, D)
    out, da, gm, gn, big, drw, dfg = call(
        kernel_c,
        [((T, D), bf16), ((J, T, 128), bf16), ((T, D), f32), ((T, D), f32), ((UNITS, 2048, 128), bf16), ((E, D), f32), ((1, D), f32)],
        SCRATCH_C, flops=1 << 33)(inputs, cotangent, gate, rt, att, wo_all, up_weight, down_weight, fgain, normed, rw)
    dq, gkv, red = call(
        kernel_d, [((J, T, 128), bf16), ((T, 128), f32), ((UNITS, 16, 128), bf16)],
        SCRATCH_D, flops=1 << 35, collective_id=2, has_side_effects=True)(
        kv_all, qa, da, big.reshape(UNITS, 2, 4, 4, 4, 16, 128))
    ing, shared, dwo, dwq, small = call(
        kernel_e,
        [((T, D), bf16), ((8, 2, 4, 4, 4, 16, 128), bf16), ((3, 4, 4, 16, 128), bf16), ((3, 4, 4, 16, 128), bf16),
         ((2, 4, SMALL // 8, 128), bf16)],
        SCRATCH_E, flops=1 << 32, collective_id=3, has_side_effects=True)(
        dq, rt, wq_all, normed, gkv, kv_weight, gn, inputs, gain, gm, drw, dfg, red)
    shared = shared.reshape(8, 2048, 128)
    slot = {u: i for i, u in enumerate(sorted(UP_UNIT + DOWN_UNIT))}
    dup = columns(jnp.stack([shared[slot[u]] for u in UP_UNIT]).reshape(16, 512, 128), D)
    ddown = columns(jnp.stack([shared[slot[u]] for u in DOWN_UNIT]), FF)
    dwo = columns(dwo.reshape(4, 3 * H, 128), 3 * H).reshape(3, H, D)
    dwq = columns(dwq.reshape(4, 3 * H, 128), 3 * H).reshape(3, H, D)
    small = small.reshape(SMALL, 128).astype(f32)
    drw = columns(small[512:608].reshape(4, E, 128), E)
    return (out, ing, small[608:612].reshape(D), small[612:616].reshape(D), small[:512], drw.T,
            jnp.swapaxes(dwq, 1, 2), dwo, dup, ddown)


def solution(mesh):
    both = P(("dp", "expert"), None)
    ex = P("expert", None, None)
    return jax.shard_map(
        per_device, mesh=mesh,
        in_specs=(both, both, P(), P(), P(), P(), ex, ex, P(), P(), both, P(("dp", "expert"))),
        out_specs=(both, both, P(), P(), P(), P(), ex, ex, P(), P()),
        check_vma=False)
```

time: 633 us -> 185 us (0.29)
  waiting for transfers between devices: 455 us -> 0 us
  Pallas kernels: 54.2 us -> 165 us
  blocking collectives: 91.2 us -> 0 us
  between operations: 14.9 us -> 0.73 us
  local copies, waits for them, and re-layouts: 3.68 us -> 14.1 us
  other arithmetic: 13.1 us -> 4.51 us
    psum x3 -> x0, waiting for transfers between devices: 316 us -> none  [the longest x1 144 us: per_device(): dkvw, drw, dgain, dfg = lax.psum((dkvw, drw, dgain, dfg), both)]
    reduce_scatter x3 -> x0, waiting for transfers between devices: 124 us -> none  [the longest x1 64 us: per_device(): gkv = lax.psum_scatter(gkv, 'expert', scatter_dimension=0, tiled=False)]
    pallas_call x5 -> x4, Pallas kernels: 54.2 us -> 165 us  [run(): pl.pallas_call(body, out_shape=[jax.ShapeDtypeStruct(s, t) for s, t in ou...]
    psum x1 -> x0, blocking collectives: 65.6 us -> none  [per_device(): dkvw, drw, dgain, dfg = lax.psum((dkvw, drw, dgain, dfg), both)]
    all_gather x1 -> x0, blocking collectives: 14.9 us -> none  [per_device(): kv_all = lax.all_gather(kv, 'expert', axis=0)]
    all_gather x2 -> x0, waiting for transfers between devices: 11.6 us -> none  [the longest x1 11.6 us: per_device(): wo_all = lax.all_gather(wo, 'expert', axis=0, tiled=True)]
    unnamed x1 -> x0, blocking collectives: 10.6 us -> none
  transfers between devices with their start and end apart: 8 -> 0, of which waited for: 7 -> 0; matrix products, arithmetic and copies ran while one was open for 2% -> 0% of each run, Pallas kernels for 3% -> 0%
where the time goes in v2:
time: 185 us; the launch traced here: 184 us
  Pallas kernels  165 us (89%)
  local copies, waits for them, and re-layouts  14.1 us (8%)
  other arithmetic  4.51 us (2%)
    pallas_call x4, Pallas kernels, run(): pl.pallas_call(body, out_shape=[jax.ShapeDtypeStruct(s, t) for s, t in ou...  165 us
    unnamed x7, local copies, waits for them, and re-layouts  5.35 us
    slice x1, local copies, waits for them, and re-layouts, per_device(): ddown = columns(jnp.stack([shared[slot[u]] for u in DOWN_UNIT]), FF)  3.89 us

profile of v2, /device:TPU:0, one launch (start us, length us, event | category | flops | bytes accessed | tf_op | source)
XLA Modules:
  0.0 184.4 jit_solution(15057064182863703978)
XLA Ops:
  0.6 35.0 %shard_map.195 = (bf16[384,512]{1,0:T(8,128)(2,1)}, f32[384,24]{1,0:T(8,128)}, bf16[8,400,128]{2,1,0:T(8,128)(2,1)}, bf16[8,192,512]{2,1,0:T(8,128)(2,1)}, bf16[...) custom-call(bf16[384,512]{1,0:T(8,128)(2,1)} %x_ref.5, f32[1,512]{1,0:T(1,128)} %bitcast.84, ...), custom_call_target="tpu_custom_call" | custom-call | flops 8589934592 | bytes 4194304 | tf_op jit(solution)/shard_map/pallas_call | solution.py:726
  35.7 25.2 %shard_map.196 = (bf16[384,512]{1,0:T(8,128)(2,1)}, bf16[8,384,128]{2,1,0:T(8,128)(2,1)}, f32[384,512]{1,0:T(8,128)}, f32[384,512]{1,0:T(8,128)}, bf16[11,2048,1...) custom-call(bf16[384,512]{1,0:T(8,128)(2,1)} %x_ref.5, bf16[384,512]{1,0:T(8,128)(2,1)} %cot_ref.1, ...), custom_call_target="tpu_custom_call" | custom-call | flops 8589934592 | bytes 4194304 | tf_op jit(solution)/shard_map/pallas_call | solution.py:726
  60.9 61.3 %shard_map.197 = (bf16[8,384,128]{2,1,0:T(8,128)(2,1)}, f32[384,128]{1,0:T(8,128)}, bf16[11,16,128]{2,1,0:T(8,128)(2,1)}) custom-call(bf16[8,400,128]{2,1,0:T(8,128)(2,1)} %get-tuple-element.37.kv_ref, bf16[8,384,128]{2,1,0:T(8,128)(2,1)} %get-tuple-element.38.qa_ref, bf16[8,384,128]{2,1,0:T(8,128)(2,1)} %get-tuple-element.39.da_ref, ...), custom_call_target="tpu_custom_call" | custom-call | flops 34359738368 | bytes 4194304 | tf_op jit(solution)/shard_map/pallas_call | solution.py:726
  122.2 43.5 %shard_map.198 = (bf16[384,512]{1,0:T(8,128)(2,1)}, bf16[8,2,4,4,4,16,128]{6,5,4,3,2,1,0:T(8,128)(2,1)}, bf16[3,4,4,16,128]{4,3,2,1,0:T(8,128)(2,1)}, bf16[3,4,4...) custom-call(bf16[8,384,128]{2,1,0:T(8,128)(2,1)} %get-tuple-element.41.dq_ref, s32[8,384]{1,0:T(8,128)} %bitcast.81, ...), custom_call_target="tpu_custom_call" | custom-call | flops 4294967296 | bytes 4194304 | tf_op jit(solution)/shard_map/pallas_call | solution.py:726
  165.7 0.0 copy-start.1
  165.7 1.0 bitcast_convert_fusion
  166.7 0.6 slice_bitcast_fusion
  167.3 0.7 slice.82
  168.0 0.6 copy.34
  168.6 1.0 convert_bitcast_fusion.2
  169.6 0.3 copy.23
  169.9 0.9 reshape.109
  170.8 0.0 copy-done.1
  170.8 0.3 copy.24
  171.1 0.9 reshape.106
  172.0 3.9 %fusion = (bf16[1,2,4,4,4,16,128]{6,5,4,3,2,1,0:T(8,128)(2,1)S(1)}, bf16[1,2,4,4,4,16,128]{6,5,4,3,2,1,0:T(8,128)(2,1)S(1)}, bf16[1,2,4,4,4,16,128]{6,5,4,3,2,1,...) fusion(bf16[8,2,4,4,4,16,128]{6,5,4,3,2,1,0:T(8,128)(2,1)} %get, ...), kind=kLoop, calls=%fused_computation.10 | loop fusion | bytes 8388608 | tf_op jit(solution)/shard_map/slice | solution.py:774
  175.9 2.3 %copy_bitcast_fusion.1 = f32[2048,512]{1,0:T(8,128)} fusion(bf16[1,2048,128]{2,1,0:T(8,128)(2,1)S(1)} %bitcast.62, bf16[1,2048,128]{2,1,0:T(8,128)(2,1)S(1)} %bitcast.63, bf16[1,2048,128]{2,1,0:T(8,128)(2,1)S(1)} %bitcast.64, bf16[1,2048,128]{2,1,0:T(8,128)(2,1)S(1)} %bitcast.61), kind=kLoop, calls=%fused_computation.1 | loop fusion | flops 4194304 | bytes 6291456 | tf_op jit(solution)/shard_map/convert_element_type | solution.py:739
  178.1 0.3 pad_maximum_fusion
  178.4 1.2 copy.25
  179.6 0.0 copy-start
  179.6 4.0 %copy.33 = f32[64,8,16,128]{3,1,2,0:T(8,128)} copy(f32[64,8,16,128]{3,2,1,0:T(8,128)S(1)} %bitcast.58) | data formatting | bytes 8388608
  183.6 0.0 copy-done
  183.6 0.7 copy.36
  (3 shorter events, 0.0 us)
Async XLA Ops:
  165.7 5.1 %copy-start.1 = (bf16[3,4,4,16,128]{4,3,2,1,0:T(8,128)(2,1)S(1)}, bf16[3,4,4,16,128]{4,3,2,1,0:T(8,128)(2,1)}, u32[]{:S(2)}) copy-start(bf16[3,4,4,16,128]{4,3,2,1,0:T(8,128)(2,1)} %get-tuple-element.52) | copy-start | bytes 589828
  179.6 4.0 %copy-start = (bf16[384,512]{1,0:T(8,128)(2,1)S(1)}, bf16[384,512]{1,0:T(8,128)(2,1)}, u32[]{:S(2)}) copy-start(bf16[384,512]{1,0:T(8,128)(2,1)} %get-tuple-element.75) | copy-start | bytes 1179652

commit v3 on v2

--- a/solution.py
+++ b/solution.py
@@ -9,9 +9,9 @@
 f32, bf16, i32 = jnp.float32, jnp.bfloat16, jnp.int32
 T, D, H, J, E, FF, NB = 384, 512, 64, 8, 24, 2048, 8
 EW = E * H
-PAIRS = E // 2
-HALF_J = 4
-ROWS = HALF_J * T
+ROWS = J * T
+SB = 2 * T
+NSB = NB // 2
 eps = 1e-06
 NEG = -1e30
 VM = pltpu.VMEM
@@ -38,18 +38,6 @@
     b = (v - a).astype(bf16).astype(f32)
     c = (v - a - b).astype(bf16).astype(f32)
     return a, b, c
-
-
-def causal(rows, cols):
-    return lax.broadcasted_iota(i32, (rows, cols), 1) <= lax.broadcasted_iota(i32, (rows, cols), 0)
-
-
-def segment_of(pos, bounds):
-    return (pos >= bounds[0]).astype(i32) + (pos >= bounds[1]).astype(i32)
-
-
-def expert_lane(rows):
-    return (lanes(rows) >= H).astype(i32)
 
 
 MESH = pl.DeviceIdType.MESH
@@ -283,87 +271,128 @@
     return n0, n1
 
 
-def prepare_keys(kv_ref, bounds, kaug, vaug):
+def segment_of(pos, bounds):
+    return (pos >= bounds[0]).astype(i32) + (pos >= bounds[1]).astype(i32)
+
+
+def sub8(v):
+    return v.reshape(8, 8, v.shape[-1])
+
+
+def route_rows(rt_ref):
+    return [jnp.broadcast_to(rt_ref[j : j + 1, :], (8, T)) for j in range(J)]
+
+
+def visible(me, sb):
+    key = lax.broadcasted_iota(i32, (T, SB), 1)
+    tok = lax.broadcasted_iota(i32, (T, SB), 0)
+    ok = key - tok <= (me - 2 * sb) * T
+    return ok
+
+
+def prepare_keys(kv_ref, bounds, kaug, vaug, vt):
     ln = lanes(T)
     for b in range(NB):
+        bs = slice(b * T, (b + 1) * T)
         kv = kv_ref[b, 0:T, :].astype(f32)
         pos = (lax.broadcasted_iota(i32, (T, 128), 0) + b * T).astype(f32)
         seg = segment_of(pos, bounds)
         feat = jnp.where((ln < H + 3) & (seg != ln - H), NEG, 0.0)
         feat = jnp.where((ln >= H + 3) & (ln < H + 6), 1.0, feat)
-        kaug[b] = jnp.where(ln < H, kv, feat).astype(bf16)
-        one = jnp.where(ln < H + 3, 1.0, 0.0)
-        vaug[b] = jnp.where(ln < H, pltpu.roll(kv, H, 1), one).astype(bf16)
-
-
-def project_queries(normed_ref, wq_ref, qall):
-    normed = normed_ref[...]
+        kaug[bs, :] = jnp.where(ln < H, kv, feat).astype(bf16)
+        if vaug is not None:
+            one = jnp.where(ln < H + 3, 1.0, 0.0)
+            vaug[bs, :] = jnp.where(ln < H, pltpu.roll(kv, H, 1), one).astype(bf16)
+        if vt is not None:
+            ones = jnp.where(lax.broadcasted_iota(i32, (16, T), 0) == 0, 1.0, 0.0)
+            vt[:, bs] = jnp.concatenate([jnp.transpose(kv)[H:], ones], axis=0).astype(bf16)
+
+
+def project_queries(normed, wq_ref, qall):
     for c in range(4):
         w = wq_ref[2 * c : 2 * c + 2].reshape(2 * 3 * H, D)
-        qall[:, c * 384 : (c + 1) * 384] = nt(normed, w) * 0.125
-
-
-def pick_queries(cols_ref, bounds, me, qall, qa):
-    R = 128
-    ln = lanes(R)
-    half = expert_lane(R)
-
-    def chunk(i, _):
-        r0 = pl.multiple_of(i * R, R)
-        pos = (lax.broadcasted_iota(i32, (R, 128), 0) + me * T + r0).astype(f32)
-        seg = segment_of(pos, bounds)
-        feat = jnp.where((ln >= H) & (seg == ln - H), 1.0, 0.0)
+        qall[c * 48 : (c + 1) * 48] = (nt(w, normed) * 0.125).reshape(48, 8, T)
+
+
+def choose(routes, table, j):
+    acc = table[0:8]
+    for e in range(1, E):
+        acc = jnp.where((routes[j] == e)[None], table[e * 8 : (e + 1) * 8], acc)
+    return acc
+
+
+def to_experts(routes, rows, out):
+    for e in range(E):
+        acc = jnp.zeros((8, 8, T), f32)
         for j in range(J):
-            rj = jnp.broadcast_to(cols_ref[pl.ds(r0, R), j : j + 1], (R, 128)) - half
-            acc = jnp.zeros((R, 128), f32)
-            for p in range(PAIRS):
-                acc = jnp.where(rj == 2 * p, qall[pl.ds(r0, R), p * 128 : (p + 1) * 128], acc)
-            acc = acc + pltpu.roll(acc, H, 1)
-            qa[j, pl.ds(r0, R), :] = jnp.where(ln < H, acc, feat).astype(bf16)
-        return 0
-
-    lax.fori_loop(0, T // R, chunk, 0)
-
-def attend_set(me, s, qa, kaug, vaug, att_ref, sbuf, mbuf, acc):
-    mbuf[...] = jnp.full(mbuf.shape, NEG, f32)
-    acc[...] = jnp.zeros(acc.shape, f32)
-
-    def score(kb, masked):
-        for j in range(HALF_J):
-            sc = nt(qa[s * HALF_J + j], kaug[kb])
+            acc = jnp.where((routes[j] == e)[None], rows[j], acc)
+        out[e * H : (e + 1) * H, :] = acc.reshape(H, T).astype(bf16)
+
+
+def pick_queries(rt_ref, bounds, me, qall, qt):
+    routes = route_rows(rt_ref)
+    pos = (lax.broadcasted_iota(i32, (H, T), 1) + me * T).astype(f32)
+    seg = segment_of(pos, (bounds[0][:, 0:1], bounds[1][:, 0:1]))
+    feat = jnp.where(lax.broadcasted_iota(i32, (H, T), 0) == seg, 1.0, 0.0).astype(bf16)
+    for j in range(J):
+        qt[0:H, j * T : (j + 1) * T] = choose(routes, qall, j).reshape(H, T).astype(bf16)
+        qt[H:, j * T : (j + 1) * T] = feat
+
+
+def attend(me, qt, kaug, vt, att, sbuf, macc, acc):
+    last = me // 2
+
+    def group(g, carry):
+        gs = pl.ds(pl.multiple_of(g * SB, SB), SB)
+        q = qt[:, gs]
+        macc[...] = jnp.full(macc.shape, NEG, f32)
+
+        def score(sb, masked):
+            s = nn(kaug[pl.ds(pl.multiple_of(sb * SB, SB), SB), :], q)
             if masked:
-                sc = jnp.where(causal(T, T), sc, NEG)
-            sbuf[kb, j] = sc
-            m = jnp.maximum(sc[:, 0:128], jnp.maximum(sc[:, 128:256], sc[:, 256:384]))
-            mbuf[j] = jnp.maximum(mbuf[j], m)
-
-    lax.fori_loop(0, me, lambda kb, c: (score(kb, False), c)[1], 0)
-    score(me, True)
-    for j in range(HALF_J):
-        mbuf[j] = jnp.broadcast_to(jnp.max(mbuf[j], axis=-1, keepdims=True), (T, 128))
-
-    def weigh(kb, c):
-        for j in range(HALF_J):
-            m = mbuf[j]
-            p = jnp.exp(sbuf[kb, j] - jnp.concatenate([m, m, m], axis=1)).astype(bf16)
-            acc[j] += nn(p, vaug[kb])
-        return c
-
-    lax.fori_loop(0, me + 1, weigh, 0)
-    ln = lanes(T)
-    for j in range(HALF_J):
-        a = acc[j]
-        tot = jnp.broadcast_to(a[:, H : H + 1], (T, 128))
-        att_ref[s * HALF_J + j] = (a / tot).astype(bf16)
-        l1, l2, l3 = split3(-(mbuf[j] + jnp.log(tot)))
-        lse = jnp.where(ln == H + 3, l1, jnp.where(ln == H + 4, l2, l3))
-        old = qa[s * HALF_J + j].astype(f32)
-        qa[s * HALF_J + j] = jnp.where((ln >= H + 3) & (ln < H + 6), lse, old).astype(bf16)
-
-
-def kernel_ab(x_ref, gain_ref, kvw_ref, rw_ref, routes_ref, seg_ref, wq_in, wo_in,
-              normed_ref, gate_ref, kv_ref, wq_ref, wo_ref, att_ref, qa_ref,
-              qall, cols_ref, kaug, vaug, sbuf, mbuf, acc, send, recv):
+                key = lax.broadcasted_iota(i32, (SB, T), 0)
+                tok = lax.broadcasted_iota(i32, (SB, T), 1)
+                ok = key - tok <= (me - 2 * sb) * T
+                s = jnp.where(jnp.concatenate([ok, ok], axis=1), s, NEG)
+            sbuf[sb] = s
+            macc[...] = jnp.maximum(macc[...], jnp.max(s.reshape(SB // 8, 8, SB), axis=0))
+
+        lax.fori_loop(0, last, lambda sb, c: (score(sb, False), c)[1], 0)
+        score(last, True)
+        m = jnp.max(macc[...], axis=0, keepdims=True)
+        macc[...] = jnp.broadcast_to(m, macc.shape)
+        acc[...] = jnp.zeros(acc.shape, f32)
+
+        def weigh(sb, c):
+            p = jnp.exp(sbuf[sb].reshape(SB // 8, 8, SB) - macc[...][None]).reshape(SB, SB).astype(bf16)
+            acc[...] += nn(vt[:, pl.ds(pl.multiple_of(sb * SB, SB), SB)], p)
+            return c
+
+        lax.fori_loop(0, last + 1, weigh, 0)
+        tot = acc[H : H + 1, :]
+        att[:, gs] = (acc[0:H, :] / tot).astype(bf16)
+        l1, l2, l3 = split3(-(m + jnp.log(tot)))
+        row = lax.broadcasted_iota(i32, (16, SB), 0)
+        old = q[H : H + 16].astype(f32)
+        new = jnp.where(row == 3, l1, jnp.where(row == 4, l2, jnp.where(row == 5, l3, old)))
+        qt[H : H + 16, gs] = new.astype(bf16)
+        return carry
+
+    lax.fori_loop(0, J // 2, group, 0)
+
+
+def gates_of(normed, rw_ref, rt_ref, gate_ref):
+    logits = nt(rw_ref[...], normed)
+    eid = lax.broadcasted_iota(i32, (E, T), 0)
+    per = [jnp.sum(jnp.where(rt_ref[j : j + 1, :] == eid, logits, 0.0), axis=0, keepdims=True) for j in range(J)]
+    v = jnp.concatenate(per, axis=0)
+    e = jnp.exp(v - jnp.max(v, axis=0, keepdims=True))
+    gate_ref[...] = e / jnp.sum(e, axis=0, keepdims=True)
+
+
+def kernel_ab(x_ref, gain_ref, kvw_ref, rw_ref, rt_ref, seg_ref, wq_in, wo_in,
+              normed_ref, gate_ref, kv_ref, wq_ref, wo_ref, att_ref, qt_ref,
+              qall, kaug, vt, sbuf, macc, acc, send, recv):
     place = Place()
     me = place.ex
     copies = Copies(place, send, recv)
@@ -387,71 +416,43 @@
         tail = jnp.where(row == 2 * s, hi, jnp.where(row == 2 * s + 1, n - 16.0 * hi, tail))
     kv_ref[me, T:KVR, :] = tail.astype(bf16)
     gk.start()
-    cols_ref[...] = jnp.transpose(routes_ref[...])
-    cols = cols_ref[...]
-    logits = nt(normed, rw_ref[...])
-    eid = lax.broadcasted_iota(i32, (T, E), 1)
-    chosen = cols[:, 0:1] == eid
-    for j in range(1, J):
-        chosen = chosen | (cols[:, j : j + 1] == eid)
-    logits = jnp.where(chosen, logits, NEG)
-    top = jnp.max(logits, axis=-1, keepdims=True)
-    e = jnp.where(chosen, jnp.exp(logits - top), 0.0)
-    gate_ref[...] = e / jnp.sum(e, axis=-1, keepdims=True)
+    gates_of(normed, rw_ref, rt_ref, gate_ref)
     gq.forward()
     go.start()
     gk.forward()
     gq.finish()
-    project_queries(normed_ref, wq_ref, qall)
+    project_queries(normed, wq_ref, qall)
     gk.finish()
     bounds = bounds_of(kv_ref)
-    prepare_keys(kv_ref, bounds, kaug, vaug)
-    pick_queries(cols_ref, bounds, me, qall, qa_ref)
+    prepare_keys(kv_ref, bounds, kaug, None, vt)
+    pick_queries(rt_ref, bounds, me, qall, qt_ref)
     go.forward()
-    lax.fori_loop(0, 2, lambda s, c: (attend_set(me, s, qa_ref, kaug, vaug, att_ref, sbuf, mbuf, acc), c)[1], 0)
+    attend(me, qt_ref, kaug, vt, att_ref, sbuf, macc, acc)
     go.finish()
     copies.drain()
 
 
-SCRATCH_AB = [VM((T, EW), f32), VM((T, J), i32), VM((NB, T, 128), bf16), VM((NB, T, 128), bf16),
-              VM((NB, HALF_J, T, T), f32), VM((HALF_J, T, 128), f32), VM((HALF_J, T, 128), f32),
-              pltpu.SemaphoreType.DMA((21,)), pltpu.SemaphoreType.DMA((21,))]
-
-
-def kernel_c(x_ref, cot_ref, gate_ref, routes_ref, att_ref, wo_ref, up_ref, down_ref, fgain_ref, normed_ref, rw_ref,
-             out_ref, da_ref, gm_ref, gn_ref, big_ref, drw_ref, dfg_ref,
-             cols_ref, gcol, ga, gall, act, gmlow, gg):
-    cols_ref[...] = jnp.transpose(routes_ref[...])
-    R = 128
-    ln = lanes(R)
-    half = expert_lane(R)
-    eidr = lax.broadcasted_iota(i32, (R, E), 1)
-
-    def spread(i, _):
-        r0 = pl.multiple_of(i * R, R)
-        g = gate_ref[pl.ds(r0, R), :]
-        tiles = []
-        for j in range(J):
-            rj = cols_ref[pl.ds(r0, R), j : j + 1]
-            gj = jnp.sum(jnp.where(rj == eidr, g, 0.0), axis=-1, keepdims=True)
-            gcol[j, pl.ds(r0, R), :] = jnp.broadcast_to(gj, (R, 128))
-            a = att_ref[j, pl.ds(r0, R), :].astype(f32)
-            a = jnp.where(ln < H, a, pltpu.roll(a, H, 1)) * gj
-            tiles.append((jnp.broadcast_to(rj, (R, 128)) - half, a))
-        for p in range(PAIRS):
-            acc = jnp.zeros((R, 128), f32)
-            for rj, a in tiles:
-                acc = jnp.where(rj == 2 * p, a, acc)
-            ga[pl.ds(r0, R), p * 128 : (p + 1) * 128] = acc.astype(bf16)
-        return 0
-
-    lax.fori_loop(0, T // R, spread, 0)
+def dma_sems(n):
+    return [pltpu.SemaphoreType.DMA((n,)), pltpu.SemaphoreType.DMA((n,))]
+
+
+SCRATCH_AB = [VM((EW // 8, 8, T), f32), VM((ROWS, 128), bf16), VM((80, ROWS), bf16),
+              VM((NSB, SB, SB), f32), VM((8, SB), f32), VM((80, SB), f32)] + dma_sems(21)
+
+
+def kernel_c(x_ref, cot_ref, gate_ref, rt_ref, att_ref, wo_ref, up_ref, down_ref, fgain_ref, normed_ref, rw_ref,
+             out_ref, dat_ref, gm_ref, gn_ref, big_ref, drw_ref, dfg_ref, rows, gat, gall):
+    routes = route_rows(rt_ref)
+    for j in range(J):
+        rows[j] = sub8(att_ref[:, j * T : (j + 1) * T].astype(f32) * gate_ref[j : j + 1, :])
+    to_experts(routes, rows, gat)
     x = x_ref[...].astype(f32)
-    mixed = x + nn(ga[...], wo_ref[...])
+    mixed = x + tn(gat[...], wo_ref[...])
     inv = lax.rsqrt(jnp.mean(mixed * mixed, axis=-1, keepdims=True) + eps)
     n = mixed * inv
     fgain = fgain_ref[...]
     second = (n * fgain).astype(bf16)
+    second_t = jnp.transpose(n * fgain).astype(bf16)
     cot = cot_ref[...]
     C = 512
     out = mixed
@@ -462,13 +463,12 @@
         v2 = v * v
         th = jnp.tanh(0.7978845608028654 * (v + 0.044715 * v * v2))
         a = (0.5 * v * (1.0 + th)).astype(bf16)
-        act[:, cs] = a
         dth = 0.5 * (1.0 + th) + 0.5 * v * (1.0 - th * th) * (0.7978845608028654 * (1.0 + 0.134145 * v2))
         gh = (nt(cot, down_ref[cs, :]) * dth).astype(bf16)
         out = out + nn(a, down_ref[cs, :])
         gsec = gsec + nt(gh, up_ref[:, cs])
         gdown = tn(a, cot).astype(bf16)
-        gup = tn(second, gh).astype(bf16)
+        gup = nn(second_t, gh).astype(bf16)
         for t in range(4):
             big_ref[DOWN_UNIT[t], cs, :] = gdown[:, t * 128 : (t + 1) * 128]
             big_ref[UP_UNIT[c], t * 512 : (t + 1) * 512, :] = gup[:, t * 128 : (t + 1) * 128]
@@ -478,55 +478,41 @@
     gm = cot.astype(f32) + inv * (hh - n * jnp.mean(hh * n, axis=-1, keepdims=True))
     gm_ref[...] = gm
     gml = gm.astype(bf16)
-    gmlow[...] = gml
-    for c in range(3):
-        gall[:, c * 512 : (c + 1) * 512] = nt(gml, wo_ref[c * 512 : (c + 1) * 512, :])
-
-    def grads(i, _):
-        r0 = pl.multiple_of(i * R, R)
-        inner = jnp.zeros((R, 1), f32)
-        ggs = []
-        for j in range(J):
-            rj = cols_ref[pl.ds(r0, R), j : j + 1]
-            rb = jnp.broadcast_to(rj, (R, 128)) - half
-            acc = jnp.zeros((R, 128), f32)
-            for p in range(PAIRS):
-                acc = jnp.where(rb == 2 * p, gall[pl.ds(r0, R), p * 128 : (p + 1) * 128], acc)
-            acc = acc + pltpu.roll(acc, H, 1)
-            a = att_ref[j, pl.ds(r0, R), :].astype(f32)
-            dot = jnp.sum(jnp.where(ln < H, acc * a, 0.0), axis=-1, keepdims=True)
-            gj = gcol[j, pl.ds(r0, R), :]
-            g1 = gj[:, 0:1]
-            inner = inner + g1 * dot
-            ggs.append((rj, g1, dot))
-            da = acc * gj
-            d1, d2, d3 = split3(-jnp.broadcast_to(dot * g1, (R, 128)))
-            ft = jnp.where(ln == H, d1, jnp.where(ln == H + 1, d2, jnp.where(ln == H + 2, d3, 0.0)))
-            da_ref[j, pl.ds(r0, R), :] = jnp.where(ln < H, da, ft).astype(bf16)
-        gl = jnp.zeros((R, E), f32)
-        for rj, g1, dot in ggs:
-            gl = jnp.where(rj == eidr, g1 * (dot - inner), gl)
-        gg[pl.ds(r0, R), :] = gl
-        return 0
-
-    lax.fori_loop(0, T // R, grads, 0)
-    gl = gg[...]
+    for c in range(4):
+        gall[c * 48 : (c + 1) * 48] = nt(wo_ref[c * 384 : (c + 1) * 384, :], gml).reshape(48, 8, T)
+    dots = []
+    row = lax.broadcasted_iota(i32, (H, T), 0)
+    for j in range(J):
+        js = slice(j * T, (j + 1) * T)
+        g = choose(routes, gall, j).reshape(H, T)
+        gate = gate_ref[j : j + 1, :]
+        dot = jnp.sum(g * att_ref[:, js].astype(f32), axis=0, keepdims=True)
+        dots.append(dot)
+        d1, d2, d3 = split3(-(dot * gate))
+        dat_ref[0:H, js] = (g * gate).astype(bf16)
+        dat_ref[H:, js] = jnp.where(row == 0, d1, jnp.where(row == 1, d2, jnp.where(row == 2, d3, 0.0))).astype(bf16)
+    dots = jnp.concatenate(dots, axis=0)
+    gates = gate_ref[...]
+    chosen = gates * (dots - jnp.sum(gates * dots, axis=0, keepdims=True))
+    eid = lax.broadcasted_iota(i32, (E, T), 0)
+    gl = jnp.zeros((E, T), f32)
+    for j in range(J):
+        gl = jnp.where(rt_ref[j : j + 1, :] == eid, chosen[j : j + 1, :], gl)
     hi = gl.astype(bf16)
     lo = (gl - hi.astype(f32)).astype(bf16)
     rw = rw_ref[...]
-    gn_ref[...] = nn(hi, rw) + nn(lo, rw)
+    gn_ref[...] = tn(hi, rw) + tn(lo, rw)
     nm = normed_ref[...]
-    drw_ref[...] = tn(hi, nm) + tn(lo, nm)
+    drw_ref[...] = nn(hi, nm) + nn(lo, nm)
     for c in range(4):
-        store_expert(big_ref, WO_UNIT, 2 * c, tn(ga[:, c * 384 : (c + 1) * 384], gmlow[...]))
-
-
-SCRATCH_C = [VM((T, J), i32), VM((J, T, 128), f32), VM((T, EW), bf16), VM((T, EW), f32),
-             VM((T, FF), bf16), VM((T, D), bf16), VM((T, E), f32)]
-
-
-def kernel_d(kv_ref, qa_ref, da_ref, big_ref, dq_ref, gkv_ref, red_ref,
-             kaug, vaug, qt, dat, dqacc, gsend, grecv, total, r0, r1, r2, r3, send, recv, ksend, krecv):
+        store_expert(big_ref, WO_UNIT, 2 * c, nn(gat[c * 384 : (c + 1) * 384, :], gml))
+
+
+SCRATCH_C = [VM((J, 8, 8, T), f32), VM((EW, T), bf16), VM((EW // 8, 8, T), f32)]
+
+
+def kernel_d(kv_ref, qt_ref, dat_ref, big_ref, dq_ref, gkv_ref, red_ref,
+             kaug, vaug, qa, da, dqacc, tot, gsend, grecv, total, r0, r1, r2, r3, send, recv, ksend, krecv):
     place = Place()
     me = place.ex
     dp = lax.axis_index("dp")
@@ -540,24 +526,39 @@
     pl.semaphore_wait(bar, len(ALL_PEERS) + NB - 1)
     for s in sums:
         s.start(0)
-    prepare_keys(kv_ref, bounds_of(kv_ref), kaug, vaug)
+    prepare_keys(kv_ref, bounds_of(kv_ref), kaug, vaug, None)
     for j in range(J):
-        qt[j] = jnp.transpose(qa_ref[j].astype(f32))[:H].astype(bf16)
-        dat[j] = jnp.transpose(da_ref[j].astype(f32))[:H].astype(bf16)
+        js = slice(j * T, (j + 1) * T)
+        qa[js, :] = jnp.transpose(qt_ref[:, js].astype(f32)).astype(bf16)
+        da[js, :] = jnp.transpose(dat_ref[:, js].astype(f32)).astype(bf16)
     dqacc[...] = jnp.zeros(dqacc.shape, f32)
-
-    def block(kb, masked):
-        def rows(j, tot):
-            p = jnp.exp(nt(qa_ref[j], kaug[kb]))
+    last = me // 2
+
+    def block(sb, masked):
+        ks = pl.ds(pl.multiple_of(sb * SB, SB), SB)
+        tot[...] = jnp.zeros(tot.shape, f32)
+
+        def rows(g):
+            gs = pl.ds(pl.multiple_of(g * SB, SB), SB)
+            p = jnp.exp(nt(qa[gs, :], kaug[ks, :]))
             if masked:
-                p = jnp.where(causal(T, T), p, 0.0)
-            ds = (p * nt(da_ref[j], vaug[kb])).astype(bf16)
-            dqacc[j] += nn(ds, kv_ref[kb, 0:T, :])
-            dk = nn(qt[j], ds)
-            dv = nn(dat[j], p.astype(bf16))
-            return tot + jnp.concatenate([dk, dv], axis=0)
-
-        return jnp.transpose(lax.fori_loop(0, J, rows, jnp.zeros((128, T), f32)))
+                ok = visible(me, sb)
+                p = jnp.where(jnp.concatenate([ok, ok], axis=0), p, 0.0)
+            ds = (p * nt(da[gs, :], vaug[ks, :])).astype(bf16)
+            kv = jnp.concatenate([kv_ref[2 * sb, 0:T, :], kv_ref[2 * sb + 1, 0:T, :]], axis=0)
+            dqacc[gs, :] += nn(ds, kv)
+            tot[0:H, :] += nn(qt_ref[0:H, gs], ds)
+            tot[H:, :] += nn(dat_ref[0:H, gs], p.astype(bf16))
+
+        def two(i, c):
+            rows(2 * i)
+            rows(2 * i + 1)
+            return c
+
+        lax.fori_loop(0, J // 4, two, 0)
+        low = jnp.transpose(tot[...]).astype(bf16)
+        gsend[2 * sb] = low[0:T]
+        gsend[2 * sb + 1] = low[T:]
 
     def to_owner(kb):
         return pltpu.make_async_remote_copy(src_ref=gsend.at[kb], dst_ref=grecv.at[me], send_sem=ksend.at[kb],
@@ -568,29 +569,39 @@
                                             recv_sem=krecv.at[b], device_id=(dp, b), device_id_type=MESH)
 
     def step(i, carry):
-        @pl.when(i < me)
+        @pl.when(i < last)
         def _():
-            gsend[i] = block(i, False).astype(bf16)
-            to_owner(i).start()
-
-        for at, level in ((1, 0), (4, 1), (5, 2), (6, 3)):
+            block(i, False)
+            to_owner(2 * i).start()
+            to_owner(2 * i + 1).start()
+
+        for at, level in ((0, 0), (2, 1)):
             @pl.when(i == at)
             def _(level=level):
                 for s in sums:
                     s.finish(level)
-                    if level < 3:
-                        s.start(level + 1)
+                    s.start(level + 1)
 
         return carry
 
-    lax.fori_loop(0, NB - 1, step, 0)
-    own = block(me, True)
+    lax.fori_loop(0, NSB - 1, step, 0)
+    block(last, True)
+
+    @pl.when(2 * last < me)
+    def _():
+        to_owner(2 * last).start()
+
+    for s in sums:
+        s.finish(2)
+        s.start(3)
     for j in range(J):
-        dq_ref[j] = dqacc[j].astype(bf16)
+        js = slice(j * T, (j + 1) * T)
+        dq_ref[:, js] = jnp.transpose(dqacc[js, :])[0:H].astype(bf16)
     for s in sums:
+        s.finish(3)
         for u in range(s.u0, s.u1):
             red_ref[u] = s.result(u)
-    gkv_ref[...] = own
+    gkv_ref[...] = gsend[me].astype(f32)
     for b in range(1, NB):
         @pl.when(b > me)
         def _(b=b):
@@ -603,12 +614,8 @@
     copies.drain()
 
 
-def dma_sems(n):
-    return [pltpu.SemaphoreType.DMA((n,)), pltpu.SemaphoreType.DMA((n,))]
-
-
-SCRATCH_D = [VM((NB, T, 128), bf16), VM((NB, T, 128), bf16), VM((J, H, T), bf16), VM((J, H, T), bf16), VM((J, T, 128), f32),
-             VM((NB, T, 128), bf16), VM((NB, T, 128), bf16),
+SCRATCH_D = [VM((ROWS, 128), bf16), VM((ROWS, 128), bf16), VM((ROWS, 128), bf16), VM((ROWS, 128), bf16), VM((ROWS, 128), f32),
+             VM((128, SB), f32), VM((NB, T, 128), bf16), VM((NB, T, 128), bf16),
              VM((UNITS, 4, 4, 4, 16, 128), bf16), VM((UNITS, 4, 4, 4, 16, 128), bf16), VM((UNITS, 3, 4, 4, 16, 128), bf16),
              VM((UNITS, 3, 4, 16, 128), bf16), VM((UNITS, 3, 16, 128), bf16)] + dma_sems(30) + dma_sems(NB)
 
@@ -616,9 +623,9 @@
 SMALL = 640
 
 
-def kernel_e(dq_ref, routes_ref, wq_ref, normed_ref, gkv_ref, kvw_ref, gn_ref, x_ref, gain_ref, gm_ref, drw_ref, dfg_ref, red_ref,
+def kernel_e(dq_ref, rt_ref, wq_ref, normed_ref, gkv_ref, kvw_ref, gn_ref, x_ref, gain_ref, gm_ref, drw_ref, dfg_ref, red_ref,
              ing_ref, all_ref, wo_ref, dwq_ref, small_ref,
-             cols_ref, dqs, big, total, r0, r1, r2, r3, ssrc, shalf, s0, s1, sy, sz, send, recv):
+             rows, dqs, big, total, r0, r1, r2, r3, ssrc, shalf, s0, s1, sy, sz, send, recv):
     place = Place()
     copies = Copies(place, send, recv)
     spreads = [Spread(copies, all_ref, u0, u1, o) for (u0, u1), o in zip(ALL_BATCHES, ORDERS)]
@@ -636,29 +643,13 @@
     for s in spreads:
         s.start(3)
     plane_o.start("y")
-    cols_ref[...] = jnp.transpose(routes_ref[...])
-    R = 128
-    ln = lanes(R)
-    half = expert_lane(R)
-
-    def spread(i, _):
-        r_ = pl.multiple_of(i * R, R)
-        tiles = []
-        for j in range(J):
-            a = dq_ref[j, pl.ds(r_, R), :].astype(f32)
-            a = jnp.where(ln < H, a, pltpu.roll(a, H, 1)) * 0.125
-            tiles.append((jnp.broadcast_to(cols_ref[pl.ds(r_, R), j : j + 1], (R, 128)) - half, a))
-        for p in range(PAIRS):
-            acc = jnp.zeros((R, 128), f32)
-            for rj, a in tiles:
-                acc = jnp.where(rj == 2 * p, a, acc)
-            dqs[pl.ds(r_, R), p * 128 : (p + 1) * 128] = acc.astype(bf16)
-        return 0
-
-    lax.fori_loop(0, T // R, spread, 0)
+    routes = route_rows(rt_ref)
+    for j in range(J):
+        rows[j] = sub8(dq_ref[:, j * T : (j + 1) * T].astype(f32) * 0.125)
+    to_experts(routes, rows, dqs)
     nm = normed_ref[...]
     for c in range(4):
-        store_expert(big, [0, 1, 2], 2 * c, tn(dqs[:, c * 384 : (c + 1) * 384], nm))
+        store_expert(big, [0, 1, 2], 2 * c, nn(dqs[c * 384 : (c + 1) * 384, :], nm))
     for s in sums:
         s.start(0)
     for s in spreads:
@@ -668,16 +659,16 @@
     plane_o.start("x")
     gkv = gkv_ref[...].astype(bf16)
     dkvw = tn(nm, gkv).astype(bf16)
-    gn = gn_ref[...] + nn(dqs[...], wq_ref[...]) + nt(gkv, kvw_ref[...])
+    gn = gn_ref[...] + tn(dqs[...], wq_ref[...]) + nt(gkv, kvw_ref[...])
     x = x_ref[...].astype(f32)
     inv = lax.rsqrt(jnp.mean(x * x, axis=-1, keepdims=True) + eps)
     n = x * inv
     dgain = jnp.sum(gn * n, axis=0, keepdims=True)
     drw = drw_ref[...]
     dfg = dfg_ref[...]
-    rows = [dkvw.astype(f32)] + [drw[:, t * 128 : (t + 1) * 128] for t in range(4)]
-    rows += [v[:, t * 128 : (t + 1) * 128] for v in (dgain, dfg) for t in range(4)] + [jnp.zeros((SMALL - 616, 128), f32)]
-    ssrc[...] = jnp.concatenate(rows, axis=0).astype(bf16).reshape(2, 4, SMALL // 8, 128)
+    parts = [dkvw.astype(f32)] + [drw[:, t * 128 : (t + 1) * 128] for t in range(4)]
+    parts += [v[:, t * 128 : (t + 1) * 128] for v in (dgain, dfg) for t in range(4)] + [jnp.zeros((SMALL - 616, 128), f32)]
+    ssrc[...] = jnp.concatenate(parts, axis=0).astype(bf16).reshape(2, 4, SMALL // 8, 128)
     small.step(0)
     for s in sums:
         s.finish(0)
@@ -713,11 +704,32 @@
     copies.drain()
 
 
-SCRATCH_E = [VM((T, J), i32), VM((T, EW), bf16), VM((3, 2048, 128), bf16),
+SCRATCH_E = [VM((J, 8, 8, T), f32), VM((EW, T), bf16), VM((3, 2048, 128), bf16),
              VM((3, 4, 4, 4, 16, 128), bf16), VM((3, 4, 4, 4, 16, 128), bf16), VM((3, 3, 4, 4, 16, 128), bf16),
              VM((3, 3, 4, 16, 128), bf16), VM((3, 3, 16, 128), bf16),
              VM((2, 4, SMALL // 8, 128), bf16), VM((4, SMALL // 8, 128), bf16), VM((4, SMALL // 8, 128), bf16),
              VM((3, SMALL // 8, 128), bf16), VM((4, SMALL // 8, 128), bf16), VM((4, SMALL // 8, 128), bf16)] + dma_sems(86)
+
+
+def kernel_f(all_ref, wo_ref, dwq_ref, small_ref, out_in, ing_in, dup_ref, ddown_ref, dwo_ref, dwqt_ref, dkvw_ref, drw_ref, dgain_ref,
+             dfg_ref, out_ref, ing_ref):
+    slot = {u: i for i, u in enumerate(sorted(UP_UNIT + DOWN_UNIT))}
+    for t in range(4):
+        ts = slice(t * 128, (t + 1) * 128)
+        ddown_ref[:, ts] = all_ref[slot[DOWN_UNIT[t]]].astype(f32)
+        for s in range(4):
+            dup_ref[:, (4 * t + s) * 128 : (4 * t + s + 1) * 128] = all_ref[slot[UP_UNIT[t]], s * 512 : (s + 1) * 512, :].astype(f32)
+        dwo_ref[:, ts] = wo_ref[t * 192 : (t + 1) * 192, :].astype(f32)
+        dwqt_ref[:, ts] = dwq_ref[t * 192 : (t + 1) * 192, :].astype(f32)
+    small = small_ref[512:SMALL, :].astype(f32)
+    dkvw_ref[...] = small_ref[0:512, :].astype(f32)
+    for t in range(4):
+        ts = slice(t * 128, (t + 1) * 128)
+        drw_ref[:, ts] = small[t * E : (t + 1) * E]
+        dgain_ref[:, ts] = small[96 + t : 97 + t]
+        dfg_ref[:, ts] = small[100 + t : 101 + t]
+    out_ref[...] = out_in[...]
+    ing_ref[...] = ing_in[...]
 
 
 def call(body, outs, scratch, vmem=56 << 20, flops=0, **kw):
@@ -735,10 +747,6 @@
     return run
 
 
-def columns(blocks, rows):
-    return jnp.swapaxes(blocks, 0, 1).reshape(rows, -1).astype(f32)
-
-
 def per_device(inputs, cotangent, norm_gain, ffn_gain, kv_weight, router_weight, query_weight, output_weight, up_weight,
                down_weight, routes, segment_ids):
     wq = jnp.swapaxes(query_weight, 1, 2).reshape(3 * H, D)
@@ -747,37 +755,34 @@
     rt = routes.T
     gain = norm_gain.reshape(1, D)
     fgain = ffn_gain.reshape(1, D)
-    normed, gate, kv_all, wq_all, wo_all, att, qa = call(
+    normed, gate, kv_all, wq_all, wo_all, att, qt = call(
         kernel_ab,
-        [((T, D), bf16), ((T, E), f32), ((NB, KVR, 128), bf16), ((NB, 3 * H, D), bf16), ((NB, 3 * H, D), bf16),
-         ((J, T, 128), bf16), ((J, T, 128), bf16)],
+        [((T, D), bf16), ((J, T), f32), ((NB, KVR, 128), bf16), ((NB, 3 * H, D), bf16), ((NB, 3 * H, D), bf16),
+         ((H, ROWS), bf16), ((128, ROWS), bf16)],
         SCRATCH_AB, flops=1 << 33, collective_id=1, has_side_effects=True)(
         inputs, gain, kv_weight, rw, rt, segment_ids.reshape(3, 128), wq, wo)
     wq_all, wo_all = wq_all.reshape(EW, D), wo_all.reshape(EW, D)
-    out, da, gm, gn, big, drw, dfg = call(
+    out, dat, gm, gn, big, drw, dfg = call(
         kernel_c,
-        [((T, D), bf16), ((J, T, 128), bf16), ((T, D), f32), ((T, D), f32), ((UNITS, 2048, 128), bf16), ((E, D), f32), ((1, D), f32)],
+        [((T, D), bf16), ((128, ROWS), bf16), ((T, D), f32), ((T, D), f32), ((UNITS, 2048, 128), bf16), ((E, D), f32), ((1, D), f32)],
         SCRATCH_C, flops=1 << 33)(inputs, cotangent, gate, rt, att, wo_all, up_weight, down_weight, fgain, normed, rw)
     dq, gkv, red = call(
-        kernel_d, [((J, T, 128), bf16), ((T, 128), f32), ((UNITS, 16, 128), bf16)],
+        kernel_d, [((H, ROWS), bf16), ((T, 128), f32), ((UNITS, 16, 128), bf16)],
         SCRATCH_D, flops=1 << 35, collective_id=2, has_side_effects=True)(
-        kv_all, qa, da, big.reshape(UNITS, 2, 4, 4, 4, 16, 128))
+        kv_all, qt, dat, big.reshape(UNITS, 2, 4, 4, 4, 16, 128))
     ing, shared, dwo, dwq, small = call(
         kernel_e,
         [((T, D), bf16), ((8, 2, 4, 4, 4, 16, 128), bf16), ((3, 4, 4, 16, 128), bf16), ((3, 4, 4, 16, 128), bf16),
          ((2, 4, SMALL // 8, 128), bf16)],
         SCRATCH_E, flops=1 << 32, collective_id=3, has_side_effects=True)(
         dq, rt, wq_all, normed, gkv, kv_weight, gn, inputs, gain, gm, drw, dfg, red)
-    shared = shared.reshape(8, 2048, 128)
-    slot = {u: i for i, u in enumerate(sorted(UP_UNIT + DOWN_UNIT))}
-    dup = columns(jnp.stack([shared[slot[u]] for u in UP_UNIT]).reshape(16, 512, 128), D)
-    ddown = columns(jnp.stack([shared[slot[u]] for u in DOWN_UNIT]), FF)
-    dwo = columns(dwo.reshape(4, 3 * H, 128), 3 * H).reshape(3, H, D)
-    dwq = columns(dwq.reshape(4, 3 * H, 128), 3 * H).reshape(3, H, D)
-    small = small.reshape(SMALL, 128).astype(f32)
-    drw = columns(small[512:608].reshape(4, E, 128), E)
-    return (out, ing, small[608:612].reshape(D), small[612:616].reshape(D), small[:512], drw.T,
-            jnp.swapaxes(dwq, 1, 2), dwo, dup, ddown)
+    dup, ddown, dwo, dwqt, dkvw, drw, dgain, dfg, out, ing = call(
+        kernel_f,
+        [((D, FF), f32), ((FF, D), f32), ((3 * H, D), f32), ((3 * H, D), f32), ((D, 128), f32), ((E, D), f32), ((1, D), f32),
+         ((1, D), f32), ((T, D), bf16), ((T, D), bf16)], [])(
+        shared.reshape(8, 2048, 128), dwo.reshape(768, 128), dwq.reshape(768, 128), small.reshape(SMALL, 128), out, ing)
+    return (out, ing, dgain.reshape(D), dfg.reshape(D), dkvw, drw.T,
+            jnp.swapaxes(dwqt.reshape(3, H, D), 1, 2), dwo.reshape(3, H, D), dup, ddown)
 
 
 def solution(mesh):

time: 185 us -> 161 us (0.87)
  local copies, waits for them, and re-layouts: 14.1 us -> 0 us
  Pallas kernels: 165 us -> 160 us
  other arithmetic: 4.51 us -> 0 us
    unnamed x7 -> x0, local copies, waits for them, and re-layouts: 5.35 us -> none
    pallas_call x4 -> x5, Pallas kernels: 165 us -> 160 us  [run(): pl.pallas_call(body, out_shape=[jax.ShapeDtypeStruct(s, t) for s, t in ou...]
    slice x3 -> x0, local copies, waits for them, and re-layouts: 4.62 us -> none  [the longest x1 3.89 us: per_device(): ddown = columns(jnp.stack([shared[slot[u]] for u in DOWN_UNIT]), FF)]
    convert_element_type x3 -> x0, other arithmetic: 3.29 us -> none  [the longest x2 2.31 us: columns(): return jnp.swapaxes(blocks, 0, 1).reshape(rows, -1).astype(f32)]
    convert_element_type x3 -> x0, local copies, waits for them, and re-layouts: 2.38 us -> none  [columns(): return jnp.swapaxes(blocks, 0, 1).reshape(rows, -1).astype(f32)]
where the time goes in v3:
time: 161 us
  Pallas kernels  160 us (99%)
    pallas_call x5, Pallas kernels, run(): pl.pallas_call(body, out_shape=[jax.ShapeDtypeStruct(s, t) for s, t in ou...  160 us

profile of v3, /device:TPU:0, one launch (start us, length us, event | category | flops | bytes accessed | tf_op | source)
XLA Modules:
  0.0 160.5 jit_solution(9831818232296087798)
XLA Ops:
  0.6 36.0 %shard_map.195 = (bf16[384,512]{1,0:T(8,128)(2,1)}, f32[8,384]{1,0:T(8,128)}, bf16[8,400,128]{2,1,0:T(8,128)(2,1)}, bf16[8,192,512]{2,1,0:T(8,128)(2,1)}, bf16[8...) custom-call(bf16[384,512]{1,0:T(8,128)(2,1)} %x_ref.5, f32[1,512]{1,0:T(1,128)} %bitcast.39, ...), custom_call_target="tpu_custom_call" | custom-call | flops 8589934592 | bytes 4194304 | tf_op jit(solution)/shard_map/pallas_call | solution.py:738
  36.6 17.4 %shard_map.196 = (bf16[384,512]{1,0:T(8,128)(2,1)}, bf16[128,3072]{1,0:T(8,128)(2,1)}, f32[384,512]{1,0:T(8,128)}, f32[384,512]{1,0:T(8,128)}, bf16[11,2048,128]...) custom-call(bf16[384,512]{1,0:T(8,128)(2,1)} %x_ref.5, bf16[384,512]{1,0:T(8,128)(2,1)} %cot_ref.1, ...), custom_call_target="tpu_custom_call" | custom-call | flops 8589934592 | bytes 4194304 | tf_op jit(solution)/shard_map/pallas_call | solution.py:738
  54.1 58.4 %shard_map.197 = (bf16[64,3072]{1,0:T(8,128)(2,1)}, f32[384,128]{1,0:T(8,128)}, bf16[11,16,128]{2,1,0:T(8,128)(2,1)}) custom-call(bf16[8,400,128]{2,1,0:T(8,128)(2,1)} %get-tuple-element.42.kv_ref, bf16[128,3072]{1,0:T(8,128)(2,1)} %get-tuple-element.43.qt_ref, bf16[128,3072]{1,0:T(8,128)(2,1)} %get-tuple-element.48.dat_ref, ...), custom_call_target="tpu_custom_call" | custom-call | flops 34359738368 | bytes 4194304 | tf_op jit(solution)/shard_map/pallas_call | solution.py:738
  112.4 40.8 %shard_map.198 = (bf16[384,512]{1,0:T(8,128)(2,1)}, bf16[8,2,4,4,4,16,128]{6,5,4,3,2,1,0:T(8,128)(2,1)}, bf16[3,4,4,16,128]{4,3,2,1,0:T(8,128)(2,1)}, bf16[3,4,4...) custom-call(bf16[64,3072]{1,0:T(8,128)(2,1)} %get-tuple-element.50.dq_ref, s32[8,384]{1,0:T(8,128)} %bitcast.36, ...), custom_call_target="tpu_custom_call" | custom-call | flops 4294967296 | bytes 4194304 | tf_op jit(solution)/shard_map/pallas_call | solution.py:738
  153.3 7.1 %shard_map.199 = (f32[512,2048]{1,0:T(8,128)}, f32[2048,512]{1,0:T(8,128)}, f32[192,512]{1,0:T(8,128)}, f32[192,512]{1,0:T(8,128)}, f32[512,128]{1,0:T(8,128)}, ...) custom-call(bf16[8,2048,128]{2,1,0:T(8,128)(2,1)} %bitcast.23, ...), custom_call_target="tpu_custom_call" | custom-call | bytes 4194304 | tf_op jit(solution)/shard_map/pallas_call | solution.py:738

commit v4 on v3

v4 whole, which is shorter than its diff:
```python
import functools
import jax
import jax.numpy as jnp
from jax import lax
from jax.experimental import pallas as pl
from jax.experimental.pallas import tpu as pltpu
from jax.sharding import PartitionSpec as P

f32, bf16, i32 = jnp.float32, jnp.bfloat16, jnp.int32
T, D, H, J, E, FF, NB = 384, 512, 64, 8, 24, 2048, 8
EW = E * H
ROWS = J * T
SB = 2 * T
NSB = NB // 2
eps = 1e-06
NEG = -1e30
VM = pltpu.VMEM


def nn(a, b):
    return lax.dot_general(a, b, (((1,), (0,)), ((), ())), preferred_element_type=f32)


def nt(a, b):
    return lax.dot_general(a, b, (((1,), (1,)), ((), ())), preferred_element_type=f32)


def tn(a, b):
    return lax.dot_general(a, b, (((0,), (0,)), ((), ())), preferred_element_type=f32)


def lanes(rows):
    return lax.broadcasted_iota(i32, (rows, 128), 1)


def split3(v):
    a = v.astype(bf16).astype(f32)
    b = (v - a).astype(bf16).astype(f32)
    c = (v - a - b).astype(bf16).astype(f32)
    return a, b, c


MESH = pl.DeviceIdType.MESH
LINES = [(a, k) for a in "xyz" for k in (1, 2, 3)]
ALL_PEERS = [("c", 0)] + LINES


class Place:
    def __init__(self):
        dp, ex = lax.axis_index("dp"), lax.axis_index("expert")
        self.ex = ex
        self.at = {"x": dp // 4, "y": dp % 4, "z": ex // 2, "c": ex % 2}
        self.peers = {("c", 0): self.device(c=1 - self.at["c"])}
        for axis, k in LINES:
            self.peers[axis, k] = self.device(**{axis: (self.at[axis] + k) % 4})

    def device(self, **moved):
        at = {**self.at, **moved}
        return (at["x"] * 4 + at["y"], at["z"] * 2 + at["c"])

    def enter(self, peers):
        bar = pltpu.get_barrier_semaphore()
        for p in peers:
            pl.semaphore_signal(bar, inc=1, device_id=self.peers[p], device_id_type=MESH)
        pl.semaphore_wait(bar, len(peers))


class Copies:
    def __init__(self, place, send, recv):
        self.place, self.send, self.recv, self.made = place, send, recv, []

    def add(self, src, dst, peer):
        self.made.append((src, dst, peer))
        return len(self.made) - 1

    def get(self, i):
        src, dst, peer = self.made[i]
        return pltpu.make_async_remote_copy(src_ref=src(), dst_ref=dst(), send_sem=self.send.at[i], recv_sem=self.recv.at[i],
                                            device_id=self.place.peers[peer], device_id_type=MESH)

    def start(self, ids):
        for i in ids:
            self.get(i).start()

    def arrived(self, ids):
        for i in ids:
            self.get(i).wait_recv()

    def sent(self, ids):
        for i in ids:
            self.get(i).wait_send()

    def drain(self):
        self.sent(range(len(self.made)))


class Scatter:
    def __init__(self, copies, big, r, parts, order):
        self.cp, self.big, self.r = copies, big, r
        self.u0, self.u1 = parts[0][0], parts[-1][1]
        at = copies.place.at
        self.m = [at[a] for a in order]
        us = pl.ds(self.u0, self.u1 - self.u0)
        self.part_ids = [
            copies.add(lambda s=s: big.at[1, pl.ds(s[0], s[1] - s[0])], lambda s=s: r[0].at[pl.ds(s[0], s[1] - s[0])], ("c", 0))
            for s in parts]
        self.ids = [self.part_ids]
        for level in (1, 2, 3):
            def piece(k, level=level):
                pre = tuple(self.m[: level - 1])
                return big.at[(0, us) + pre + ((self.m[level - 1] + k) % 4,)]
            self.ids.append([
                copies.add(functools.partial(piece, k), lambda k=k, level=level: r[level].at[us, k - 1], (order[level - 1], k))
                for k in (1, 2, 3)])

    def start_part(self, i):
        self.cp.start([self.part_ids[i]])

    def start(self, level):
        self.cp.start(self.ids[level])

    def finish(self, level):
        self.cp.arrived(self.ids[level])
        for u in range(self.u0, self.u1):
            if level == 0:
                for a in range(4):
                    v = self.big[0, u, a].astype(f32) + self.r[0][u, a].astype(f32)
                    self.big[0, u, a] = v.astype(bf16)
                continue
            at = (0, u) + tuple(self.m[:level])
            v = self.big[at].astype(f32)
            for k in range(3):
                v = v + self.r[level][u, k].astype(f32)
            self.big[at] = v.astype(bf16)

    def result(self, u):
        return self.big[(0, u) + tuple(self.m)]


class Spread:
    def __init__(self, copies, out, u0, u1, order):
        self.cp, self.out = copies, out
        at = copies.place.at
        self.c, self.m = at["c"], [at[a] for a in order]
        us = pl.ds(u0, u1 - u0)
        self.ids = []
        for level in range(4):
            ref = lambda level=level: out.at[(us, self.c) + tuple(self.m[:level])]
            peers = [("c", 0)] if level == 0 else [(order[level - 1], k) for k in (1, 2, 3)]
            self.ids.append([copies.add(ref, ref, p) for p in peers])

    def put(self, u, value):
        self.out[(u, self.c) + tuple(self.m)] = value

    def start(self, level):
        self.cp.start(self.ids[level])

    def finish(self, level):
        self.cp.arrived(self.ids[level])


class SpreadPlane:
    def __init__(self, copies, out, u0, u1):
        self.cp, self.out = copies, out
        self.x, self.y = copies.place.at["x"], copies.place.at["y"]
        us = pl.ds(u0, u1 - u0)
        one = lambda: out.at[us, self.x, self.y]
        row = lambda: out.at[us, self.x]
        self.ids = {"y": [copies.add(one, one, ("y", k)) for k in (1, 2, 3)],
                    "x": [copies.add(row, row, ("x", k)) for k in (1, 2, 3)]}

    def put(self, u, value):
        self.out[u, self.x, self.y] = value

    def start(self, axis):
        self.cp.start(self.ids[axis])

    def finish(self, axis):
        self.cp.arrived(self.ids[axis])


class SmallSum:
    def __init__(self, copies, src, half, r0, r1, by, bz, out):
        self.cp, self.src, self.half, self.r0, self.r1, self.by, self.bz, self.out = copies, src, half, r0, r1, by, bz, out
        at = copies.place.at
        self.c, self.x, self.y, self.z = at["c"], at["x"], at["y"], at["z"]
        own_half = lambda: out.at[self.c]
        own = lambda: out.at[self.c, self.x]
        self.ids = [
            [copies.add(lambda: src.at[1 - self.c], lambda: r0, ("c", 0))],
            [copies.add(lambda k=k: half.at[(self.x + k) % 4], lambda k=k: r1.at[k - 1], ("x", k)) for k in (1, 2, 3)],
            [copies.add(lambda: by.at[self.y], lambda: by.at[self.y], ("y", k)) for k in (1, 2, 3)],
            [copies.add(lambda: bz.at[self.z], lambda: bz.at[self.z], ("z", k)) for k in (1, 2, 3)],
            [copies.add(own, own, ("x", k)) for k in (1, 2, 3)],
            [copies.add(own_half, own_half, ("c", 0))],
        ]

    def step(self, i):
        if i:
            self.cp.arrived(self.ids[i - 1])
        if i == 1:
            for a in range(4):
                self.half[a] = (self.src[self.c, a].astype(f32) + self.r0[a].astype(f32)).astype(bf16)
        if i == 2:
            v = self.half[self.x].astype(f32)
            for k in range(3):
                v = v + self.r1[k].astype(f32)
            self.by[self.y] = v.astype(bf16)
        if i in (3, 4):
            b = self.by if i == 3 else self.bz
            v = (b[0].astype(f32) + b[1].astype(f32) + b[2].astype(f32) + b[3].astype(f32)).astype(bf16)
            if i == 3:
                self.bz[self.z] = v
            else:
                self.out[self.c, self.x] = v
        if i < 6:
            self.cp.start(self.ids[i])


ORDERS = ["xyz", "yzx", "zxy"]
BATCHES = [[(0, 3), (3, 4)], [(4, 7), (7, 8)], [(8, 10), (10, 11)]]
ALL_BATCHES = [(0, 3), (3, 6), (6, 8)]
UP_UNIT, DOWN_UNIT, WO_UNIT = [0, 1, 2, 4], [5, 6, 8, 9], [3, 7, 10]
UNITS = 11
STEPS = [(u, i) for i, u in enumerate(sorted(UP_UNIT + DOWN_UNIT))]


def expert_row(ex, piece, order):
    at = {"x": piece // 4, "y": piece % 4, "z": ex // 2}
    r = ex % 2
    for a in order:
        r = r * 4 + at[a]
    return r * 16


def store_expert(big, core, units, ex0, value):
    low = value.astype(bf16)
    for o in range(2):
        slot = (core + (ex0 + o) % 2) % 2
        for row in range(0, 768, 16):
            v, piece = row // 256, (row % 256) // 16
            ct, r = row // 192, row % 192
            base = expert_row(ex0 + o, piece, ORDERS[v]) % 1024
            big[slot, units[v], base : base + 16, :] = low[o * 192 + r : o * 192 + r + 16, ct * 128 : (ct + 1) * 128]


KVR = T + 16


class Gather:
    def __init__(self, copies, out):
        self.cp, self.out = copies, out
        at, ex = copies.place.at, copies.place.ex
        own = lambda: out.at[ex]
        from_z = lambda k: out.at[((at["z"] - k + 4) % 4) * 2 + at["c"]]
        self.line = [copies.add(own, own, ("z", k)) for k in (1, 2, 3)]
        self.core = [copies.add(functools.partial(from_z, k), functools.partial(from_z, k), ("c", 0)) for k in (0, 1, 2, 3)]

    def start(self):
        self.cp.start(self.line)
        self.cp.start(self.core[:1])

    def forward(self):
        for k in range(3):
            self.cp.arrived(self.line[k : k + 1])
            self.cp.start(self.core[k + 1 : k + 2])

    def finish(self):
        self.cp.arrived(self.core)


def bounds_of(kv_ref):
    n0 = n1 = 0.0
    for b in range(NB):
        tail = kv_ref[b, T:KVR, :].astype(f32)
        n0 = n0 + 16.0 * tail[0:1] + tail[1:2]
        n1 = n1 + 16.0 * tail[2:3] + tail[3:4]
    return n0, n1


def segment_of(pos, bounds):
    return (pos >= bounds[0]).astype(i32) + (pos >= bounds[1]).astype(i32)


def sub8(v):
    return v.reshape(8, 8, v.shape[-1])


def route_rows(rt_ref):
    return [jnp.broadcast_to(rt_ref[j : j + 1, :], (8, T)) for j in range(J)]


def visible(me, sb):
    key = lax.broadcasted_iota(i32, (T, SB), 1)
    tok = lax.broadcasted_iota(i32, (T, SB), 0)
    ok = key - tok <= (me - 2 * sb) * T
    return ok


def prepare_keys(kv_ref, bounds, kaug, vaug, vt):
    ln = lanes(T)
    for b in range(NB):
        bs = slice(b * T, (b + 1) * T)
        kv = kv_ref[b, 0:T, :].astype(f32)
        pos = (lax.broadcasted_iota(i32, (T, 128), 0) + b * T).astype(f32)
        seg = segment_of(pos, bounds)
        feat = jnp.where((ln < H + 3) & (seg != ln - H), NEG, 0.0)
        feat = jnp.where((ln >= H + 3) & (ln < H + 6), 1.0, feat)
        kaug[bs, :] = jnp.where(ln < H, kv, feat).astype(bf16)
        if vaug is not None:
            one = jnp.where(ln < H + 3, 1.0, 0.0)
            vaug[bs, :] = jnp.where(ln < H, pltpu.roll(kv, H, 1), one).astype(bf16)
        if vt is not None:
            ones = jnp.where(lax.broadcasted_iota(i32, (16, T), 0) == 0, 1.0, 0.0)
            vt[:, bs] = jnp.concatenate([jnp.transpose(kv)[H:], ones], axis=0).astype(bf16)


def project_queries(normed, wq_ref, qall):
    for c in range(4):
        w = wq_ref[2 * c : 2 * c + 2].reshape(2 * 3 * H, D)
        qall[c * 48 : (c + 1) * 48] = (nt(w, normed) * 0.125).reshape(48, 8, T)


def choose(routes, table, j):
    acc = table[0:8]
    for e in range(1, E):
        acc = jnp.where((routes[j] == e)[None], table[e * 8 : (e + 1) * 8], acc)
    return acc


def to_experts(routes, rows, out):
    for e in range(E):
        acc = jnp.zeros((8, 8, T), f32)
        for j in range(J):
            acc = jnp.where((routes[j] == e)[None], rows[j], acc)
        out[e * H : (e + 1) * H, :] = acc.reshape(H, T).astype(bf16)


def pick_queries(rt_ref, bounds, me, qall, qt):
    routes = route_rows(rt_ref)
    pos = (lax.broadcasted_iota(i32, (H, T), 1) + me * T).astype(f32)
    seg = segment_of(pos, (bounds[0][:, 0:1], bounds[1][:, 0:1]))
    feat = jnp.where(lax.broadcasted_iota(i32, (H, T), 0) == seg, 1.0, 0.0).astype(bf16)
    for j in range(J):
        qt[0:H, j * T : (j + 1) * T] = choose(routes, qall, j).reshape(H, T).astype(bf16)
        qt[H:, j * T : (j + 1) * T] = feat


def attend(me, qt, kaug, vt, att, macc, acc):
    last = me // 2
    macc[...] = jnp.full(macc.shape, NEG, f32)
    acc[...] = jnp.zeros(acc.shape, f32)

    def block(sb, masked):
        ks = pl.ds(pl.multiple_of(sb * SB, SB), SB)
        for g in range(J // 2):
            gs = slice(g * SB, (g + 1) * SB)
            s = nn(kaug[ks, :], qt[:, gs])
            if masked:
                key = lax.broadcasted_iota(i32, (SB, T), 0)
                tok = lax.broadcasted_iota(i32, (SB, T), 1)
                ok = key - tok <= (me - 2 * sb) * T
                s = jnp.where(jnp.concatenate([ok, ok], axis=1), s, NEG)
            s = s.reshape(SB // 8, 8, SB)
            old = macc[:, gs]
            top = jnp.max(jnp.maximum(old, jnp.max(s, axis=0)), axis=0, keepdims=True)
            top = jnp.broadcast_to(top, (8, SB))
            p = jnp.exp(s - top[None]).reshape(SB, SB).astype(bf16)
            kept = acc[:, gs].reshape(10, 8, SB) * jnp.exp(old - top)[None]
            acc[:, gs] = kept.reshape(80, SB) + nn(vt[:, ks], p)
            macc[:, gs] = top

    lax.fori_loop(0, last, lambda sb, c: (block(sb, False), c)[1], 0)
    block(last, True)
    for g in range(J // 2):
        gs = slice(g * SB, (g + 1) * SB)
        tot = acc[H : H + 1, gs]
        att[:, gs] = (acc[0:H, gs] / tot).astype(bf16)
        l1, l2, l3 = split3(-(macc[0:1, gs] + jnp.log(tot)))
        row = lax.broadcasted_iota(i32, (16, SB), 0)
        feat = qt[H : H + 16, gs].astype(f32)
        feat = jnp.where(row == 3, l1, jnp.where(row == 4, l2, jnp.where(row == 5, l3, feat)))
        qt[H : H + 16, gs] = feat.astype(bf16)


def gates_of(normed, rw_ref, rt_ref, gate_ref):
    logits = nt(rw_ref[...], normed)
    eid = lax.broadcasted_iota(i32, (E, T), 0)
    per = [jnp.sum(jnp.where(rt_ref[j : j + 1, :] == eid, logits, 0.0), axis=0, keepdims=True) for j in range(J)]
    v = jnp.concatenate(per, axis=0)
    e = jnp.exp(v - jnp.max(v, axis=0, keepdims=True))
    gate_ref[...] = e / jnp.sum(e, axis=0, keepdims=True)


SMALL = 640


def dma_sems(n):
    return [pltpu.SemaphoreType.DMA((n,)), pltpu.SemaphoreType.DMA((n,))]


def kernel_all(x_ref, cot_ref, gain_ref, fgain_ref, kvw_ref, rw_ref, rt_ref, seg_ref, wq_in, wo_in, up_hbm, down_hbm,
               out_ref, ing_ref, all_ref, dwo_ref, dwq_ref, small_ref,
               up_ref, down_ref, wsem, normed_ref, gate_ref, kv_ref, wq_ref, wo_ref, att_ref, qt_ref, table, kaug, vaug, vt, macc, acc,
               rows, gat, gm_ref, gn_ref, drw_ref, dfg_ref, big, r0, r1, r2, r3,
               dat_ref, qa, da, dqacc, tot, gsend, grecv, lbig, l0, l1, l2, l3, ssrc, shalf, s0, s1, sy, sz, send, recv, ksend, krecv):
    place = Place()
    me, core = place.ex, place.at["c"]
    dp = lax.axis_index("dp")
    copies = Copies(place, send, recv)
    gq, gk, go = Gather(copies, wq_ref), Gather(copies, kv_ref), Gather(copies, wo_ref)
    big7 = big.reshape(2, UNITS, 4, 4, 4, 16, 128)
    lbig7 = lbig.reshape(2, 3, 4, 4, 4, 16, 128)
    early = [Scatter(copies, big7, (r0, r1, r2, r3), parts, o) for parts, o in zip(BATCHES, ORDERS)]
    late = [Scatter(copies, lbig7, (l0, l1, l2, l3), [(u, u + 1)], o) for u, o in enumerate(ORDERS)]
    spreads = [Spread(copies, all_ref, u0, u1, o) for (u0, u1), o in zip(ALL_BATCHES, ORDERS)]
    plane_o = SpreadPlane(copies, dwo_ref, 0, 3)
    plane_q = SpreadPlane(copies, dwq_ref, 0, 3)
    small = SmallSum(copies, ssrc, shalf, s0, s1, sy, sz, small_ref)

    bar = pltpu.get_barrier_semaphore()
    for p in ALL_PEERS:
        pl.semaphore_signal(bar, inc=1, device_id=place.peers[p], device_id_type=MESH)
    for k in range(1, NB):
        pl.semaphore_signal(bar, inc=1, device_id=(dp, (me + k) % NB), device_id_type=MESH)
    loads = [pltpu.make_async_copy(up_hbm, up_ref, wsem.at[0]), pltpu.make_async_copy(down_hbm, down_ref, wsem.at[1])]
    for cp in loads:
        cp.start()
    wq_ref[me] = wq_in[...]
    wo_ref[me] = wo_in[...]
    pl.semaphore_wait(bar, len(ALL_PEERS) + NB - 1)
    gq.start()

    x = x_ref[...].astype(f32)
    inv = lax.rsqrt(jnp.mean(x * x, axis=-1, keepdims=True) + eps)
    normed = (x * inv * gain_ref[...]).astype(bf16)
    normed_ref[...] = normed
    kv_ref[me, 0:T, :] = nn(normed, kvw_ref[...]).astype(bf16)
    seg = seg_ref[...]
    row = lax.broadcasted_iota(i32, (16, 128), 0)
    tail = jnp.zeros((16, 128), f32)
    for s in range(2):
        n = jnp.sum(jnp.sum((seg <= s).astype(f32), axis=0, keepdims=True), axis=1, keepdims=True)
        n = jnp.broadcast_to(n, (16, 128))
        hi = jnp.floor(n * 0.0625)
        tail = jnp.where(row == 2 * s, hi, jnp.where(row == 2 * s + 1, n - 16.0 * hi, tail))
    kv_ref[me, T:KVR, :] = tail.astype(bf16)
    gk.start()
    gates_of(normed, rw_ref, rt_ref, gate_ref)
    gq.forward()
    go.start()
    gk.forward()
    gq.finish()
    project_queries(normed, wq_ref, table)
    gk.finish()
    bounds = bounds_of(kv_ref)
    prepare_keys(kv_ref, bounds, kaug, vaug, vt)
    pick_queries(rt_ref, bounds, me, table, qt_ref)
    attend(me, qt_ref, kaug, vt, att_ref, macc, acc)

    go.forward()
    routes = route_rows(rt_ref)
    for j in range(J):
        rows[j] = sub8(att_ref[:, j * T : (j + 1) * T].astype(f32) * gate_ref[j : j + 1, :])
    to_experts(routes, rows, gat)
    go.finish()
    x = x_ref[...].astype(f32)
    wo_all = wo_ref[...].reshape(EW, D)
    mixed = x + tn(gat[...], wo_all)
    inv = lax.rsqrt(jnp.mean(mixed * mixed, axis=-1, keepdims=True) + eps)
    n = mixed * inv
    fgain = fgain_ref[...]
    second = (n * fgain).astype(bf16)
    second_t = jnp.transpose(n * fgain).astype(bf16)
    cot = cot_ref[...]
    for cp in loads:
        cp.wait()
    C = 512
    out = mixed
    gsec = jnp.zeros((T, D), f32)
    for c in range(FF // C):
        cs = slice(c * C, (c + 1) * C)
        v = nn(second, up_ref[:, cs])
        v2 = v * v
        th = jnp.tanh(0.7978845608028654 * (v + 0.044715 * v * v2))
        a = (0.5 * v * (1.0 + th)).astype(bf16)
        dth = 0.5 * (1.0 + th) + 0.5 * v * (1.0 - th * th) * (0.7978845608028654 * (1.0 + 0.134145 * v2))
        gh = (nt(cot, down_ref[cs, :]) * dth).astype(bf16)
        out = out + nn(a, down_ref[cs, :])
        gsec = gsec + nt(gh, up_ref[:, cs])
        gdown = tn(a, cot).astype(bf16)
        gup = nn(second_t, gh).astype(bf16)
        for t in range(4):
            ts = slice(t * 128, (t + 1) * 128)
            big[(core + c // 2) % 2, DOWN_UNIT[t], c % 2 * C : c % 2 * C + C, :] = gdown[:, ts]
            big[(core + t // 2) % 2, UP_UNIT[c], t % 2 * 512 : t % 2 * 512 + 512, :] = gup[:, ts]
    for s in early:
        s.start_part(0)
    out_ref[...] = out.astype(bf16)
    dfg_ref[...] = jnp.sum(gsec * n, axis=0, keepdims=True)
    hh = gsec * fgain
    gm = cot.astype(f32) + inv * (hh - n * jnp.mean(hh * n, axis=-1, keepdims=True))
    gm_ref[...] = gm
    gml = gm.astype(bf16)
    for c in range(4):
        store_expert(big, core, WO_UNIT, 2 * c, nn(gat[c * 384 : (c + 1) * 384, :], gml))
    for s in early:
        s.start_part(1)
    for c in range(4):
        w = wo_ref[2 * c : 2 * c + 2].reshape(2 * 3 * H, D)
        table[c * 48 : (c + 1) * 48] = nt(w, gml).reshape(48, 8, T)
    dots = []
    row = lax.broadcasted_iota(i32, (H, T), 0)
    for j in range(J):
        js = slice(j * T, (j + 1) * T)
        g = choose(routes, table, j).reshape(H, T)
        gate = gate_ref[j : j + 1, :]
        dot = jnp.sum(g * att_ref[:, js].astype(f32), axis=0, keepdims=True)
        dots.append(dot)
        d1, d2, d3 = split3(-(dot * gate))
        dat_ref[0:H, js] = (g * gate).astype(bf16)
        dat_ref[H:, js] = jnp.where(row == 0, d1, jnp.where(row == 1, d2, jnp.where(row == 2, d3, 0.0))).astype(bf16)
    dots = jnp.concatenate(dots, axis=0)
    gates = gate_ref[...]
    chosen = gates * (dots - jnp.sum(gates * dots, axis=0, keepdims=True))
    eid = lax.broadcasted_iota(i32, (E, T), 0)
    gl = jnp.zeros((E, T), f32)
    for j in range(J):
        gl = jnp.where(rt_ref[j : j + 1, :] == eid, chosen[j : j + 1, :], gl)
    hi = gl.astype(bf16)
    lo = (gl - hi.astype(f32)).astype(bf16)
    rw = rw_ref[...]
    gn_ref[...] = tn(hi, rw) + tn(lo, rw)
    nm = normed_ref[...]
    drw_ref[...] = nn(hi, nm) + nn(lo, nm)

    for j in range(J):
        js = slice(j * T, (j + 1) * T)
        qa[js, :] = jnp.transpose(qt_ref[:, js].astype(f32)).astype(bf16)
        da[js, :] = jnp.transpose(dat_ref[:, js].astype(f32)).astype(bf16)
    for s in early:
        s.finish(0)
        s.start(1)
    dqacc[...] = jnp.zeros(dqacc.shape, f32)
    last = me // 2

    def half_block(sb, half, masked):
        ks = pl.ds(pl.multiple_of(sb * SB, SB), SB)

        @pl.when(half == 0)
        def _():
            tot[...] = jnp.zeros(tot.shape, f32)

        for i in range(2):
            gs = pl.ds(pl.multiple_of((half * 2 + i) * SB, SB), SB)
            p = jnp.exp(nt(qa[gs, :], kaug[ks, :]))
            if masked:
                ok = visible(me, sb)
                p = jnp.where(jnp.concatenate([ok, ok], axis=0), p, 0.0)
            ds = (p * nt(da[gs, :], vaug[ks, :])).astype(bf16)
            kv = jnp.concatenate([kv_ref[2 * sb, 0:T, :], kv_ref[2 * sb + 1, 0:T, :]], axis=0)
            dqacc[gs, :] += nn(ds, kv)
            tot[0:H, :] += nn(qt_ref[0:H, gs], ds)
            tot[H:, :] += nn(dat_ref[0:H, gs], p.astype(bf16))

        @pl.when(half == 1)
        def _():
            low = jnp.transpose(tot[...]).astype(bf16)
            gsend[2 * sb] = low[0:T]
            gsend[2 * sb + 1] = low[T:]

    def to_owner(kb):
        return pltpu.make_async_remote_copy(src_ref=gsend.at[kb], dst_ref=grecv.at[me], send_sem=ksend.at[kb],
                                            recv_sem=krecv.at[me], device_id=(dp, kb), device_id_type=MESH)

    def from_device(b):
        return pltpu.make_async_remote_copy(src_ref=gsend.at[b], dst_ref=grecv.at[b], send_sem=ksend.at[b],
                                            recv_sem=krecv.at[b], device_id=(dp, b), device_id_type=MESH)

    def level(i):
        for s in early:
            s.finish(i)
            if i < 3:
                s.start(i + 1)

    def share_start():
        for (u0, u1), s in zip(ALL_BATCHES, spreads):
            for u in range(u0, u1):
                real = sorted(UP_UNIT + DOWN_UNIT)[u]
                s.put(u, early[u // 3].result(real))
            s.start(3)
        for v in range(3):
            plane_o.put(v, early[v].result(WO_UNIT[v]))
        plane_o.start("y")

    def step(i, carry):
        sb, half = i // 2, i % 2

        @pl.when(sb < last)
        def _():
            half_block(sb, half, False)

            @pl.when(half == 1)
            def _():
                to_owner(2 * sb).start()
                to_owner(2 * sb + 1).start()

        for at, lv in ((3, 1), (4, 2), (5, 3)):
            @pl.when(i == at)
            def _(lv=lv):
                level(lv)
                if lv == 3:
                    share_start()

        return carry

    lax.fori_loop(0, 2 * (NSB - 1), step, 0)

    def last_step(half, carry):
        half_block(last, half, True)

        @pl.when(half == 0)
        def _():
            for s in spreads:
                s.finish(3)
                s.start(2)
            plane_o.finish("y")
            plane_o.start("x")

        return carry

    lax.fori_loop(0, 2, last_step, 0)

    @pl.when(2 * last < me)
    def _():
        to_owner(2 * last).start()

    for s in spreads:
        s.finish(2)
        s.start(1)
    plane_o.finish("x")
    for j in range(J):
        js = slice(j * T, (j + 1) * T)
        rows[j] = sub8(jnp.transpose(dqacc[js, :])[0:H].astype(bf16).astype(f32) * 0.125)
    to_experts(routes, rows, gat)
    for c in range(4):
        store_expert(lbig, core, [0, 1, 2], 2 * c, nn(gat[c * 384 : (c + 1) * 384, :], nm))
    for s in late:
        s.start(0)
    gkv = gsend[me].astype(f32)
    acc_kv = tot
    acc_kv[:, 0:T] = jnp.transpose(gkv)
    for b in range(1, NB):
        @pl.when(b > me)
        def _(b=b):
            from_device(b).wait_recv()
            acc_kv[:, 0:T] += jnp.transpose(grecv[b].astype(f32))
    gkv = jnp.transpose(acc_kv[:, 0:T]).astype(bf16)
    dkvw = tn(nm, gkv).astype(bf16)
    gn = gn_ref[...] + tn(gat[...], wq_ref[...].reshape(EW, D)) + nt(gkv, kvw_ref[...])
    x = x_ref[...].astype(f32)
    inv = lax.rsqrt(jnp.mean(x * x, axis=-1, keepdims=True) + eps)
    n = x * inv
    dgain = jnp.sum(gn * n, axis=0, keepdims=True)
    drw = drw_ref[...]
    dfg = dfg_ref[...]
    parts = [dkvw.astype(f32)] + [drw[:, t * 128 : (t + 1) * 128] for t in range(4)]
    parts += [v[:, t * 128 : (t + 1) * 128] for v in (dgain, dfg) for t in range(4)] + [jnp.zeros((SMALL - 616, 128), f32)]
    ssrc[...] = jnp.concatenate(parts, axis=0).astype(bf16).reshape(2, 4, SMALL // 8, 128)
    small.step(0)
    for s in late:
        s.finish(0)
        s.start(1)
    small.step(1)
    hh = gn * gain_ref[...]
    ing_ref[...] = (gm_ref[...] + inv * (hh - n * jnp.mean(hh * n, axis=-1, keepdims=True))).astype(bf16)
    small.step(2)
    for lv in (1, 2):
        for s in late:
            s.finish(lv)
            s.start(lv + 1)
        small.step(lv + 2)
    for s in late:
        s.finish(3)
    for v in range(3):
        plane_q.put(v, late[v].result(v))
    plane_q.start("y")
    for s in spreads:
        s.finish(1)
        s.start(0)
    small.step(5)
    plane_q.finish("y")
    plane_q.start("x")
    small.step(6)
    plane_q.finish("x")
    for s in spreads:
        s.finish(0)
    for b in range(NB - 1):
        @pl.when(b < me)
        def _(b=b):
            to_owner(b).wait_send()
    copies.drain()


SCRATCH = [
    VM((D, FF), bf16), VM((FF, D), bf16), pltpu.SemaphoreType.DMA((2,)), VM((T, D), bf16), VM((J, T), f32), VM((NB, KVR, 128), bf16),
    VM((NB, 3 * H, D), bf16), VM((NB, 3 * H, D), bf16), VM((H, ROWS), bf16), VM((128, ROWS), bf16), VM((EW // 8, 8, T), f32),
    VM((ROWS, 128), bf16), VM((ROWS, 128), bf16), VM((80, ROWS), bf16), VM((8, ROWS), f32), VM((80, ROWS), f32),
    VM((J, 8, 8, T), f32), VM((EW, T), bf16), VM((T, D), f32), VM((T, D), f32), VM((E, D), f32), VM((1, D), f32),
    VM((2, UNITS, 1024, 128), bf16), VM((UNITS, 4, 4, 4, 16, 128), bf16), VM((UNITS, 3, 4, 4, 16, 128), bf16),
    VM((UNITS, 3, 4, 16, 128), bf16), VM((UNITS, 3, 16, 128), bf16),
    VM((128, ROWS), bf16), VM((ROWS, 128), bf16), VM((ROWS, 128), bf16), VM((ROWS, 128), f32), VM((128, SB), f32),
    VM((NB, T, 128), bf16), VM((NB, T, 128), bf16),
    VM((2, 3, 1024, 128), bf16), VM((3, 4, 4, 4, 16, 128), bf16), VM((3, 3, 4, 4, 16, 128), bf16), VM((3, 3, 4, 16, 128), bf16),
    VM((3, 3, 16, 128), bf16),
    VM((2, 4, SMALL // 8, 128), bf16), VM((4, SMALL // 8, 128), bf16), VM((4, SMALL // 8, 128), bf16),
    VM((3, SMALL // 8, 128), bf16), VM((4, SMALL // 8, 128), bf16), VM((4, SMALL // 8, 128), bf16),
] + dma_sems(143) + dma_sems(NB)


def kernel_f(up_in, down_in, wo_ref, dwq_ref, small_ref, out_in, ing_in, dup_ref, ddown_ref, dwo_ref, dwqt_ref, dkvw_ref, drw_ref,
             dgain_ref, dfg_ref, out_ref, ing_ref):
    ddown_ref[...] = down_in[0].astype(f32)
    for s in range(4):
        dup_ref[:, s * 128 : (s + 1) * 128] = up_in[0, s * 512 : (s + 1) * 512, :].astype(f32)

    @pl.when(pl.program_id(0) == 0)
    def _():
        for t in range(4):
            ts = slice(t * 128, (t + 1) * 128)
            dwo_ref[:, ts] = wo_ref[t * 192 : (t + 1) * 192, :].astype(f32)
            dwqt_ref[:, ts] = dwq_ref[t * 192 : (t + 1) * 192, :].astype(f32)
        small = small_ref[512:SMALL, :].astype(f32)
        dkvw_ref[...] = small_ref[0:512, :].astype(f32)
        for t in range(4):
            ts = slice(t * 128, (t + 1) * 128)
            drw_ref[:, ts] = small[t * E : (t + 1) * E]
            dgain_ref[:, ts] = small[96 + t : 97 + t]
            dfg_ref[:, ts] = small[100 + t : 101 + t]
        out_ref[...] = out_in[...]
        ing_ref[...] = ing_in[...]


def per_device(inputs, cotangent, norm_gain, ffn_gain, kv_weight, router_weight, query_weight, output_weight, up_weight,
               down_weight, routes, segment_ids):
    wq = jnp.swapaxes(query_weight, 1, 2).reshape(3 * H, D)
    wo = output_weight.reshape(3 * H, D)
    vmem, anywhere = pl.BlockSpec(memory_space=VM), pl.BlockSpec(memory_space=pl.ANY)
    S = jax.ShapeDtypeStruct
    out, ing, shared, dwo, dwq, small = pl.pallas_call(
        kernel_all,
        out_shape=[S((T, D), bf16), S((T, D), bf16), S((8, 2, 4, 4, 4, 16, 128), bf16), S((3, 4, 4, 16, 128), bf16),
                   S((3, 4, 4, 16, 128), bf16), S((2, 4, SMALL // 8, 128), bf16)],
        in_specs=[vmem] * 10 + [anywhere] * 2,
        out_specs=[vmem] * 6,
        scratch_shapes=SCRATCH,
        compiler_params=pltpu.CompilerParams(vmem_limit_bytes=62 << 20, collective_id=1, has_side_effects=True),
        cost_estimate=pl.CostEstimate(flops=1 << 35, bytes_accessed=1 << 24, transcendentals=0),
    )(inputs, cotangent, norm_gain.reshape(1, D), ffn_gain.reshape(1, D), kv_weight, router_weight.T, routes.T,
      segment_ids.reshape(3, 128), wq, wo, up_weight, down_weight)
    shared = shared.reshape(8, 2048, 128)

    def whole(*shape):
        return pl.BlockSpec(shape, lambda i: (0,) * len(shape))

    dup, ddown, dwo, dwqt, dkvw, drw, dgain, dfg, out, ing = pl.pallas_call(
        kernel_f,
        grid=(4,),
        out_shape=[S((D, FF), f32), S((FF, D), f32), S((3 * H, D), f32), S((3 * H, D), f32), S((D, 128), f32), S((E, D), f32),
                   S((1, D), f32), S((1, D), f32), S((T, D), bf16), S((T, D), bf16)],
        in_specs=[pl.BlockSpec((1, 2048, 128), lambda i: (i, 0, 0)), pl.BlockSpec((1, 2048, 128), lambda i: (4 + i, 0, 0)),
                  whole(768, 128), whole(768, 128), whole(SMALL, 128), whole(T, D), whole(T, D)],
        out_specs=[pl.BlockSpec((D, 512), lambda i: (0, i)), pl.BlockSpec((FF, 128), lambda i: (0, i)), whole(3 * H, D),
                   whole(3 * H, D), whole(D, 128), whole(E, D), whole(1, D), whole(1, D), whole(T, D), whole(T, D)],
        compiler_params=pltpu.CompilerParams(vmem_limit_bytes=40 << 20),
    )(shared, shared, dwo.reshape(768, 128), dwq.reshape(768, 128), small.reshape(SMALL, 128), out, ing)
    return (out, ing, dgain.reshape(D), dfg.reshape(D), dkvw, drw.T,
            jnp.swapaxes(dwqt.reshape(3, H, D), 1, 2), dwo.reshape(3, H, D), dup, ddown)


def solution(mesh):
    both = P(("dp", "expert"), None)
    ex = P("expert", None, None)
    return jax.shard_map(
        per_device, mesh=mesh,
        in_specs=(both, both, P(), P(), P(), P(), ex, ex, P(), P(), both, P(("dp", "expert"))),
        out_specs=(both, both, P(), P(), P(), P(), ex, ex, P(), P()),
        check_vma=False)
```

time: 161 us -> 139 us (0.86)
  Pallas kernels: 160 us -> 131 us
  local copies, waits for them, and re-layouts: 0 us -> 6.94 us
    pallas_call x5 -> x2, Pallas kernels: 160 us -> 131 us  [the longest x1 127 us: per_device(): pl.pallas_call(kernel_all, out_shape=[S((T, D), bf16), S((T, D), bf16), S...]
    unnamed x0 -> x12, local copies, waits for them, and re-layouts: none -> 6.94 us
where the time goes in v4:
time: 139 us
  Pallas kernels  131 us (94%)
  local copies, waits for them, and re-layouts  6.94 us (5%)
    pallas_call x1, Pallas kernels, per_device(): pl.pallas_call(kernel_all, out_shape=[S((T, D), bf16), S((T, D), bf16), S...  127 us
    unnamed x12, local copies, waits for them, and re-layouts  6.94 us
    pallas_call x1, Pallas kernels, per_device(): pl.pallas_call(kernel_f, grid=(4,), out_shape=[S((D, FF), f32), S((FF, D)...  4.42 us

profile of v4, /device:TPU:0, one launch (start us, length us, event | category | flops | bytes accessed | tf_op | source)
XLA Modules:
  0.0 138.9 jit_solution(3918839102076062310)
XLA Ops:
  0.6 126.7 %shard_map.195 = (bf16[384,512]{1,0:T(8,128)(2,1)}, bf16[384,512]{1,0:T(8,128)(2,1)}, bf16[8,2,4,4,4,16,128]{6,5,4,3,2,1,0:T(8,128)(2,1)}, bf16[3,4,4,16,128]{4,...) custom-call(bf16[384,512]{1,0:T(8,128)(2,1)} %x_ref.1, ...), custom_call_target="tpu_custom_call" | custom-call | flops 34359738368 | bytes 16777216 | tf_op jit(solution)/shard_map/pallas_call | solution.py:750
  127.3 0.0 copy-start
  127.4 2.2 %copy-done = bf16[8,2,4,4,4,16,128]{6,5,4,3,2,1,0:T(8,128)(2,1)S(1)} copy-done((bf16[8,2,4,4,4,16,128]{6,5,4,3,2,1,0:T(8,128)(2,1)S(1)}, bf16[8,2,4,4,4,16,128]{6,5,4,3,2,1,0:T(8,128)(2,1)}, u32[]{:S(2)}) %copy-start) | copy-done | bytes 4194328
  129.5 0.0 copy-start.1
  129.5 1.0 copy-done.1
  130.5 0.0 copy-start.2
  130.5 1.0 copy-done.2
  131.5 0.0 copy-start.3
  131.5 0.9 copy-done.3
  132.5 0.0 copy-start.4
  132.5 0.9 copy-done.4
  133.4 0.0 copy-start.5
  133.4 0.9 copy-done.5
  134.3 4.4 %shard_map.196 = (f32[512,2048]{1,0:T(8,128)}, f32[2048,512]{1,0:T(8,128)}, f32[192,512]{1,0:T(8,128)}, f32[192,512]{1,0:T(8,128)}, f32[512,128]{1,0:T(8,128)}, ...) custom-call(bf16[8,2048,128]{2,1,0:T(8,128)(2,1)S(1)} %bitcast.20, ...), custom_call_target="tpu_custom_call" | custom-call | tf_op jit(solution)/shard_map/pallas_call | solution.py:766
Async XLA Ops:
  127.3 2.2 %copy-start = (bf16[8,2,4,4,4,16,128]{6,5,4,3,2,1,0:T(8,128)(2,1)S(1)}, bf16[8,2,4,4,4,16,128]{6,5,4,3,2,1,0:T(8,128)(2,1)}, u32[]{:S(2)}) copy-start(bf16[8,2,4,4,4,16,128]{6,5,4,3,2,1,0:T(8,128)(2,1)} %get-tuple-element.26) | copy-start | bytes 12582916
  129.5 1.0 copy-start.1
  130.5 1.0 copy-start.2
  131.5 0.9 copy-start.3
  132.5 0.9 copy-start.4
  133.4 0.9 copy-start.5

commit v5 on v4

--- a/solution.py
+++ b/solution.py
@@ -146,14 +146,23 @@
         self.ids = []
         for level in range(4):
             ref = lambda level=level: out.at[(us, self.c) + tuple(self.m[:level])]
-            peers = [("c", 0)] if level == 0 else [(order[level - 1], k) for k in (1, 2, 3)]
-            self.ids.append([copies.add(ref, ref, p) for p in peers])
+            piece = lambda k=0: out.at[us, self.c, (self.m[0] - k + 4) % 4]
+            if level == 0:
+                self.ids.append([copies.add(lambda k=k: piece(k), lambda k=k: piece(k), ("c", 0)) for k in range(4)])
+            else:
+                self.ids.append([copies.add(ref, ref, (order[level - 1], k)) for k in (1, 2, 3)])
 
     def put(self, u, value):
         self.out[(u, self.c) + tuple(self.m)] = value
 
     def start(self, level):
         self.cp.start(self.ids[level])
+        if level == 1:
+            self.cp.start(self.ids[0][:1])
+
+    def forward(self, k):
+        self.cp.arrived(self.ids[1][k - 1 : k])
+        self.cp.start(self.ids[0][k : k + 1])
 
     def finish(self, level):
         self.cp.arrived(self.ids[level])
@@ -218,7 +227,8 @@
 
 
 ORDERS = ["xyz", "yzx", "zxy"]
-BATCHES = [[(0, 3), (3, 4)], [(4, 7), (7, 8)], [(8, 10), (10, 11)]]
+BATCHES = [[(0, 1), (1, 2), (2, 3), (3, 4)], [(4, 5), (5, 7), (7, 8)], [(8, 10), (10, 11)]]
+UP_PART, DOWN_PARTS, WO_PARTS = [(0, 0), (0, 1), (0, 2), (1, 0)], [(1, 1), (2, 0)], [(0, 3), (1, 2), (2, 1)]
 ALL_BATCHES = [(0, 3), (3, 6), (6, 8)]
 UP_UNIT, DOWN_UNIT, WO_UNIT = [0, 1, 2, 4], [5, 6, 8, 9], [3, 7, 10]
 UNITS = 11
@@ -336,13 +346,17 @@
         out[e * H : (e + 1) * H, :] = acc.reshape(H, T).astype(bf16)
 
 
-def pick_queries(rt_ref, bounds, me, qall, qt):
+def pick_queries(rt_ref, table, qt):
     routes = route_rows(rt_ref)
+    for j in range(J):
+        qt[0:H, j * T : (j + 1) * T] = choose(routes, table, j).reshape(H, T).astype(bf16)
+
+
+def mark_queries(bounds, me, qt):
     pos = (lax.broadcasted_iota(i32, (H, T), 1) + me * T).astype(f32)
     seg = segment_of(pos, (bounds[0][:, 0:1], bounds[1][:, 0:1]))
     feat = jnp.where(lax.broadcasted_iota(i32, (H, T), 0) == seg, 1.0, 0.0).astype(bf16)
     for j in range(J):
-        qt[0:H, j * T : (j + 1) * T] = choose(routes, qall, j).reshape(H, T).astype(bf16)
         qt[H:, j * T : (j + 1) * T] = feat
 
 
@@ -351,24 +365,38 @@
     macc[...] = jnp.full(macc.shape, NEG, f32)
     acc[...] = jnp.zeros(acc.shape, f32)
 
+    def score(sb, g, masked):
+        s = nn(kaug[pl.ds(pl.multiple_of(sb * SB, SB), SB), :], qt[:, g * SB : (g + 1) * SB])
+        if masked:
+            key = lax.broadcasted_iota(i32, (SB, T), 0)
+            tok = lax.broadcasted_iota(i32, (SB, T), 1)
+            ok = key - tok <= (me - 2 * sb) * T
+            s = jnp.where(jnp.concatenate([ok, ok], axis=1), s, NEG)
+        return s.reshape(SB // 8, 8, SB)
+
+    def soften(s, g):
+        gs = slice(g * SB, (g + 1) * SB)
+        old = macc[:, gs]
+        top = jnp.max(jnp.maximum(old, jnp.max(s, axis=0)), axis=0, keepdims=True)
+        top = jnp.broadcast_to(top, (8, SB))
+        macc[:, gs] = top
+        return jnp.exp(s - top[None]).reshape(SB, SB).astype(bf16), jnp.exp(old - top)
+
+    def weigh(sb, g, p, kept):
+        gs = slice(g * SB, (g + 1) * SB)
+        old = acc[:, gs].reshape(10, 8, SB) * kept[None]
+        acc[:, gs] = old.reshape(80, SB) + nn(vt[:, pl.ds(pl.multiple_of(sb * SB, SB), SB)], p)
+
     def block(sb, masked):
-        ks = pl.ds(pl.multiple_of(sb * SB, SB), SB)
+        s = score(sb, 0, masked)
+        held = None
         for g in range(J // 2):
-            gs = slice(g * SB, (g + 1) * SB)
-            s = nn(kaug[ks, :], qt[:, gs])
-            if masked:
-                key = lax.broadcasted_iota(i32, (SB, T), 0)
-                tok = lax.broadcasted_iota(i32, (SB, T), 1)
-                ok = key - tok <= (me - 2 * sb) * T
-                s = jnp.where(jnp.concatenate([ok, ok], axis=1), s, NEG)
-            s = s.reshape(SB // 8, 8, SB)
-            old = macc[:, gs]
-            top = jnp.max(jnp.maximum(old, jnp.max(s, axis=0)), axis=0, keepdims=True)
-            top = jnp.broadcast_to(top, (8, SB))
-            p = jnp.exp(s - top[None]).reshape(SB, SB).astype(bf16)
-            kept = acc[:, gs].reshape(10, 8, SB) * jnp.exp(old - top)[None]
-            acc[:, gs] = kept.reshape(80, SB) + nn(vt[:, ks], p)
-            macc[:, gs] = top
+            ahead = score(sb, g + 1, masked) if g + 1 < J // 2 else None
+            new = soften(s, g)
+            if g:
+                weigh(sb, g - 1, *held)
+            held, s = new, ahead
+        weigh(sb, J // 2 - 1, *held)
 
     lax.fori_loop(0, last, lambda sb, c: (block(sb, False), c)[1], 0)
     block(last, True)
@@ -448,14 +476,15 @@
     gk.start()
     gates_of(normed, rw_ref, rt_ref, gate_ref)
     gq.forward()
-    go.start()
-    gk.forward()
     gq.finish()
     project_queries(normed, wq_ref, table)
+    pick_queries(rt_ref, table, qt_ref)
+    gk.forward()
     gk.finish()
     bounds = bounds_of(kv_ref)
     prepare_keys(kv_ref, bounds, kaug, vaug, vt)
-    pick_queries(rt_ref, bounds, me, table, qt_ref)
+    mark_queries(bounds, me, qt_ref)
+    go.start()
     attend(me, qt_ref, kaug, vt, att_ref, macc, acc)
 
     go.forward()
@@ -494,8 +523,9 @@
             ts = slice(t * 128, (t + 1) * 128)
             big[(core + c // 2) % 2, DOWN_UNIT[t], c % 2 * C : c % 2 * C + C, :] = gdown[:, ts]
             big[(core + t // 2) % 2, UP_UNIT[c], t % 2 * 512 : t % 2 * 512 + 512, :] = gup[:, ts]
-    for s in early:
-        s.start_part(0)
+        early[UP_PART[c][0]].start_part(UP_PART[c][1])
+    for b, i in DOWN_PARTS:
+        early[b].start_part(i)
     out_ref[...] = out.astype(bf16)
     dfg_ref[...] = jnp.sum(gsec * n, axis=0, keepdims=True)
     hh = gsec * fgain
@@ -504,8 +534,8 @@
     gml = gm.astype(bf16)
     for c in range(4):
         store_expert(big, core, WO_UNIT, 2 * c, nn(gat[c * 384 : (c + 1) * 384, :], gml))
-    for s in early:
-        s.start_part(1)
+    for b, i in WO_PARTS:
+        early[b].start_part(i)
     for c in range(4):
         w = wo_ref[2 * c : 2 * c + 2].reshape(2 * 3 * H, D)
         table[c * 48 : (c + 1) * 48] = nt(w, gml).reshape(48, 8, T)
@@ -538,9 +568,6 @@
         js = slice(j * T, (j + 1) * T)
         qa[js, :] = jnp.transpose(qt_ref[:, js].astype(f32)).astype(bf16)
         da[js, :] = jnp.transpose(dat_ref[:, js].astype(f32)).astype(bf16)
-    for s in early:
-        s.finish(0)
-        s.start(1)
     dqacc[...] = jnp.zeros(dqacc.shape, f32)
     last = me // 2
 
@@ -605,12 +632,10 @@
                 to_owner(2 * sb).start()
                 to_owner(2 * sb + 1).start()
 
-        for at, lv in ((3, 1), (4, 2), (5, 3)):
+        for at, lv in ((0, 0), (4, 1), (5, 2)):
             @pl.when(i == at)
             def _(lv=lv):
                 level(lv)
-                if lv == 3:
-                    share_start()
 
         return carry
 
@@ -621,11 +646,8 @@
 
         @pl.when(half == 0)
         def _():
-            for s in spreads:
-                s.finish(3)
-                s.start(2)
-            plane_o.finish("y")
-            plane_o.start("x")
+            level(3)
+            share_start()
 
         return carry
 
@@ -636,9 +658,10 @@
         to_owner(2 * last).start()
 
     for s in spreads:
-        s.finish(2)
-        s.start(1)
-    plane_o.finish("x")
+        s.finish(3)
+        s.start(2)
+    plane_o.finish("y")
+    plane_o.start("x")
     for j in range(J):
         js = slice(j * T, (j + 1) * T)
         rows[j] = sub8(jnp.transpose(dqacc[js, :])[0:H].astype(bf16).astype(f32) * 0.125)
@@ -647,9 +670,8 @@
         store_expert(lbig, core, [0, 1, 2], 2 * c, nn(gat[c * 384 : (c + 1) * 384, :], nm))
     for s in late:
         s.start(0)
-    gkv = gsend[me].astype(f32)
     acc_kv = tot
-    acc_kv[:, 0:T] = jnp.transpose(gkv)
+    acc_kv[:, 0:T] = jnp.transpose(gsend[me].astype(f32))
     for b in range(1, NB):
         @pl.when(b > me)
         def _(b=b):
@@ -657,6 +679,13 @@
             acc_kv[:, 0:T] += jnp.transpose(grecv[b].astype(f32))
     gkv = jnp.transpose(acc_kv[:, 0:T]).astype(bf16)
     dkvw = tn(nm, gkv).astype(bf16)
+    for s in late:
+        s.finish(0)
+        s.start(1)
+    for s in spreads:
+        s.finish(2)
+        s.start(1)
+    plane_o.finish("x")
     gn = gn_ref[...] + tn(gat[...], wq_ref[...].reshape(EW, D)) + nt(gkv, kvw_ref[...])
     x = x_ref[...].astype(f32)
     inv = lax.rsqrt(jnp.mean(x * x, axis=-1, keepdims=True) + eps)
@@ -669,30 +698,30 @@
     ssrc[...] = jnp.concatenate(parts, axis=0).astype(bf16).reshape(2, 4, SMALL // 8, 128)
     small.step(0)
     for s in late:
-        s.finish(0)
-        s.start(1)
+        s.finish(1)
+        s.start(2)
     small.step(1)
     hh = gn * gain_ref[...]
     ing_ref[...] = (gm_ref[...] + inv * (hh - n * jnp.mean(hh * n, axis=-1, keepdims=True))).astype(bf16)
+    for s in late:
+        s.finish(2)
+        s.start(3)
     small.step(2)
-    for lv in (1, 2):
-        for s in late:
-            s.finish(lv)
-            s.start(lv + 1)
-        small.step(lv + 2)
     for s in late:
         s.finish(3)
     for v in range(3):
         plane_q.put(v, late[v].result(v))
     plane_q.start("y")
-    for s in spreads:
-        s.finish(1)
-        s.start(0)
-    small.step(5)
+    small.step(3)
+    for k in (1, 2, 3):
+        for s in spreads:
+            s.forward(k)
     plane_q.finish("y")
     plane_q.start("x")
+    small.step(4)
+    small.step(5)
+    plane_q.finish("x")
     small.step(6)
-    plane_q.finish("x")
     for s in spreads:
         s.finish(0)
     for b in range(NB - 1):
@@ -715,7 +744,7 @@
     VM((3, 3, 16, 128), bf16),
     VM((2, 4, SMALL // 8, 128), bf16), VM((4, SMALL // 8, 128), bf16), VM((4, SMALL // 8, 128), bf16),
     VM((3, SMALL // 8, 128), bf16), VM((4, SMALL // 8, 128), bf16), VM((4, SMALL // 8, 128), bf16),
-] + dma_sems(143) + dma_sems(NB)
+] + dma_sems(152) + dma_sems(NB)
 
 
 def kernel_f(up_in, down_in, wo_ref, dwq_ref, small_ref, out_in, ing_in, dup_ref, ddown_ref, dwo_ref, dwqt_ref, dkvw_ref, drw_ref,
@@ -772,7 +801,7 @@
                   whole(768, 128), whole(768, 128), whole(SMALL, 128), whole(T, D), whole(T, D)],
         out_specs=[pl.BlockSpec((D, 512), lambda i: (0, i)), pl.BlockSpec((FF, 128), lambda i: (0, i)), whole(3 * H, D),
                    whole(3 * H, D), whole(D, 128), whole(E, D), whole(1, D), whole(1, D), whole(T, D), whole(T, D)],
-        compiler_params=pltpu.CompilerParams(vmem_limit_bytes=40 << 20),
+        compiler_params=pltpu.CompilerParams(vmem_limit_bytes=62 << 20),
     )(shared, shared, dwo.reshape(768, 128), dwq.reshape(768, 128), small.reshape(SMALL, 128), out, ing)
     return (out, ing, dgain.reshape(D), dfg.reshape(D), dkvw, drw.T,
             jnp.swapaxes(dwqt.reshape(3, H, D), 1, 2), dwo.reshape(3, H, D), dup, ddown)

time: 139 us -> 134 us (0.964); the launches traced: 139 us -> 132 us
  local copies, waits for them, and re-layouts: 6.94 us -> 0 us
    unnamed x12 -> x0, local copies, waits for them, and re-layouts: 6.94 us -> none
    pallas_call x1, Pallas kernels: 127 us -> 124 us  [per_device(): pl.pallas_call(kernel_all, out_shape=[S((T, D), bf16), S((T, D), bf16), S...]
    pallas_call x1, Pallas kernels: 4.42 us -> 7.24 us  [per_device(): pl.pallas_call(kernel_f, grid=(4,), out_shape=[S((D, FF), f32), S((FF, D)...]
where the time goes in v5:
time: 134 us; the launch traced here: 132 us
  Pallas kernels  131 us (98%)
    pallas_call x1, Pallas kernels, per_device(): pl.pallas_call(kernel_all, out_shape=[S((T, D), bf16), S((T, D), bf16), S...  124 us
    pallas_call x1, Pallas kernels, per_device(): pl.pallas_call(kernel_f, grid=(4,), out_shape=[S((D, FF), f32), S((FF, D)...  7.24 us

profile of v5, /device:TPU:0, one launch (start us, length us, event | category | flops | bytes accessed | tf_op | source)
XLA Modules:
  0.0 131.9 jit_solution(6694579732847962419)
XLA Ops:
  0.6 123.8 %shard_map.195 = (bf16[384,512]{1,0:T(8,128)(2,1)}, bf16[384,512]{1,0:T(8,128)(2,1)}, bf16[8,2,4,4,4,16,128]{6,5,4,3,2,1,0:T(8,128)(2,1)}, bf16[3,4,4,16,128]{4,...) custom-call(bf16[384,512]{1,0:T(8,128)(2,1)} %x_ref.1, ...), custom_call_target="tpu_custom_call" | custom-call | flops 34359738368 | bytes 16777216 | tf_op jit(solution)/shard_map/pallas_call | solution.py:779
  124.5 7.2 %shard_map.196 = (f32[512,2048]{1,0:T(8,128)}, f32[2048,512]{1,0:T(8,128)}, f32[192,512]{1,0:T(8,128)}, f32[192,512]{1,0:T(8,128)}, f32[512,128]{1,0:T(8,128)}, ...) custom-call(bf16[8,2048,128]{2,1,0:T(8,128)(2,1)} %bitcast.20, ...), custom_call_target="tpu_custom_call" | custom-call | tf_op jit(solution)/shard_map/pallas_call | solution.py:795

commit v6 on v5

--- a/solution.py
+++ b/solution.py
@@ -95,97 +95,103 @@
 
 
 class Scatter:
-    def __init__(self, copies, big, r, parts, order):
-        self.cp, self.big, self.r = copies, big, r
-        self.u0, self.u1 = parts[0][0], parts[-1][1]
+    def __init__(self, copies, big, r, ex, parts, groups, order):
+        self.cp, self.big, self.r, self.ex = copies, big, r, ex
+        self.parts, self.groups, self.u0, self.u1 = parts, groups, parts[0][0], parts[-1][1]
         at = copies.place.at
-        self.m = [at[a] for a in order]
-        us = pl.ds(self.u0, self.u1 - self.u0)
-        self.part_ids = [
-            copies.add(lambda s=s: big.at[1, pl.ds(s[0], s[1] - s[0])], lambda s=s: r[0].at[pl.ds(s[0], s[1] - s[0])], ("c", 0))
-            for s in parts]
-        self.ids = [self.part_ids]
-        for level in (1, 2, 3):
-            def piece(k, level=level):
-                pre = tuple(self.m[: level - 1])
-                return big.at[(0, us) + pre + ((self.m[level - 1] + k) % 4,)]
-            self.ids.append([
-                copies.add(functools.partial(piece, k), lambda k=k, level=level: r[level].at[us, k - 1], (order[level - 1], k))
-                for k in (1, 2, 3)])
-
-    def start_part(self, i):
+        self.m = m = [at[a] for a in order]
+        rng = lambda g: pl.ds(g[0], g[1] - g[0])
+        us = rng((self.u0, self.u1))
+        self.part_ids = [copies.add(lambda g=g: big.at[1, rng(g)], lambda g=g: r[0].at[rng(g)], ("c", 0)) for g in parts]
+        self.group_ids = [
+            [copies.add(lambda g=g, k=k: big.at[0, rng(g), (m[0] + k) % 4], lambda g=g, k=k: r[1].at[rng(g), k - 1], (order[0], k))
+             for k in (1, 2, 3)] for g in groups]
+        self.ids2 = [copies.add(lambda k=k: big.at[0, us, m[0], (m[1] + k) % 4], lambda k=k: r[2].at[us, k - 1], (order[1], k))
+                     for k in (1, 2, 3)]
+        own = lambda: ex.at[us, m[2]]
+        self.ids3 = [copies.add(own, own, (order[2], k)) for k in (1, 2, 3)]
+
+    def start0(self, i):
         self.cp.start([self.part_ids[i]])
 
-    def start(self, level):
-        self.cp.start(self.ids[level])
-
-    def finish(self, level):
-        self.cp.arrived(self.ids[level])
+    def pass0(self, h):
+        g = self.groups[h]
+        self.cp.arrived([i for i, p in zip(self.part_ids, self.parts) if g[0] <= p[0] < g[1]])
+        for u in range(*g):
+            for a in range(4):
+                v = self.big[0, u, a].astype(f32) + self.r[0][u, a].astype(f32)
+                self.big[0, u, a] = v.astype(bf16)
+        self.cp.start(self.group_ids[h])
+
+    def add3(self, u, at, r):
+        v = self.big[at].astype(f32)
+        for k in range(3):
+            v = v + r[u, k].astype(f32)
+        return v.astype(bf16)
+
+    def pass1(self):
+        for h, g in enumerate(self.groups):
+            self.cp.arrived(self.group_ids[h])
+            for u in range(*g):
+                at = (0, u, self.m[0])
+                self.big[at] = self.add3(u, at, self.r[1])
+        self.cp.start(self.ids2)
+
+    def pass2(self):
+        self.cp.arrived(self.ids2)
         for u in range(self.u0, self.u1):
-            if level == 0:
-                for a in range(4):
-                    v = self.big[0, u, a].astype(f32) + self.r[0][u, a].astype(f32)
-                    self.big[0, u, a] = v.astype(bf16)
-                continue
-            at = (0, u) + tuple(self.m[:level])
-            v = self.big[at].astype(f32)
-            for k in range(3):
-                v = v + self.r[level][u, k].astype(f32)
-            self.big[at] = v.astype(bf16)
+            self.ex[u, self.m[2]] = self.add3(u, (0, u, self.m[0], self.m[1]), self.r[2])
+        self.cp.start(self.ids3)
+
+    def pass3(self):
+        self.cp.arrived(self.ids3)
 
     def result(self, u):
-        return self.big[(0, u) + tuple(self.m)]
+        e = [self.ex[u, i].astype(f32) for i in range(4)]
+        return (e[0] + e[1] + e[2] + e[3]).astype(bf16)
 
 
 class Spread:
     def __init__(self, copies, out, u0, u1, order):
-        self.cp, self.out = copies, out
+        self.cp, self.out, self.u0, self.u1 = copies, out, u0, u1
         at = copies.place.at
         self.c, self.m = at["c"], [at[a] for a in order]
         us = pl.ds(u0, u1 - u0)
-        self.ids = []
-        for level in range(4):
-            ref = lambda level=level: out.at[(us, self.c) + tuple(self.m[:level])]
-            piece = lambda k=0: out.at[us, self.c, (self.m[0] - k + 4) % 4]
-            if level == 0:
-                self.ids.append([copies.add(lambda k=k: piece(k), lambda k=k: piece(k), ("c", 0)) for k in range(4)])
-            else:
-                self.ids.append([copies.add(ref, ref, (order[level - 1], k)) for k in (1, 2, 3)])
-
-    def put(self, u, value):
-        self.out[(u, self.c) + tuple(self.m)] = value
-
-    def start(self, level):
-        self.cp.start(self.ids[level])
-        if level == 1:
-            self.cp.start(self.ids[0][:1])
+        piece = lambda k=0: out.at[us, self.c, (self.m[0] - k + 4) % 4]
+        quarter = lambda: out.at[us, self.c, self.m[0], self.m[1]]
+        self.ids2 = [copies.add(quarter, quarter, (order[1], k)) for k in (1, 2, 3)]
+        self.ids1 = [copies.add(piece, piece, (order[0], k)) for k in (1, 2, 3)]
+        self.ids0 = [copies.add(lambda k=k: piece(k), lambda k=k: piece(k), ("c", 0)) for k in range(4)]
+
+    def begin(self, values):
+        for u, v in zip(range(self.u0, self.u1), values):
+            self.out[u, self.c, self.m[0], self.m[1]] = v
+        self.cp.start(self.ids2)
+
+    def pass2(self):
+        self.cp.arrived(self.ids2)
+        self.cp.start(self.ids1 + self.ids0[:1])
 
     def forward(self, k):
-        self.cp.arrived(self.ids[1][k - 1 : k])
-        self.cp.start(self.ids[0][k : k + 1])
-
-    def finish(self, level):
-        self.cp.arrived(self.ids[level])
-
-
-class SpreadPlane:
-    def __init__(self, copies, out, u0, u1):
-        self.cp, self.out = copies, out
-        self.x, self.y = copies.place.at["x"], copies.place.at["y"]
-        us = pl.ds(u0, u1 - u0)
-        one = lambda: out.at[us, self.x, self.y]
-        row = lambda: out.at[us, self.x]
-        self.ids = {"y": [copies.add(one, one, ("y", k)) for k in (1, 2, 3)],
-                    "x": [copies.add(row, row, ("x", k)) for k in (1, 2, 3)]}
-
-    def put(self, u, value):
-        self.out[u, self.x, self.y] = value
-
-    def start(self, axis):
-        self.cp.start(self.ids[axis])
-
-    def finish(self, axis):
-        self.cp.arrived(self.ids[axis])
+        self.cp.arrived(self.ids1[k - 1 : k])
+        self.cp.start(self.ids0[k : k + 1])
+
+    def finish(self):
+        self.cp.arrived(self.ids0)
+
+
+class SpreadOwner:
+    def __init__(self, copies, out, u, axis):
+        self.cp, self.out, self.u, self.p = copies, out, u, copies.place.at[axis]
+        ref = lambda: out.at[u, self.p]
+        self.ids = [copies.add(ref, ref, (axis, k)) for k in (1, 2, 3)]
+
+    def begin(self, value):
+        self.out[self.u, self.p] = value
+        self.cp.start(self.ids)
+
+    def finish(self):
+        self.cp.arrived(self.ids)
 
 
 class SmallSum:
@@ -226,17 +232,23 @@
             self.cp.start(self.ids[i])
 
 
-ORDERS = ["xyz", "yzx", "zxy"]
-BATCHES = [[(0, 1), (1, 2), (2, 3), (3, 4)], [(4, 5), (5, 7), (7, 8)], [(8, 10), (10, 11)]]
-UP_PART, DOWN_PARTS, WO_PARTS = [(0, 0), (0, 1), (0, 2), (1, 0)], [(1, 1), (2, 0)], [(0, 3), (1, 2), (2, 1)]
-ALL_BATCHES = [(0, 3), (3, 6), (6, 8)]
-UP_UNIT, DOWN_UNIT, WO_UNIT = [0, 1, 2, 4], [5, 6, 8, 9], [3, 7, 10]
 UNITS = 11
-STEPS = [(u, i) for i, u in enumerate(sorted(UP_UNIT + DOWN_UNIT))]
+UP_UNIT, DOWN_UNIT, WO_UNIT = [0, 4, 5, 8], [1, 2, 6, 9], [3, 7, 10]
+SHARED = sorted(UP_UNIT + DOWN_UNIT)
+OWNER_ORDERS = ["zxy", "xzy", "yzx"]
+EARLY = [([(0, 1), (1, 3), (3, 4)], [(0, 1), (1, 4)], "zxy"), ([(4, 5), (5, 6), (6, 7)], [(4, 6), (6, 7)], "xyz"),
+         ([(7, 8)], [(7, 8)], "xzy"), ([(8, 9), (9, 10), (10, 11)], [(8, 9), (9, 11)], "yzx")]
+UP_PART, DOWN_PARTS, WO_PARTS = [(0, 0), (1, 0), (1, 1), (3, 0)], [(0, 1), (1, 2), (3, 1)], [(0, 2), (2, 0), (3, 2)]
+SPREADS = [(0, 3, "zxy"), (3, 6, "xyz"), (6, 8, "yzx")]
+
+
+def plane_axes(order):
+    return [a for a in order if a != "z"]
 
 
 def expert_row(ex, piece, order):
-    at = {"x": piece // 4, "y": piece % 4, "z": ex // 2}
+    p, q = plane_axes(order)
+    at = {p: piece // 4, q: piece % 4, "z": ex // 2}
     r = ex % 2
     for a in order:
         r = r * 4 + at[a]
@@ -250,7 +262,7 @@
         for row in range(0, 768, 16):
             v, piece = row // 256, (row % 256) // 16
             ct, r = row // 192, row % 192
-            base = expert_row(ex0 + o, piece, ORDERS[v]) % 1024
+            base = expert_row(ex0 + o, piece, OWNER_ORDERS[v]) % 1024
             big[slot, units[v], base : base + 16, :] = low[o * 192 + r : o * 192 + r + 16, ct * 128 : (ct + 1) * 128]
 
 
@@ -430,8 +442,8 @@
 def kernel_all(x_ref, cot_ref, gain_ref, fgain_ref, kvw_ref, rw_ref, rt_ref, seg_ref, wq_in, wo_in, up_hbm, down_hbm,
                out_ref, ing_ref, all_ref, dwo_ref, dwq_ref, small_ref,
                up_ref, down_ref, wsem, normed_ref, gate_ref, kv_ref, wq_ref, wo_ref, att_ref, qt_ref, table, kaug, vaug, vt, macc, acc,
-               rows, gat, gm_ref, gn_ref, drw_ref, dfg_ref, big, r0, r1, r2, r3,
-               dat_ref, qa, da, dqacc, tot, gsend, grecv, lbig, l0, l1, l2, l3, ssrc, shalf, s0, s1, sy, sz, send, recv, ksend, krecv):
+               rows, gat, gm_ref, gn_ref, drw_ref, dfg_ref, big, r0, r1, r2, ex,
+               dat_ref, qa, da, dqacc, tot, gsend, grecv, lbig, l0, l1, l2, lex, ssrc, shalf, s0, s1, sy, sz, send, recv, ksend, krecv):
     place = Place()
     me, core = place.ex, place.at["c"]
     dp = lax.axis_index("dp")
@@ -439,11 +451,11 @@
     gq, gk, go = Gather(copies, wq_ref), Gather(copies, kv_ref), Gather(copies, wo_ref)
     big7 = big.reshape(2, UNITS, 4, 4, 4, 16, 128)
     lbig7 = lbig.reshape(2, 3, 4, 4, 4, 16, 128)
-    early = [Scatter(copies, big7, (r0, r1, r2, r3), parts, o) for parts, o in zip(BATCHES, ORDERS)]
-    late = [Scatter(copies, lbig7, (l0, l1, l2, l3), [(u, u + 1)], o) for u, o in enumerate(ORDERS)]
-    spreads = [Spread(copies, all_ref, u0, u1, o) for (u0, u1), o in zip(ALL_BATCHES, ORDERS)]
-    plane_o = SpreadPlane(copies, dwo_ref, 0, 3)
-    plane_q = SpreadPlane(copies, dwq_ref, 0, 3)
+    early = [Scatter(copies, big7, (r0, r1, r2), ex, parts, groups, o) for parts, groups, o in EARLY]
+    late = [Scatter(copies, lbig7, (l0, l1, l2), lex, [(u, u + 1)], [(u, u + 1)], o) for u, o in enumerate(OWNER_ORDERS)]
+    spreads = [Spread(copies, all_ref, u0, u1, o) for u0, u1, o in SPREADS]
+    owned_o = [SpreadOwner(copies, dwo_ref, u, plane_axes(o)[0]) for u, o in enumerate(OWNER_ORDERS)]
+    owned_q = [SpreadOwner(copies, dwq_ref, u, plane_axes(o)[0]) for u, o in enumerate(OWNER_ORDERS)]
     small = SmallSum(copies, ssrc, shalf, s0, s1, sy, sz, small_ref)
 
     bar = pltpu.get_barrier_semaphore()
@@ -523,9 +535,9 @@
             ts = slice(t * 128, (t + 1) * 128)
             big[(core + c // 2) % 2, DOWN_UNIT[t], c % 2 * C : c % 2 * C + C, :] = gdown[:, ts]
             big[(core + t // 2) % 2, UP_UNIT[c], t % 2 * 512 : t % 2 * 512 + 512, :] = gup[:, ts]
-        early[UP_PART[c][0]].start_part(UP_PART[c][1])
+        early[UP_PART[c][0]].start0(UP_PART[c][1])
     for b, i in DOWN_PARTS:
-        early[b].start_part(i)
+        early[b].start0(i)
     out_ref[...] = out.astype(bf16)
     dfg_ref[...] = jnp.sum(gsec * n, axis=0, keepdims=True)
     hh = gsec * fgain
@@ -535,10 +547,12 @@
     for c in range(4):
         store_expert(big, core, WO_UNIT, 2 * c, nn(gat[c * 384 : (c + 1) * 384, :], gml))
     for b, i in WO_PARTS:
-        early[b].start_part(i)
+        early[b].start0(i)
     for c in range(4):
         w = wo_ref[2 * c : 2 * c + 2].reshape(2 * 3 * H, D)
         table[c * 48 : (c + 1) * 48] = nt(w, gml).reshape(48, 8, T)
+    for i in (0, 1, 3):
+        early[i].pass0(0)
     dots = []
     row = lax.broadcasted_iota(i32, (H, T), 0)
     for j in range(J):
@@ -604,21 +618,17 @@
         return pltpu.make_async_remote_copy(src_ref=gsend.at[b], dst_ref=grecv.at[b], send_sem=ksend.at[b],
                                             recv_sem=krecv.at[b], device_id=(dp, b), device_id_type=MESH)
 
-    def level(i):
+    def at_0():
+        for i, h in ((0, 1), (1, 1), (2, 0), (3, 1)):
+            early[i].pass0(h)
+
+    def at_4():
         for s in early:
-            s.finish(i)
-            if i < 3:
-                s.start(i + 1)
-
-    def share_start():
-        for (u0, u1), s in zip(ALL_BATCHES, spreads):
-            for u in range(u0, u1):
-                real = sorted(UP_UNIT + DOWN_UNIT)[u]
-                s.put(u, early[u // 3].result(real))
-            s.start(3)
-        for v in range(3):
-            plane_o.put(v, early[v].result(WO_UNIT[v]))
-        plane_o.start("y")
+            s.pass1()
+
+    def at_6():
+        for s in early:
+            s.pass2()
 
     def step(i, carry):
         sb, half = i // 2, i % 2
@@ -632,10 +642,8 @@
                 to_owner(2 * sb).start()
                 to_owner(2 * sb + 1).start()
 
-        for at, lv in ((0, 0), (4, 1), (5, 2)):
-            @pl.when(i == at)
-            def _(lv=lv):
-                level(lv)
+        pl.when(i == 0)(at_0)
+        pl.when(i == 4)(at_4)
 
         return carry
 
@@ -644,11 +652,7 @@
     def last_step(half, carry):
         half_block(last, half, True)
 
-        @pl.when(half == 0)
-        def _():
-            level(3)
-            share_start()
-
+        pl.when(half == 0)(at_6)
         return carry
 
     lax.fori_loop(0, 2, last_step, 0)
@@ -657,11 +661,6 @@
     def _():
         to_owner(2 * last).start()
 
-    for s in spreads:
-        s.finish(3)
-        s.start(2)
-    plane_o.finish("y")
-    plane_o.start("x")
     for j in range(J):
         js = slice(j * T, (j + 1) * T)
         rows[j] = sub8(jnp.transpose(dqacc[js, :])[0:H].astype(bf16).astype(f32) * 0.125)
@@ -669,7 +668,13 @@
     for c in range(4):
         store_expert(lbig, core, [0, 1, 2], 2 * c, nn(gat[c * 384 : (c + 1) * 384, :], nm))
     for s in late:
-        s.start(0)
+        s.start0(0)
+    for s in early:
+        s.pass3()
+    for s, (u0, u1, _) in zip(spreads, SPREADS):
+        s.begin([early[{0: 0, 4: 1, 8: 3}[4 * (SHARED[u] // 4)]].result(SHARED[u]) for u in range(u0, u1)])
+    for s, e, u in zip(owned_o, (early[0], early[2], early[3]), WO_UNIT):
+        s.begin(e.result(u))
     acc_kv = tot
     acc_kv[:, 0:T] = jnp.transpose(gsend[me].astype(f32))
     for b in range(1, NB):
@@ -680,12 +685,9 @@
     gkv = jnp.transpose(acc_kv[:, 0:T]).astype(bf16)
     dkvw = tn(nm, gkv).astype(bf16)
     for s in late:
-        s.finish(0)
-        s.start(1)
+        s.pass0(0)
     for s in spreads:
-        s.finish(2)
-        s.start(1)
-    plane_o.finish("x")
+        s.pass2()
     gn = gn_ref[...] + tn(gat[...], wq_ref[...].reshape(EW, D)) + nt(gkv, kvw_ref[...])
     x = x_ref[...].astype(f32)
     inv = lax.rsqrt(jnp.mean(x * x, axis=-1, keepdims=True) + eps)
@@ -698,32 +700,27 @@
     ssrc[...] = jnp.concatenate(parts, axis=0).astype(bf16).reshape(2, 4, SMALL // 8, 128)
     small.step(0)
     for s in late:
-        s.finish(1)
-        s.start(2)
+        s.pass1()
     small.step(1)
     hh = gn * gain_ref[...]
     ing_ref[...] = (gm_ref[...] + inv * (hh - n * jnp.mean(hh * n, axis=-1, keepdims=True))).astype(bf16)
     for s in late:
-        s.finish(2)
-        s.start(3)
+        s.pass2()
     small.step(2)
-    for s in late:
-        s.finish(3)
-    for v in range(3):
-        plane_q.put(v, late[v].result(v))
-    plane_q.start("y")
+    for s, t, u in zip(owned_q, late, range(3)):
+        t.pass3()
+        s.begin(t.result(u))
     small.step(3)
     for k in (1, 2, 3):
         for s in spreads:
             s.forward(k)
-    plane_q.finish("y")
-    plane_q.start("x")
+    for s in owned_o + owned_q:
+        s.finish()
     small.step(4)
     small.step(5)
-    plane_q.finish("x")
     small.step(6)
     for s in spreads:
-        s.finish(0)
+        s.finish()
     for b in range(NB - 1):
         @pl.when(b < me)
         def _(b=b):
@@ -737,21 +734,22 @@
     VM((ROWS, 128), bf16), VM((ROWS, 128), bf16), VM((80, ROWS), bf16), VM((8, ROWS), f32), VM((80, ROWS), f32),
     VM((J, 8, 8, T), f32), VM((EW, T), bf16), VM((T, D), f32), VM((T, D), f32), VM((E, D), f32), VM((1, D), f32),
     VM((2, UNITS, 1024, 128), bf16), VM((UNITS, 4, 4, 4, 16, 128), bf16), VM((UNITS, 3, 4, 4, 16, 128), bf16),
-    VM((UNITS, 3, 4, 16, 128), bf16), VM((UNITS, 3, 16, 128), bf16),
+    VM((UNITS, 3, 4, 16, 128), bf16), VM((UNITS, 4, 4, 16, 128), bf16),
     VM((128, ROWS), bf16), VM((ROWS, 128), bf16), VM((ROWS, 128), bf16), VM((ROWS, 128), f32), VM((128, SB), f32),
     VM((NB, T, 128), bf16), VM((NB, T, 128), bf16),
     VM((2, 3, 1024, 128), bf16), VM((3, 4, 4, 4, 16, 128), bf16), VM((3, 3, 4, 4, 16, 128), bf16), VM((3, 3, 4, 16, 128), bf16),
-    VM((3, 3, 16, 128), bf16),
+    VM((3, 4, 4, 16, 128), bf16),
     VM((2, 4, SMALL // 8, 128), bf16), VM((4, SMALL // 8, 128), bf16), VM((4, SMALL // 8, 128), bf16),
     VM((3, SMALL // 8, 128), bf16), VM((4, SMALL // 8, 128), bf16), VM((4, SMALL // 8, 128), bf16),
-] + dma_sems(152) + dma_sems(NB)
-
-
-def kernel_f(up_in, down_in, wo_ref, dwq_ref, small_ref, out_in, ing_in, dup_ref, ddown_ref, dwo_ref, dwqt_ref, dkvw_ref, drw_ref,
-             dgain_ref, dfg_ref, out_ref, ing_ref):
-    ddown_ref[...] = down_in[0].astype(f32)
-    for s in range(4):
-        dup_ref[:, s * 128 : (s + 1) * 128] = up_in[0, s * 512 : (s + 1) * 512, :].astype(f32)
+] + dma_sems(168) + dma_sems(NB)
+
+
+def kernel_f(u0, u1, u2, u3, d0, d1, d2, d3, wo_ref, dwq_ref, small_ref, out_in, ing_in, dup_ref, ddown_ref, dwo_ref, dwqt_ref, dkvw_ref,
+             drw_ref, dgain_ref, dfg_ref, out_ref, ing_ref):
+    for t, (u, d) in enumerate(zip((u0, u1, u2, u3), (d0, d1, d2, d3))):
+        ddown_ref[:, t * 128 : (t + 1) * 128] = d[0].astype(f32)
+        for s in range(4):
+            dup_ref[:, (4 * t + s) * 128 : (4 * t + s + 1) * 128] = u[0, s].astype(f32)
 
     @pl.when(pl.program_id(0) == 0)
     def _():
@@ -787,7 +785,9 @@
         cost_estimate=pl.CostEstimate(flops=1 << 35, bytes_accessed=1 << 24, transcendentals=0),
     )(inputs, cotangent, norm_gain.reshape(1, D), ffn_gain.reshape(1, D), kv_weight, router_weight.T, routes.T,
       segment_ids.reshape(3, 128), wq, wo, up_weight, down_weight)
-    shared = shared.reshape(8, 2048, 128)
+    up_slots, down_slots = ([SHARED.index(u) for u in units] for units in (UP_UNIT, DOWN_UNIT))
+    ups = [pl.BlockSpec((1, 4, 128, 128), lambda i, k=k: (k, 0, i, 0)) for k in up_slots]
+    downs = [pl.BlockSpec((1, 512, 128), lambda i, k=k: (k, i, 0)) for k in down_slots]
 
     def whole(*shape):
         return pl.BlockSpec(shape, lambda i: (0,) * len(shape))
@@ -797,12 +797,12 @@
         grid=(4,),
         out_shape=[S((D, FF), f32), S((FF, D), f32), S((3 * H, D), f32), S((3 * H, D), f32), S((D, 128), f32), S((E, D), f32),
                    S((1, D), f32), S((1, D), f32), S((T, D), bf16), S((T, D), bf16)],
-        in_specs=[pl.BlockSpec((1, 2048, 128), lambda i: (i, 0, 0)), pl.BlockSpec((1, 2048, 128), lambda i: (4 + i, 0, 0)),
+        in_specs=ups + downs + [
                   whole(768, 128), whole(768, 128), whole(SMALL, 128), whole(T, D), whole(T, D)],
-        out_specs=[pl.BlockSpec((D, 512), lambda i: (0, i)), pl.BlockSpec((FF, 128), lambda i: (0, i)), whole(3 * H, D),
+        out_specs=[pl.BlockSpec((128, FF), lambda i: (i, 0)), pl.BlockSpec((512, D), lambda i: (i, 0)), whole(3 * H, D),
                    whole(3 * H, D), whole(D, 128), whole(E, D), whole(1, D), whole(1, D), whole(T, D), whole(T, D)],
         compiler_params=pltpu.CompilerParams(vmem_limit_bytes=62 << 20),
-    )(shared, shared, dwo.reshape(768, 128), dwq.reshape(768, 128), small.reshape(SMALL, 128), out, ing)
+    )(*[shared.reshape(8, 4, 512, 128)] * 4, *[shared.reshape(8, 2048, 128)] * 4, dwo.reshape(768, 128), dwq.reshape(768, 128), small.reshape(SMALL, 128), out, ing)
     return (out, ing, dgain.reshape(D), dfg.reshape(D), dkvw, drw.T,
             jnp.swapaxes(dwqt.reshape(3, H, D), 1, 2), dwo.reshape(3, H, D), dup, ddown)
 

time: 134 us -> 133 us (level)
  no operation moved by 1% of the time
where the time goes in v6:
time: 133 us; the launch traced here: 131 us
  Pallas kernels  130 us (98%)
    pallas_call x1, Pallas kernels, per_device(): pl.pallas_call(kernel_all, out_shape=[S((T, D), bf16), S((T, D), bf16), S...  123 us
    pallas_call x1, Pallas kernels, per_device(): pl.pallas_call(kernel_f, grid=(4,), out_shape=[S((D, FF), f32), S((FF, D)...  7.52 us

profile of v6, /device:TPU:0, one launch (start us, length us, event | category | flops | bytes accessed | tf_op | source)
XLA Modules:
  0.0 131.0 jit_solution(5930113630791562585)
XLA Ops:
  0.6 122.6 %shard_map.195 = (bf16[384,512]{1,0:T(8,128)(2,1)}, bf16[384,512]{1,0:T(8,128)(2,1)}, bf16[8,2,4,4,4,16,128]{6,5,4,3,2,1,0:T(8,128)(2,1)}, bf16[3,4,4,16,128]{4,...) custom-call(bf16[384,512]{1,0:T(8,128)(2,1)} %x_ref.1, ...), custom_call_target="tpu_custom_call" | custom-call | flops 34359738368 | bytes 16777216 | tf_op jit(solution)/shard_map/pallas_call | solution.py:777
  123.2 7.5 %shard_map.196 = (f32[512,2048]{1,0:T(8,128)}, f32[2048,512]{1,0:T(8,128)}, f32[192,512]{1,0:T(8,128)}, f32[192,512]{1,0:T(8,128)}, f32[512,128]{1,0:T(8,128)}, ...) custom-call(bf16[8,4,512,128]{3,2,1,0:T(8,128)(2,1)} %bitcast.21, ...), custom_call_target="tpu_custom_call" | custom-call | tf_op jit(solution)/shard_map/pallas_call | solution.py:795

commit v7 on v6

--- a/solution.py
+++ b/solution.py
@@ -157,11 +157,13 @@
         at = copies.place.at
         self.c, self.m = at["c"], [at[a] for a in order]
         us = pl.ds(u0, u1 - u0)
-        piece = lambda k=0: out.at[us, self.c, (self.m[0] - k + 4) % 4]
         quarter = lambda: out.at[us, self.c, self.m[0], self.m[1]]
         self.ids2 = [copies.add(quarter, quarter, (order[1], k)) for k in (1, 2, 3)]
-        self.ids1 = [copies.add(piece, piece, (order[0], k)) for k in (1, 2, 3)]
-        self.ids0 = [copies.add(lambda k=k: piece(k), lambda k=k: piece(k), ("c", 0)) for k in range(4)]
+        self.ids1, self.ids0 = [], []
+        for u in range(u0, u1):
+            piece = lambda k=0, u=u: out.at[u, self.c, (self.m[0] - k + 4) % 4]
+            self.ids1.append([copies.add(piece, piece, (order[0], k)) for k in (1, 2, 3)])
+            self.ids0.append([copies.add(functools.partial(piece, k), functools.partial(piece, k), ("c", 0)) for k in range(4)])
 
     def begin(self, values):
         for u, v in zip(range(self.u0, self.u1), values):
@@ -170,14 +172,20 @@
 
     def pass2(self):
         self.cp.arrived(self.ids2)
-        self.cp.start(self.ids1 + self.ids0[:1])
-
-    def forward(self, k):
-        self.cp.arrived(self.ids1[k - 1 : k])
-        self.cp.start(self.ids0[k : k + 1])
+
+    def send(self, i):
+        if i < len(self.ids1):
+            self.cp.start(self.ids1[i] + self.ids0[i][:1])
+
+    def forward(self, i):
+        if i < len(self.ids1):
+            for k in (1, 2, 3):
+                self.cp.arrived(self.ids1[i][k - 1 : k])
+                self.cp.start(self.ids0[i][k : k + 1])
 
     def finish(self):
-        self.cp.arrived(self.ids0)
+        for ids in self.ids0:
+            self.cp.arrived(ids)
 
 
 class SpreadOwner:
@@ -661,6 +669,12 @@
     def _():
         to_owner(2 * last).start()
 
+    for s in early:
+        s.pass3()
+    for s, (u0, u1, _) in zip(spreads, SPREADS):
+        s.begin([early[{0: 0, 4: 1, 8: 3}[4 * (SHARED[u] // 4)]].result(SHARED[u]) for u in range(u0, u1)])
+    for s, e, u in zip(owned_o, (early[0], early[2], early[3]), WO_UNIT):
+        s.begin(e.result(u))
     for j in range(J):
         js = slice(j * T, (j + 1) * T)
         rows[j] = sub8(jnp.transpose(dqacc[js, :])[0:H].astype(bf16).astype(f32) * 0.125)
@@ -669,12 +683,6 @@
         store_expert(lbig, core, [0, 1, 2], 2 * c, nn(gat[c * 384 : (c + 1) * 384, :], nm))
     for s in late:
         s.start0(0)
-    for s in early:
-        s.pass3()
-    for s, (u0, u1, _) in zip(spreads, SPREADS):
-        s.begin([early[{0: 0, 4: 1, 8: 3}[4 * (SHARED[u] // 4)]].result(SHARED[u]) for u in range(u0, u1)])
-    for s, e, u in zip(owned_o, (early[0], early[2], early[3]), WO_UNIT):
-        s.begin(e.result(u))
     acc_kv = tot
     acc_kv[:, 0:T] = jnp.transpose(gsend[me].astype(f32))
     for b in range(1, NB):
@@ -688,6 +696,7 @@
         s.pass0(0)
     for s in spreads:
         s.pass2()
+        s.send(0)
     gn = gn_ref[...] + tn(gat[...], wq_ref[...].reshape(EW, D)) + nt(gkv, kvw_ref[...])
     x = x_ref[...].astype(f32)
     inv = lax.rsqrt(jnp.mean(x * x, axis=-1, keepdims=True) + eps)
@@ -699,25 +708,31 @@
     parts += [v[:, t * 128 : (t + 1) * 128] for v in (dgain, dfg) for t in range(4)] + [jnp.zeros((SMALL - 616, 128), f32)]
     ssrc[...] = jnp.concatenate(parts, axis=0).astype(bf16).reshape(2, 4, SMALL // 8, 128)
     small.step(0)
+    small.step(1)
     for s in late:
         s.pass1()
-    small.step(1)
+    for s in spreads:
+        s.send(1)
+    small.step(2)
     hh = gn * gain_ref[...]
     ing_ref[...] = (gm_ref[...] + inv * (hh - n * jnp.mean(hh * n, axis=-1, keepdims=True))).astype(bf16)
     for s in late:
         s.pass2()
-    small.step(2)
+    for s in spreads:
+        s.send(2)
+        s.forward(0)
+    small.step(3)
     for s, t, u in zip(owned_q, late, range(3)):
         t.pass3()
         s.begin(t.result(u))
-    small.step(3)
-    for k in (1, 2, 3):
-        for s in spreads:
-            s.forward(k)
+    for s in spreads:
+        s.forward(1)
+    small.step(4)
     for s in owned_o + owned_q:
         s.finish()
-    small.step(4)
     small.step(5)
+    for s in spreads:
+        s.forward(2)
     small.step(6)
     for s in spreads:
         s.finish()
@@ -741,7 +756,7 @@
     VM((3, 4, 4, 16, 128), bf16),
     VM((2, 4, SMALL // 8, 128), bf16), VM((4, SMALL // 8, 128), bf16), VM((4, SMALL // 8, 128), bf16),
     VM((3, SMALL // 8, 128), bf16), VM((4, SMALL // 8, 128), bf16), VM((4, SMALL // 8, 128), bf16),
-] + dma_sems(168) + dma_sems(NB)
+] + dma_sems(203) + dma_sems(NB)
 
 
 def kernel_f(u0, u1, u2, u3, d0, d1, d2, d3, wo_ref, dwq_ref, small_ref, out_in, ing_in, dup_ref, ddown_ref, dwo_ref, dwqt_ref, dkvw_ref,

time: 133 us -> 129 us (0.970)
  Pallas kernels: 130 us -> 126 us
    pallas_call x1, Pallas kernels: 123 us -> 119 us  [per_device(): pl.pallas_call(kernel_all, out_shape=[S((T, D), bf16), S((T, D), bf16), S...]
where the time goes in v7:
time: 129 us; the launch traced here: 127 us
  Pallas kernels  126 us (98%)
    pallas_call x1, Pallas kernels, per_device(): pl.pallas_call(kernel_all, out_shape=[S((T, D), bf16), S((T, D), bf16), S...  119 us
    pallas_call x1, Pallas kernels, per_device(): pl.pallas_call(kernel_f, grid=(4,), out_shape=[S((D, FF), f32), S((FF, D)...  7.52 us

profile of v7, /device:TPU:0, one launch (start us, length us, event | category | flops | bytes accessed | tf_op | source)
XLA Modules:
  0.0 127.1 jit_solution(16381183664541080290)
XLA Ops:
  0.6 118.7 %shard_map.195 = (bf16[384,512]{1,0:T(8,128)(2,1)}, bf16[384,512]{1,0:T(8,128)(2,1)}, bf16[8,2,4,4,4,16,128]{6,5,4,3,2,1,0:T(8,128)(2,1)}, bf16[3,4,4,16,128]{4,...) custom-call(bf16[384,512]{1,0:T(8,128)(2,1)} %x_ref.1, ...), custom_call_target="tpu_custom_call" | custom-call | flops 34359738368 | bytes 16777216 | tf_op jit(solution)/shard_map/pallas_call | solution.py:792
  119.4 7.5 %shard_map.196 = (f32[512,2048]{1,0:T(8,128)}, f32[2048,512]{1,0:T(8,128)}, f32[192,512]{1,0:T(8,128)}, f32[192,512]{1,0:T(8,128)}, f32[512,128]{1,0:T(8,128)}, ...) custom-call(bf16[8,4,512,128]{3,2,1,0:T(8,128)(2,1)} %bitcast.21, ...), custom_call_target="tpu_custom_call" | custom-call | tf_op jit(solution)/shard_map/pallas_call | solution.py:810

commit v8 on v7

--- a/solution.py
+++ b/solution.py
@@ -57,12 +57,6 @@
     def device(self, **moved):
         at = {**self.at, **moved}
         return (at["x"] * 4 + at["y"], at["z"] * 2 + at["c"])
-
-    def enter(self, peers):
-        bar = pltpu.get_barrier_semaphore()
-        for p in peers:
-            pl.semaphore_signal(bar, inc=1, device_id=self.peers[p], device_id_type=MESH)
-        pl.semaphore_wait(bar, len(peers))
 
 
 class Copies:
@@ -152,8 +146,8 @@
 
 
 class Spread:
-    def __init__(self, copies, out, u0, u1, order):
-        self.cp, self.out, self.u0, self.u1 = copies, out, u0, u1
+    def __init__(self, copies, out, kept, kept_sem, u0, u1, order):
+        self.cp, self.out, self.kept, self.kept_sem, self.u0, self.u1 = copies, out, kept, kept_sem, u0, u1
         at = copies.place.at
         self.c, self.m = at["c"], [at[a] for a in order]
         us = pl.ds(u0, u1 - u0)
@@ -183,9 +177,13 @@
                 self.cp.arrived(self.ids1[i][k - 1 : k])
                 self.cp.start(self.ids0[i][k : k + 1])
 
-    def finish(self):
-        for ids in self.ids0:
-            self.cp.arrived(ids)
+    def finish(self, i):
+        if i < len(self.ids0):
+            self.cp.arrived(self.ids0[i])
+            self.keep(self.u0 + i).start()
+
+    def keep(self, u):
+        return pltpu.make_async_copy(self.out.at[u], self.kept.at[u], self.kept_sem.at[u])
 
 
 class SpreadOwner:
@@ -241,12 +239,12 @@
 
 
 UNITS = 11
-UP_UNIT, DOWN_UNIT, WO_UNIT = [0, 4, 5, 8], [1, 2, 6, 9], [3, 7, 10]
+UP_UNIT, DOWN_UNIT, WO_UNIT = [0, 4, 8, 2], [1, 5, 9, 6], [3, 7, 10]
 SHARED = sorted(UP_UNIT + DOWN_UNIT)
 OWNER_ORDERS = ["zxy", "xzy", "yzx"]
-EARLY = [([(0, 1), (1, 3), (3, 4)], [(0, 1), (1, 4)], "zxy"), ([(4, 5), (5, 6), (6, 7)], [(4, 6), (6, 7)], "xyz"),
-         ([(7, 8)], [(7, 8)], "xzy"), ([(8, 9), (9, 10), (10, 11)], [(8, 9), (9, 11)], "yzx")]
-UP_PART, DOWN_PARTS, WO_PARTS = [(0, 0), (1, 0), (1, 1), (3, 0)], [(0, 1), (1, 2), (3, 1)], [(0, 2), (2, 0), (3, 2)]
+EARLY = [([(0, 2), (2, 3), (3, 4)], [(0, 2), (2, 4)], "zxy"), ([(4, 6), (6, 7)], [(4, 6), (6, 7)], "xyz"),
+         ([(7, 8)], [(7, 8)], "xzy"), ([(8, 10), (10, 11)], [(8, 10), (10, 11)], "yzx")]
+CHUNK_PARTS, WO_PARTS = [[(0, 0)], [(1, 0)], [(3, 0)], [(0, 1), (1, 1)]], [(0, 2), (2, 0), (3, 1)]
 SPREADS = [(0, 3, "zxy"), (3, 6, "xyz"), (6, 8, "yzx")]
 
 
@@ -448,8 +446,8 @@
 
 
 def kernel_all(x_ref, cot_ref, gain_ref, fgain_ref, kvw_ref, rw_ref, rt_ref, seg_ref, wq_in, wo_in, up_hbm, down_hbm,
-               out_ref, ing_ref, all_ref, dwo_ref, dwq_ref, small_ref,
-               up_ref, down_ref, wsem, normed_ref, gate_ref, kv_ref, wq_ref, wo_ref, att_ref, qt_ref, table, kaug, vaug, vt, macc, acc,
+               out_ref, ing_ref, all_hbm, dwo_ref, dwq_ref, small_ref,
+               shared, all_sem, up_ref, down_ref, wsem, normed_ref, gate_ref, kv_ref, wq_ref, wo_ref, att_ref, qt_ref, table, kaug, vaug, vt, macc, acc,
                rows, gat, gm_ref, gn_ref, drw_ref, dfg_ref, big, r0, r1, r2, ex,
                dat_ref, qa, da, dqacc, tot, gsend, grecv, lbig, l0, l1, l2, lex, ssrc, shalf, s0, s1, sy, sz, send, recv, ksend, krecv):
     place = Place()
@@ -461,7 +459,7 @@
     lbig7 = lbig.reshape(2, 3, 4, 4, 4, 16, 128)
     early = [Scatter(copies, big7, (r0, r1, r2), ex, parts, groups, o) for parts, groups, o in EARLY]
     late = [Scatter(copies, lbig7, (l0, l1, l2), lex, [(u, u + 1)], [(u, u + 1)], o) for u, o in enumerate(OWNER_ORDERS)]
-    spreads = [Spread(copies, all_ref, u0, u1, o) for u0, u1, o in SPREADS]
+    spreads = [Spread(copies, shared, all_hbm, all_sem, u0, u1, o) for u0, u1, o in SPREADS]
     owned_o = [SpreadOwner(copies, dwo_ref, u, plane_axes(o)[0]) for u, o in enumerate(OWNER_ORDERS)]
     owned_q = [SpreadOwner(copies, dwq_ref, u, plane_axes(o)[0]) for u, o in enumerate(OWNER_ORDERS)]
     small = SmallSum(copies, ssrc, shalf, s0, s1, sy, sz, small_ref)
@@ -476,8 +474,6 @@
         cp.start()
     wq_ref[me] = wq_in[...]
     wo_ref[me] = wo_in[...]
-    pl.semaphore_wait(bar, len(ALL_PEERS) + NB - 1)
-    gq.start()
 
     x = x_ref[...].astype(f32)
     inv = lax.rsqrt(jnp.mean(x * x, axis=-1, keepdims=True) + eps)
@@ -493,6 +489,8 @@
         hi = jnp.floor(n * 0.0625)
         tail = jnp.where(row == 2 * s, hi, jnp.where(row == 2 * s + 1, n - 16.0 * hi, tail))
     kv_ref[me, T:KVR, :] = tail.astype(bf16)
+    pl.semaphore_wait(bar, len(ALL_PEERS) + NB - 1)
+    gq.start()
     gk.start()
     gates_of(normed, rw_ref, rt_ref, gate_ref)
     gq.forward()
@@ -527,25 +525,30 @@
     C = 512
     out = mixed
     gsec = jnp.zeros((T, D), f32)
+    ahead = nn(second, up_ref[:, 0:C]), nt(cot, down_ref[0:C, :])
     for c in range(FF // C):
         cs = slice(c * C, (c + 1) * C)
-        v = nn(second, up_ref[:, cs])
+        v, gact = ahead
+        if c + 1 < FF // C:
+            ns = slice((c + 1) * C, (c + 2) * C)
+            ahead = nn(second, up_ref[:, ns]), nt(cot, down_ref[ns, :])
         v2 = v * v
         th = jnp.tanh(0.7978845608028654 * (v + 0.044715 * v * v2))
         a = (0.5 * v * (1.0 + th)).astype(bf16)
         dth = 0.5 * (1.0 + th) + 0.5 * v * (1.0 - th * th) * (0.7978845608028654 * (1.0 + 0.134145 * v2))
-        gh = (nt(cot, down_ref[cs, :]) * dth).astype(bf16)
+        gh = (gact * dth).astype(bf16)
         out = out + nn(a, down_ref[cs, :])
         gsec = gsec + nt(gh, up_ref[:, cs])
         gdown = tn(a, cot).astype(bf16)
         gup = nn(second_t, gh).astype(bf16)
         for t in range(4):
             ts = slice(t * 128, (t + 1) * 128)
-            big[(core + c // 2) % 2, DOWN_UNIT[t], c % 2 * C : c % 2 * C + C, :] = gdown[:, ts]
+            big[(core + t // 2) % 2, DOWN_UNIT[c], t % 2 * 512 : t % 2 * 512 + 512, :] = gdown[:, ts]
             big[(core + t // 2) % 2, UP_UNIT[c], t % 2 * 512 : t % 2 * 512 + 512, :] = gup[:, ts]
-        early[UP_PART[c][0]].start0(UP_PART[c][1])
-    for b, i in DOWN_PARTS:
-        early[b].start0(i)
+        for b, i in CHUNK_PARTS[c]:
+            early[b].start0(i)
+    for i in (0, 1, 3):
+        early[i].pass0(0)
     out_ref[...] = out.astype(bf16)
     dfg_ref[...] = jnp.sum(gsec * n, axis=0, keepdims=True)
     hh = gsec * fgain
@@ -559,8 +562,6 @@
     for c in range(4):
         w = wo_ref[2 * c : 2 * c + 2].reshape(2 * 3 * H, D)
         table[c * 48 : (c + 1) * 48] = nt(w, gml).reshape(48, 8, T)
-    for i in (0, 1, 3):
-        early[i].pass0(0)
     dots = []
     row = lax.broadcasted_iota(i32, (H, T), 0)
     for j in range(J):
@@ -591,6 +592,8 @@
         qa[js, :] = jnp.transpose(qt_ref[:, js].astype(f32)).astype(bf16)
         da[js, :] = jnp.transpose(dat_ref[:, js].astype(f32)).astype(bf16)
     dqacc[...] = jnp.zeros(dqacc.shape, f32)
+    for i, h in ((0, 1), (1, 1), (2, 0), (3, 1)):
+        early[i].pass0(h)
     last = me // 2
 
     def half_block(sb, half, masked):
@@ -626,15 +629,11 @@
         return pltpu.make_async_remote_copy(src_ref=gsend.at[b], dst_ref=grecv.at[b], send_sem=ksend.at[b],
                                             recv_sem=krecv.at[b], device_id=(dp, b), device_id_type=MESH)
 
-    def at_0():
-        for i, h in ((0, 1), (1, 1), (2, 0), (3, 1)):
-            early[i].pass0(h)
-
-    def at_4():
+    def at_3():
         for s in early:
             s.pass1()
 
-    def at_6():
+    def at_5():
         for s in early:
             s.pass2()
 
@@ -650,8 +649,8 @@
                 to_owner(2 * sb).start()
                 to_owner(2 * sb + 1).start()
 
-        pl.when(i == 0)(at_0)
-        pl.when(i == 4)(at_4)
+        pl.when(i == 3)(at_3)
+        pl.when(i == 5)(at_5)
 
         return carry
 
@@ -660,7 +659,6 @@
     def last_step(half, carry):
         half_block(last, half, True)
 
-        pl.when(half == 0)(at_6)
         return carry
 
     lax.fori_loop(0, 2, last_step, 0)
@@ -671,32 +669,35 @@
 
     for s in early:
         s.pass3()
-    for s, (u0, u1, _) in zip(spreads, SPREADS):
-        s.begin([early[{0: 0, 4: 1, 8: 3}[4 * (SHARED[u] // 4)]].result(SHARED[u]) for u in range(u0, u1)])
+    for s, e, (u0, u1, _) in zip(spreads, (early[0], early[1], early[3]), SPREADS):
+        s.begin([e.result(SHARED[u]) for u in range(u0, u1)])
     for s, e, u in zip(owned_o, (early[0], early[2], early[3]), WO_UNIT):
         s.begin(e.result(u))
     for j in range(J):
         js = slice(j * T, (j + 1) * T)
         rows[j] = sub8(jnp.transpose(dqacc[js, :])[0:H].astype(bf16).astype(f32) * 0.125)
     to_experts(routes, rows, gat)
+    for s in spreads:
+        s.pass2()
+        s.send(0)
     for c in range(4):
         store_expert(lbig, core, [0, 1, 2], 2 * c, nn(gat[c * 384 : (c + 1) * 384, :], nm))
     for s in late:
         s.start0(0)
-    acc_kv = tot
-    acc_kv[:, 0:T] = jnp.transpose(gsend[me].astype(f32))
+    for s in spreads:
+        s.send(1)
+    dqacc[0:T, :] = gsend[me].astype(f32)
     for b in range(1, NB):
         @pl.when(b > me)
         def _(b=b):
             from_device(b).wait_recv()
-            acc_kv[:, 0:T] += jnp.transpose(grecv[b].astype(f32))
-    gkv = jnp.transpose(acc_kv[:, 0:T]).astype(bf16)
+            dqacc[0:T, :] += grecv[b].astype(f32)
+    gkv = dqacc[0:T, :].astype(bf16)
     dkvw = tn(nm, gkv).astype(bf16)
     for s in late:
         s.pass0(0)
     for s in spreads:
-        s.pass2()
-        s.send(0)
+        s.send(2)
     gn = gn_ref[...] + tn(gat[...], wq_ref[...].reshape(EW, D)) + nt(gkv, kvw_ref[...])
     x = x_ref[...].astype(f32)
     inv = lax.rsqrt(jnp.mean(x * x, axis=-1, keepdims=True) + eps)
@@ -712,30 +713,32 @@
     for s in late:
         s.pass1()
     for s in spreads:
-        s.send(1)
+        s.forward(0)
     small.step(2)
     hh = gn * gain_ref[...]
     ing_ref[...] = (gm_ref[...] + inv * (hh - n * jnp.mean(hh * n, axis=-1, keepdims=True))).astype(bf16)
     for s in late:
         s.pass2()
     for s in spreads:
-        s.send(2)
-        s.forward(0)
+        s.finish(0)
+        s.forward(1)
     small.step(3)
     for s, t, u in zip(owned_q, late, range(3)):
         t.pass3()
         s.begin(t.result(u))
     for s in spreads:
-        s.forward(1)
+        s.finish(1)
+        s.forward(2)
     small.step(4)
     for s in owned_o + owned_q:
         s.finish()
     small.step(5)
     for s in spreads:
-        s.forward(2)
+        s.finish(2)
     small.step(6)
     for s in spreads:
-        s.finish()
+        for u in range(s.u0, s.u1):
+            s.keep(u).wait()
     for b in range(NB - 1):
         @pl.when(b < me)
         def _(b=b):
@@ -744,6 +747,7 @@
 
 
 SCRATCH = [
+    VM((8, 2, 4, 4, 4, 16, 128), bf16), pltpu.SemaphoreType.DMA((8,)),
     VM((D, FF), bf16), VM((FF, D), bf16), pltpu.SemaphoreType.DMA((2,)), VM((T, D), bf16), VM((J, T), f32), VM((NB, KVR, 128), bf16),
     VM((NB, 3 * H, D), bf16), VM((NB, 3 * H, D), bf16), VM((H, ROWS), bf16), VM((128, ROWS), bf16), VM((EW // 8, 8, T), f32),
     VM((ROWS, 128), bf16), VM((ROWS, 128), bf16), VM((80, ROWS), bf16), VM((8, ROWS), f32), VM((80, ROWS), f32),
@@ -756,13 +760,13 @@
     VM((3, 4, 4, 16, 128), bf16),
     VM((2, 4, SMALL // 8, 128), bf16), VM((4, SMALL // 8, 128), bf16), VM((4, SMALL // 8, 128), bf16),
     VM((3, SMALL // 8, 128), bf16), VM((4, SMALL // 8, 128), bf16), VM((4, SMALL // 8, 128), bf16),
-] + dma_sems(203) + dma_sems(NB)
-
-
-def kernel_f(u0, u1, u2, u3, d0, d1, d2, d3, wo_ref, dwq_ref, small_ref, out_in, ing_in, dup_ref, ddown_ref, dwo_ref, dwqt_ref, dkvw_ref,
+] + dma_sems(201) + dma_sems(NB)
+
+
+def kernel_f(u0, u1, u2, u3, down, wo_ref, dwq_ref, small_ref, out_in, ing_in, dup_ref, ddown_ref, dwo_ref, dwqt_ref, dkvw_ref,
              drw_ref, dgain_ref, dfg_ref, out_ref, ing_ref):
-    for t, (u, d) in enumerate(zip((u0, u1, u2, u3), (d0, d1, d2, d3))):
-        ddown_ref[:, t * 128 : (t + 1) * 128] = d[0].astype(f32)
+    for t, u in enumerate((u0, u1, u2, u3)):
+        ddown_ref[:, t * 128 : (t + 1) * 128] = down[0, t].astype(f32)
         for s in range(4):
             dup_ref[:, (4 * t + s) * 128 : (4 * t + s + 1) * 128] = u[0, s].astype(f32)
 
@@ -794,15 +798,16 @@
         out_shape=[S((T, D), bf16), S((T, D), bf16), S((8, 2, 4, 4, 4, 16, 128), bf16), S((3, 4, 4, 16, 128), bf16),
                    S((3, 4, 4, 16, 128), bf16), S((2, 4, SMALL // 8, 128), bf16)],
         in_specs=[vmem] * 10 + [anywhere] * 2,
-        out_specs=[vmem] * 6,
+        out_specs=[vmem, vmem, anywhere, vmem, vmem, vmem],
         scratch_shapes=SCRATCH,
         compiler_params=pltpu.CompilerParams(vmem_limit_bytes=62 << 20, collective_id=1, has_side_effects=True),
         cost_estimate=pl.CostEstimate(flops=1 << 35, bytes_accessed=1 << 24, transcendentals=0),
     )(inputs, cotangent, norm_gain.reshape(1, D), ffn_gain.reshape(1, D), kv_weight, router_weight.T, routes.T,
       segment_ids.reshape(3, 128), wq, wo, up_weight, down_weight)
     up_slots, down_slots = ([SHARED.index(u) for u in units] for units in (UP_UNIT, DOWN_UNIT))
+    assert down_slots == [1, 4, 7, 5]
     ups = [pl.BlockSpec((1, 4, 128, 128), lambda i, k=k: (k, 0, i, 0)) for k in up_slots]
-    downs = [pl.BlockSpec((1, 512, 128), lambda i, k=k: (k, i, 0)) for k in down_slots]
+    downs = [pl.BlockSpec((1, 4, 512, 128), lambda i: (1 + 3 * i - 5 * (i // 3), 0, 0, 0))]
 
     def whole(*shape):
         return pl.BlockSpec(shape, lambda i: (0,) * len(shape))
@@ -817,7 +822,7 @@
         out_specs=[pl.BlockSpec((128, FF), lambda i: (i, 0)), pl.BlockSpec((512, D), lambda i: (i, 0)), whole(3 * H, D),
                    whole(3 * H, D), whole(D, 128), whole(E, D), whole(1, D), whole(1, D), whole(T, D), whole(T, D)],
         compiler_params=pltpu.CompilerParams(vmem_limit_bytes=62 << 20),
-    )(*[shared.reshape(8, 4, 512, 128)] * 4, *[shared.reshape(8, 2048, 128)] * 4, dwo.reshape(768, 128), dwq.reshape(768, 128), small.reshape(SMALL, 128), out, ing)
+    )(*[shared.reshape(8, 4, 512, 128)] * 5, dwo.reshape(768, 128), dwq.reshape(768, 128), small.reshape(SMALL, 128), out, ing)
     return (out, ing, dgain.reshape(D), dfg.reshape(D), dkvw, drw.T,
             jnp.swapaxes(dwqt.reshape(3, H, D), 1, 2), dwo.reshape(3, H, D), dup, ddown)
 

time: 129 us -> 128 us (level)
  no operation moved by 1% of the time
where the time goes in v8:
time: 128 us; the launch traced here: 127 us
  Pallas kernels  126 us (98%)
    pallas_call x1, Pallas kernels, per_device(): pl.pallas_call(kernel_all, out_shape=[S((T, D), bf16), S((T, D), bf16), S...  118 us
    pallas_call x1, Pallas kernels, per_device(): pl.pallas_call(kernel_f, grid=(4,), out_shape=[S((D, FF), f32), S((FF, D)...  7.53 us

profile of v8, /device:TPU:0, one launch (start us, length us, event | category | flops | bytes accessed | tf_op | source)
XLA Modules:
  0.0 126.8 jit_solution(674723063484945990)
XLA Ops:
  0.6 118.5 %shard_map.195 = (bf16[384,512]{1,0:T(8,128)(2,1)}, bf16[384,512]{1,0:T(8,128)(2,1)}, bf16[8,2,4,4,4,16,128]{6,5,4,3,2,1,0:T(8,128)(2,1)}, bf16[3,4,4,16,128]{4,...) custom-call(bf16[384,512]{1,0:T(8,128)(2,1)} %x_ref.1, ...), custom_call_target="tpu_custom_call" | custom-call | flops 34359738368 | bytes 16777216 | tf_op jit(solution)/shard_map/pallas_call | solution.py:796
  119.1 7.5 %shard_map.196 = (f32[512,2048]{1,0:T(8,128)}, f32[2048,512]{1,0:T(8,128)}, f32[192,512]{1,0:T(8,128)}, f32[192,512]{1,0:T(8,128)}, f32[512,128]{1,0:T(8,128)}, ...) custom-call(bf16[8,4,512,128]{3,2,1,0:T(8,128)(2,1)} %bitcast.20, ...), custom_call_target="tpu_custom_call" | custom-call | tf_op jit(solution)/shard_map/pallas_call | solution.py:815

commit v9 on v8

--- a/solution.py
+++ b/solution.py
@@ -677,15 +677,13 @@
         js = slice(j * T, (j + 1) * T)
         rows[j] = sub8(jnp.transpose(dqacc[js, :])[0:H].astype(bf16).astype(f32) * 0.125)
     to_experts(routes, rows, gat)
-    for s in spreads:
-        s.pass2()
-        s.send(0)
     for c in range(4):
         store_expert(lbig, core, [0, 1, 2], 2 * c, nn(gat[c * 384 : (c + 1) * 384, :], nm))
     for s in late:
         s.start0(0)
     for s in spreads:
-        s.send(1)
+        s.pass2()
+        s.send(0)
     dqacc[0:T, :] = gsend[me].astype(f32)
     for b in range(1, NB):
         @pl.when(b > me)
@@ -697,7 +695,7 @@
     for s in late:
         s.pass0(0)
     for s in spreads:
-        s.send(2)
+        s.send(1)
     gn = gn_ref[...] + tn(gat[...], wq_ref[...].reshape(EW, D)) + nt(gkv, kvw_ref[...])
     x = x_ref[...].astype(f32)
     inv = lax.rsqrt(jnp.mean(x * x, axis=-1, keepdims=True) + eps)
@@ -712,24 +710,25 @@
     small.step(1)
     for s in late:
         s.pass1()
+    small.step(2)
     for s in spreads:
+        s.send(2)
         s.forward(0)
-    small.step(2)
     hh = gn * gain_ref[...]
     ing_ref[...] = (gm_ref[...] + inv * (hh - n * jnp.mean(hh * n, axis=-1, keepdims=True))).astype(bf16)
     for s in late:
         s.pass2()
+    small.step(3)
     for s in spreads:
         s.finish(0)
         s.forward(1)
-    small.step(3)
     for s, t, u in zip(owned_q, late, range(3)):
         t.pass3()
         s.begin(t.result(u))
+    small.step(4)
     for s in spreads:
         s.finish(1)
         s.forward(2)
-    small.step(4)
     for s in owned_o + owned_q:
         s.finish()
     small.step(5)

time: 128 us -> 126 us (0.984)
  Pallas kernels: 126 us -> 123 us
    pallas_call x1, Pallas kernels: 118 us -> 116 us  [per_device(): pl.pallas_call(kernel_all, out_shape=[S((T, D), bf16), S((T, D), bf16), S...]
where the time goes in v9:
time: 126 us; the launch traced here: 124 us
  Pallas kernels  123 us (98%)
    pallas_call x1, Pallas kernels, per_device(): pl.pallas_call(kernel_all, out_shape=[S((T, D), bf16), S((T, D), bf16), S...  116 us
    pallas_call x1, Pallas kernels, per_device(): pl.pallas_call(kernel_f, grid=(4,), out_shape=[S((D, FF), f32), S((FF, D)...  7.53 us

profile of v9, /device:TPU:0, one launch (start us, length us, event | category | flops | bytes accessed | tf_op | source)
XLA Modules:
  0.0 124.1 jit_solution(16403601409525376966)
XLA Ops:
  0.6 115.7 %shard_map.195 = (bf16[384,512]{1,0:T(8,128)(2,1)}, bf16[384,512]{1,0:T(8,128)(2,1)}, bf16[8,2,4,4,4,16,128]{6,5,4,3,2,1,0:T(8,128)(2,1)}, bf16[3,4,4,16,128]{4,...) custom-call(bf16[384,512]{1,0:T(8,128)(2,1)} %x_ref.1, ...), custom_call_target="tpu_custom_call" | custom-call | flops 34359738368 | bytes 16777216 | tf_op jit(solution)/shard_map/pallas_call | solution.py:795
  116.4 7.5 %shard_map.196 = (f32[512,2048]{1,0:T(8,128)}, f32[2048,512]{1,0:T(8,128)}, f32[192,512]{1,0:T(8,128)}, f32[192,512]{1,0:T(8,128)}, f32[512,128]{1,0:T(8,128)}, ...) custom-call(bf16[8,4,512,128]{3,2,1,0:T(8,128)(2,1)} %bitcast.20, ...), custom_call_target="tpu_custom_call" | custom-call | tf_op jit(solution)/shard_map/pallas_call | solution.py:814

commit v10 on v9

--- a/solution.py
+++ b/solution.py
@@ -61,7 +61,7 @@
 
 class Copies:
     def __init__(self, place, send, recv):
-        self.place, self.send, self.recv, self.made = place, send, recv, []
+        self.place, self.send, self.recv, self.made, self.open = place, send, recv, [], set()
 
     def add(self, src, dst, peer):
         self.made.append((src, dst, peer))
@@ -73,6 +73,7 @@
                                             device_id=self.place.peers[peer], device_id_type=MESH)
 
     def start(self, ids):
+        self.open |= set(ids)
         for i in ids:
             self.get(i).start()
 
@@ -80,23 +81,27 @@
         for i in ids:
             self.get(i).wait_recv()
 
-    def sent(self, ids):
-        for i in ids:
+    def drain(self, keep=()):
+        for i in sorted(self.open - set(keep)):
             self.get(i).wait_send()
-
-    def drain(self):
-        self.sent(range(len(self.made)))
+        self.open &= set(keep)
 
 
 class Scatter:
-    def __init__(self, copies, big, r, ex, parts, groups, order):
+    def __init__(self, copies, big, r, ex, parts, groups, order, cut=False):
         self.cp, self.big, self.r, self.ex = copies, big, r, ex
         self.parts, self.groups, self.u0, self.u1 = parts, groups, parts[0][0], parts[-1][1]
         at = copies.place.at
         self.m = m = [at[a] for a in order]
         rng = lambda g: pl.ds(g[0], g[1] - g[0])
         us = rng((self.u0, self.u1))
-        self.part_ids = [copies.add(lambda g=g: big.at[1, rng(g)], lambda g=g: r[0].at[rng(g)], ("c", 0)) for g in parts]
+        if cut:
+            self.parts = parts * 4
+            z = order.index("z")
+            at_z = lambda q: (parts[0][0],) + (slice(None),) * z + (q,)
+            self.part_ids = [copies.add(lambda q=q: big.at[(1,) + at_z(q)], lambda q=q: r[0].at[at_z(q)], ("c", 0)) for q in range(4)]
+        else:
+            self.part_ids = [copies.add(lambda g=g: big.at[1, rng(g)], lambda g=g: r[0].at[rng(g)], ("c", 0)) for g in parts]
         self.group_ids = [
             [copies.add(lambda g=g, k=k: big.at[0, rng(g), (m[0] + k) % 4], lambda g=g, k=k: r[1].at[rng(g), k - 1], (order[0], k))
              for k in (1, 2, 3)] for g in groups]
@@ -356,8 +361,8 @@
     return acc
 
 
-def to_experts(routes, rows, out):
-    for e in range(E):
+def to_experts(routes, rows, out, experts=range(E)):
+    for e in experts:
         acc = jnp.zeros((8, 8, T), f32)
         for j in range(J):
             acc = jnp.where((routes[j] == e)[None], rows[j], acc)
@@ -458,7 +463,7 @@
     big7 = big.reshape(2, UNITS, 4, 4, 4, 16, 128)
     lbig7 = lbig.reshape(2, 3, 4, 4, 4, 16, 128)
     early = [Scatter(copies, big7, (r0, r1, r2), ex, parts, groups, o) for parts, groups, o in EARLY]
-    late = [Scatter(copies, lbig7, (l0, l1, l2), lex, [(u, u + 1)], [(u, u + 1)], o) for u, o in enumerate(OWNER_ORDERS)]
+    late = [Scatter(copies, lbig7, (l0, l1, l2), lex, [(u, u + 1)], [(u, u + 1)], o, cut=True) for u, o in enumerate(OWNER_ORDERS)]
     spreads = [Spread(copies, shared, all_hbm, all_sem, u0, u1, o) for u0, u1, o in SPREADS]
     owned_o = [SpreadOwner(copies, dwo_ref, u, plane_axes(o)[0]) for u, o in enumerate(OWNER_ORDERS)]
     owned_q = [SpreadOwner(copies, dwq_ref, u, plane_axes(o)[0]) for u, o in enumerate(OWNER_ORDERS)]
@@ -676,11 +681,11 @@
     for j in range(J):
         js = slice(j * T, (j + 1) * T)
         rows[j] = sub8(jnp.transpose(dqacc[js, :])[0:H].astype(bf16).astype(f32) * 0.125)
-    to_experts(routes, rows, gat)
     for c in range(4):
+        to_experts(routes, rows, gat, range(6 * c, 6 * c + 6))
         store_expert(lbig, core, [0, 1, 2], 2 * c, nn(gat[c * 384 : (c + 1) * 384, :], nm))
-    for s in late:
-        s.start0(0)
+        for s in late:
+            s.start0(c)
     for s in spreads:
         s.pass2()
         s.send(0)
@@ -692,6 +697,7 @@
             dqacc[0:T, :] += grecv[b].astype(f32)
     gkv = dqacc[0:T, :].astype(bf16)
     dkvw = tn(nm, gkv).astype(bf16)
+    done = set(copies.open)
     for s in late:
         s.pass0(0)
     for s in spreads:
@@ -707,6 +713,7 @@
     parts += [v[:, t * 128 : (t + 1) * 128] for v in (dgain, dfg) for t in range(4)] + [jnp.zeros((SMALL - 616, 128), f32)]
     ssrc[...] = jnp.concatenate(parts, axis=0).astype(bf16).reshape(2, 4, SMALL // 8, 128)
     small.step(0)
+    copies.drain(copies.open - done)
     small.step(1)
     for s in late:
         s.pass1()
@@ -729,6 +736,7 @@
     for s in spreads:
         s.finish(1)
         s.forward(2)
+    copies.drain([i for s in owned_q for i in s.ids] + small.ids[4])
     for s in owned_o + owned_q:
         s.finish()
     small.step(5)
@@ -759,31 +767,51 @@
     VM((3, 4, 4, 16, 128), bf16),
     VM((2, 4, SMALL // 8, 128), bf16), VM((4, SMALL // 8, 128), bf16), VM((4, SMALL // 8, 128), bf16),
     VM((3, SMALL // 8, 128), bf16), VM((4, SMALL // 8, 128), bf16), VM((4, SMALL // 8, 128), bf16),
-] + dma_sems(201) + dma_sems(NB)
-
-
-def kernel_f(u0, u1, u2, u3, down, wo_ref, dwq_ref, small_ref, out_in, ing_in, dup_ref, ddown_ref, dwo_ref, dwqt_ref, dkvw_ref,
-             drw_ref, dgain_ref, dfg_ref, out_ref, ing_ref):
-    for t, u in enumerate((u0, u1, u2, u3)):
-        ddown_ref[:, t * 128 : (t + 1) * 128] = down[0, t].astype(f32)
-        for s in range(4):
-            dup_ref[:, (4 * t + s) * 128 : (4 * t + s + 1) * 128] = u[0, s].astype(f32)
-
-    @pl.when(pl.program_id(0) == 0)
-    def _():
+] + dma_sems(210) + dma_sems(NB)
+
+
+def kernel_f(all_hbm, wo_hbm, dwq_hbm, small_hbm, out_in, ing_in,
+             dup_hbm, ddown_hbm, dwo_ref, dwqt_ref, dkvw_ref, drw_ref, dgain_ref, dfg_ref, out_hbm, ing_hbm,
+             units, wo_ref, dwq_ref, small_ref, up, down, held, in_sem, out_sem):
+    order = [SHARED.index(u) for pair in zip(UP_UNIT, DOWN_UNIT) for u in pair]
+    loads = [pltpu.make_async_copy(all_hbm.at[u], units.at[u], in_sem.at[i]) for i, u in enumerate(order)]
+    loads += [pltpu.make_async_copy(src, dst, in_sem.at[8 + i])
+              for i, (src, dst) in enumerate(((wo_hbm, wo_ref), (dwq_hbm, dwq_ref), (small_hbm, small_ref),
+                                              (out_in, held.at[0]), (ing_in, held.at[1])))]
+    for cp in loads:
+        cp.start()
+    stores = []
+    for c in range(4):
+        cs = slice(c * 512, (c + 1) * 512)
+        u, d = order[2 * c : 2 * c + 2]
+        loads[2 * c].wait()
         for t in range(4):
-            ts = slice(t * 128, (t + 1) * 128)
-            dwo_ref[:, ts] = wo_ref[t * 192 : (t + 1) * 192, :].astype(f32)
-            dwqt_ref[:, ts] = dwq_ref[t * 192 : (t + 1) * 192, :].astype(f32)
-        small = small_ref[512:SMALL, :].astype(f32)
-        dkvw_ref[...] = small_ref[0:512, :].astype(f32)
+            up[:, c * 512 + t * 128 : c * 512 + (t + 1) * 128] = units[u, t].astype(f32)
+        stores.append(pltpu.make_async_copy(up.at[:, cs], dup_hbm.at[:, cs], out_sem.at[2 * c]))
+        stores[-1].start()
+        loads[2 * c + 1].wait()
         for t in range(4):
-            ts = slice(t * 128, (t + 1) * 128)
-            drw_ref[:, ts] = small[t * E : (t + 1) * E]
-            dgain_ref[:, ts] = small[96 + t : 97 + t]
-            dfg_ref[:, ts] = small[100 + t : 101 + t]
-        out_ref[...] = out_in[...]
-        ing_ref[...] = ing_in[...]
+            down[cs, t * 128 : (t + 1) * 128] = units[d, t].astype(f32)
+        stores.append(pltpu.make_async_copy(down.at[cs], ddown_hbm.at[cs], out_sem.at[2 * c + 1]))
+        stores[-1].start()
+    for cp in loads[8:]:
+        cp.wait()
+    for i, dst in enumerate((out_hbm, ing_hbm)):
+        stores.append(pltpu.make_async_copy(held.at[i], dst, out_sem.at[8 + i]))
+        stores[-1].start()
+    for t in range(4):
+        ts = slice(t * 128, (t + 1) * 128)
+        dwo_ref[:, ts] = wo_ref[t * 192 : (t + 1) * 192, :].astype(f32)
+        dwqt_ref[:, ts] = dwq_ref[t * 192 : (t + 1) * 192, :].astype(f32)
+    small = small_ref[512:SMALL, :].astype(f32)
+    dkvw_ref[...] = small_ref[0:512, :].astype(f32)
+    for t in range(4):
+        ts = slice(t * 128, (t + 1) * 128)
+        drw_ref[:, ts] = small[t * E : (t + 1) * E]
+        dgain_ref[:, ts] = small[96 + t : 97 + t]
+        dfg_ref[:, ts] = small[100 + t : 101 + t]
+    for cp in stores:
+        cp.wait()
 
 
 def per_device(inputs, cotangent, norm_gain, ffn_gain, kv_weight, router_weight, query_weight, output_weight, up_weight,
@@ -803,25 +831,17 @@
         cost_estimate=pl.CostEstimate(flops=1 << 35, bytes_accessed=1 << 24, transcendentals=0),
     )(inputs, cotangent, norm_gain.reshape(1, D), ffn_gain.reshape(1, D), kv_weight, router_weight.T, routes.T,
       segment_ids.reshape(3, 128), wq, wo, up_weight, down_weight)
-    up_slots, down_slots = ([SHARED.index(u) for u in units] for units in (UP_UNIT, DOWN_UNIT))
-    assert down_slots == [1, 4, 7, 5]
-    ups = [pl.BlockSpec((1, 4, 128, 128), lambda i, k=k: (k, 0, i, 0)) for k in up_slots]
-    downs = [pl.BlockSpec((1, 4, 512, 128), lambda i: (1 + 3 * i - 5 * (i // 3), 0, 0, 0))]
-
-    def whole(*shape):
-        return pl.BlockSpec(shape, lambda i: (0,) * len(shape))
-
     dup, ddown, dwo, dwqt, dkvw, drw, dgain, dfg, out, ing = pl.pallas_call(
         kernel_f,
-        grid=(4,),
         out_shape=[S((D, FF), f32), S((FF, D), f32), S((3 * H, D), f32), S((3 * H, D), f32), S((D, 128), f32), S((E, D), f32),
                    S((1, D), f32), S((1, D), f32), S((T, D), bf16), S((T, D), bf16)],
-        in_specs=ups + downs + [
-                  whole(768, 128), whole(768, 128), whole(SMALL, 128), whole(T, D), whole(T, D)],
-        out_specs=[pl.BlockSpec((128, FF), lambda i: (i, 0)), pl.BlockSpec((512, D), lambda i: (i, 0)), whole(3 * H, D),
-                   whole(3 * H, D), whole(D, 128), whole(E, D), whole(1, D), whole(1, D), whole(T, D), whole(T, D)],
+        in_specs=[anywhere] * 6,
+        out_specs=[anywhere] * 2 + [vmem] * 6 + [anywhere] * 2,
+        scratch_shapes=[VM((8, 4, 512, 128), bf16), VM((768, 128), bf16), VM((768, 128), bf16), VM((SMALL, 128), bf16),
+                        VM((D, FF), f32), VM((FF, D), f32), VM((2, T, D), bf16), pltpu.SemaphoreType.DMA((13,)),
+                        pltpu.SemaphoreType.DMA((10,))],
         compiler_params=pltpu.CompilerParams(vmem_limit_bytes=62 << 20),
-    )(*[shared.reshape(8, 4, 512, 128)] * 5, dwo.reshape(768, 128), dwq.reshape(768, 128), small.reshape(SMALL, 128), out, ing)
+    )(shared.reshape(8, 4, 512, 128), dwo.reshape(768, 128), dwq.reshape(768, 128), small.reshape(SMALL, 128), out, ing)
     return (out, ing, dgain.reshape(D), dfg.reshape(D), dkvw, drw.T,
             jnp.swapaxes(dwqt.reshape(3, H, D), 1, 2), dwo.reshape(3, H, D), dup, ddown)
 

time: 126 us -> 124 us (0.984)
  Pallas kernels: 123 us -> 121 us
    pallas_call x1, Pallas kernels: 7.53 us -> 5.87 us  [per_device(): pl.pallas_call(kernel_f, out_shape=[S((D, FF), f32), S((FF, D), f32), S((...]
where the time goes in v10:
time: 124 us; the launch traced here: 122 us
  Pallas kernels  121 us (98%)
    pallas_call x1, Pallas kernels, per_device(): pl.pallas_call(kernel_all, out_shape=[S((T, D), bf16), S((T, D), bf16), S...  116 us
    pallas_call x1, Pallas kernels, per_device(): pl.pallas_call(kernel_f, out_shape=[S((D, FF), f32), S((FF, D), f32), S((...  5.87 us

profile of v10, /device:TPU:0, one launch (start us, length us, event | category | flops | bytes accessed | tf_op | source)
XLA Modules:
  0.0 122.3 jit_solution(779938625459406520)
XLA Ops:
  0.6 115.6 %shard_map.195 = (bf16[384,512]{1,0:T(8,128)(2,1)}, bf16[384,512]{1,0:T(8,128)(2,1)}, bf16[8,2,4,4,4,16,128]{6,5,4,3,2,1,0:T(8,128)(2,1)}, bf16[3,4,4,16,128]{4,...) custom-call(bf16[384,512]{1,0:T(8,128)(2,1)} %x_ref.1, ...), custom_call_target="tpu_custom_call" | custom-call | flops 34359738368 | bytes 16777216 | tf_op jit(solution)/shard_map/pallas_call | solution.py:823
  116.2 5.9 %shard_map.196 = (f32[512,2048]{1,0:T(8,128)}, f32[2048,512]{1,0:T(8,128)}, f32[192,512]{1,0:T(8,128)}, f32[192,512]{1,0:T(8,128)}, f32[512,128]{1,0:T(8,128)}, ...) custom-call(bf16[8,4,512,128]{3,2,1,0:T(8,128)(2,1)} %bitcast.20, ...), custom_call_target="tpu_custom_call" | custom-call | tf_op jit(solution)/shard_map/pallas_call | solution.py:834

commit v11 on v10

--- a/solution.py
+++ b/solution.py
@@ -298,21 +298,51 @@
             self.cp.arrived(self.line[k : k + 1])
             self.cp.start(self.core[k + 1 : k + 2])
 
+    def neighbour(self):
+        self.cp.arrived(self.core[:1])
+
     def finish(self):
-        self.cp.arrived(self.core)
-
-
-def bounds_of(kv_ref):
-    n0 = n1 = 0.0
-    for b in range(NB):
-        tail = kv_ref[b, T:KVR, :].astype(f32)
-        n0 = n0 + 16.0 * tail[0:1] + tail[1:2]
-        n1 = n1 + 16.0 * tail[2:3] + tail[3:4]
-    return n0, n1
-
-
-def segment_of(pos, bounds):
-    return (pos >= bounds[0]).astype(i32) + (pos >= bounds[1]).astype(i32)
+        self.cp.arrived(self.core[1:])
+
+
+class WideGather(Gather):
+    def __init__(self, copies, out):
+        self.cp, self.out = copies, out
+        at, ex = copies.place.at, copies.place.ex
+        wide, rows = D // 2, 3 * H // 4
+        block = lambda k: ((at["z"] - k + 4) % 4) * 2 + at["c"]
+
+        def quarter(axis, b):
+            column = wide + 128 * "xy".index(axis)
+            return out.at[b, pl.ds(pl.multiple_of(at[axis] * rows, 16), rows), column : column + 128]
+
+        def both(make, peer):
+            return copies.add(make, make, peer)
+
+        self.quarters = [[both(functools.partial(quarter, a, ex), ("z", k)) for a in "xy"] for k in (1, 2, 3)]
+        self.line = [both(lambda: out.at[ex, :, 0:wide], ("z", k)) for k in (1, 2, 3)]
+        self.relays = [[both(lambda a=a, k=k: quarter(a, block(k)), (a, d)) for a in "xy" for d in (1, 2, 3)] for k in (1, 2, 3)]
+        self.core = [both(lambda k=k: out.at[block(k)], ("c", 0)) for k in range(4)]
+
+    def start(self):
+        for ids in self.quarters:
+            self.cp.start(ids)
+        super().start()
+
+    def relay(self):
+        for ids, on in zip(self.quarters, self.relays):
+            self.cp.arrived(ids)
+            self.cp.start(on)
+
+    def forward(self):
+        for k in range(3):
+            self.cp.arrived(self.relays[k] + self.line[k : k + 1])
+            self.cp.start(self.core[k + 1 : k + 2])
+
+
+def segment_in_block(tail, pos):
+    tail = tail.astype(f32)
+    return (pos >= 16.0 * tail[0:1] + tail[1:2]).astype(i32) + (pos >= 16.0 * tail[2:3] + tail[3:4]).astype(i32)
 
 
 def sub8(v):
@@ -330,22 +360,18 @@
     return ok
 
 
-def prepare_keys(kv_ref, bounds, kaug, vaug, vt):
+def prepare_keys(kv_ref, b, kaug, vaug, vt):
     ln = lanes(T)
-    for b in range(NB):
-        bs = slice(b * T, (b + 1) * T)
-        kv = kv_ref[b, 0:T, :].astype(f32)
-        pos = (lax.broadcasted_iota(i32, (T, 128), 0) + b * T).astype(f32)
-        seg = segment_of(pos, bounds)
-        feat = jnp.where((ln < H + 3) & (seg != ln - H), NEG, 0.0)
-        feat = jnp.where((ln >= H + 3) & (ln < H + 6), 1.0, feat)
-        kaug[bs, :] = jnp.where(ln < H, kv, feat).astype(bf16)
-        if vaug is not None:
-            one = jnp.where(ln < H + 3, 1.0, 0.0)
-            vaug[bs, :] = jnp.where(ln < H, pltpu.roll(kv, H, 1), one).astype(bf16)
-        if vt is not None:
-            ones = jnp.where(lax.broadcasted_iota(i32, (16, T), 0) == 0, 1.0, 0.0)
-            vt[:, bs] = jnp.concatenate([jnp.transpose(kv)[H:], ones], axis=0).astype(bf16)
+    bs = pl.ds(pl.multiple_of(b * T, T), T)
+    kv = kv_ref[b, 0:T, :].astype(f32)
+    seg = segment_in_block(kv_ref[b, T:KVR, :], lax.broadcasted_iota(i32, (T, 128), 0).astype(f32))
+    feat = jnp.where((ln < H + 3) & (seg != ln - H), NEG, 0.0)
+    feat = jnp.where((ln >= H + 3) & (ln < H + 6), 1.0, feat)
+    kaug[bs, :] = jnp.where(ln < H, kv, feat).astype(bf16)
+    one = jnp.where(ln < H + 3, 1.0, 0.0)
+    vaug[bs, :] = jnp.where(ln < H, pltpu.roll(kv, H, 1), one).astype(bf16)
+    ones = jnp.where(lax.broadcasted_iota(i32, (16, T), 0) == 0, 1.0, 0.0)
+    vt[:, bs] = jnp.concatenate([jnp.transpose(kv)[H:], ones], axis=0).astype(bf16)
 
 
 def project_queries(normed, wq_ref, qall):
@@ -375,15 +401,15 @@
         qt[0:H, j * T : (j + 1) * T] = choose(routes, table, j).reshape(H, T).astype(bf16)
 
 
-def mark_queries(bounds, me, qt):
-    pos = (lax.broadcasted_iota(i32, (H, T), 1) + me * T).astype(f32)
-    seg = segment_of(pos, (bounds[0][:, 0:1], bounds[1][:, 0:1]))
+def mark_queries(kv_ref, me, qt):
+    pos = lax.broadcasted_iota(i32, (H, T), 1).astype(f32)
+    seg = segment_in_block(kv_ref[me, T:KVR, :][:, 0:1], pos)
     feat = jnp.where(lax.broadcasted_iota(i32, (H, T), 0) == seg, 1.0, 0.0).astype(bf16)
     for j in range(J):
         qt[H:, j * T : (j + 1) * T] = feat
 
 
-def attend(me, qt, kaug, vt, att, macc, acc):
+def attend(me, qt, kaug, vt, att, macc, acc, others):
     last = me // 2
     macc[...] = jnp.full(macc.shape, NEG, f32)
     acc[...] = jnp.zeros(acc.shape, f32)
@@ -421,8 +447,9 @@
             held, s = new, ahead
         weigh(sb, J // 2 - 1, *held)
 
+    block(last, True)
+    others()
     lax.fori_loop(0, last, lambda sb, c: (block(sb, False), c)[1], 0)
-    block(last, True)
     for g in range(J // 2):
         gs = slice(g * SB, (g + 1) * SB)
         tot = acc[H : H + 1, gs]
@@ -459,7 +486,7 @@
     me, core = place.ex, place.at["c"]
     dp = lax.axis_index("dp")
     copies = Copies(place, send, recv)
-    gq, gk, go = Gather(copies, wq_ref), Gather(copies, kv_ref), Gather(copies, wo_ref)
+    gq, gk, go = WideGather(copies, wq_ref), Gather(copies, kv_ref), Gather(copies, wo_ref)
     big7 = big.reshape(2, UNITS, 4, 4, 4, 16, 128)
     lbig7 = lbig.reshape(2, 3, 4, 4, 4, 16, 128)
     early = [Scatter(copies, big7, (r0, r1, r2), ex, parts, groups, o) for parts, groups, o in EARLY]
@@ -498,23 +525,31 @@
     gq.start()
     gk.start()
     gates_of(normed, rw_ref, rt_ref, gate_ref)
+    gq.relay()
     gq.forward()
+    gq.neighbour()
     gq.finish()
     project_queries(normed, wq_ref, table)
     pick_queries(rt_ref, table, qt_ref)
+    mark_queries(kv_ref, me, qt_ref)
     gk.forward()
-    gk.finish()
-    bounds = bounds_of(kv_ref)
-    prepare_keys(kv_ref, bounds, kaug, vaug, vt)
-    mark_queries(bounds, me, qt_ref)
     go.start()
-    attend(me, qt_ref, kaug, vt, att_ref, macc, acc)
+    gk.neighbour()
+    for i in range(2):
+        prepare_keys(kv_ref, 2 * (me // 2) + i, kaug, vaug, vt)
+
+    def others():
+        gk.finish()
+        lax.fori_loop(0, NB, lambda b, c: (prepare_keys(kv_ref, b, kaug, vaug, vt), c)[1], 0)
+
+    attend(me, qt_ref, kaug, vt, att_ref, macc, acc, others)
 
     go.forward()
     routes = route_rows(rt_ref)
     for j in range(J):
         rows[j] = sub8(att_ref[:, j * T : (j + 1) * T].astype(f32) * gate_ref[j : j + 1, :])
     to_experts(routes, rows, gat)
+    go.neighbour()
     go.finish()
     x = x_ref[...].astype(f32)
     wo_all = wo_ref[...].reshape(EW, D)
@@ -767,7 +802,7 @@
     VM((3, 4, 4, 16, 128), bf16),
     VM((2, 4, SMALL // 8, 128), bf16), VM((4, SMALL // 8, 128), bf16), VM((4, SMALL // 8, 128), bf16),
     VM((3, SMALL // 8, 128), bf16), VM((4, SMALL // 8, 128), bf16), VM((4, SMALL // 8, 128), bf16),
-] + dma_sems(210) + dma_sems(NB)
+] + dma_sems(234) + dma_sems(NB)
 
 
 def kernel_f(all_hbm, wo_hbm, dwq_hbm, small_hbm, out_in, ing_in,

time: 124 us -> 120 us (0.968)
  Pallas kernels: 121 us -> 118 us
    pallas_call x1, Pallas kernels: 116 us -> 112 us  [per_device(): pl.pallas_call(kernel_all, out_shape=[S((T, D), bf16), S((T, D), bf16), S...]
where the time goes in v11:
time: 120 us; the launch traced here: 119 us
  Pallas kernels  118 us (98%)
    pallas_call x1, Pallas kernels, per_device(): pl.pallas_call(kernel_all, out_shape=[S((T, D), bf16), S((T, D), bf16), S...  112 us
    pallas_call x1, Pallas kernels, per_device(): pl.pallas_call(kernel_f, out_shape=[S((D, FF), f32), S((FF, D), f32), S((...  5.87 us

profile of v11, /device:TPU:0, one launch (start us, length us, event | category | flops | bytes accessed | tf_op | source)
XLA Modules:
  0.0 118.9 jit_solution(18246550614174599330)
XLA Ops:
  0.6 112.2 %shard_map.195 = (bf16[384,512]{1,0:T(8,128)(2,1)}, bf16[384,512]{1,0:T(8,128)(2,1)}, bf16[8,2,4,4,4,16,128]{6,5,4,3,2,1,0:T(8,128)(2,1)}, bf16[3,4,4,16,128]{4,...) custom-call(bf16[384,512]{1,0:T(8,128)(2,1)} %x_ref.1, ...), custom_call_target="tpu_custom_call" | custom-call | flops 34359738368 | bytes 16777216 | tf_op jit(solution)/shard_map/pallas_call | solution.py:858
  112.9 5.9 %shard_map.196 = (f32[512,2048]{1,0:T(8,128)}, f32[2048,512]{1,0:T(8,128)}, f32[192,512]{1,0:T(8,128)}, f32[192,512]{1,0:T(8,128)}, f32[512,128]{1,0:T(8,128)}, ...) custom-call(bf16[8,4,512,128]{3,2,1,0:T(8,128)(2,1)} %bitcast.20, ...), custom_call_target="tpu_custom_call" | custom-call | tf_op jit(solution)/shard_map/pallas_call | solution.py:869
